TPU v7x, 512 devices: a whole 4x4x16 slice. The times are simulated.
512 devices in a mesh: chan: 8 (over y_hi, x), gx: 16 (over z), gy: 4 (over y_lo, core).
Axes of the slice: x: 4, y: 4 (y_hi: 2, y_lo: 2; y = y_hi * 2 + y_lo), z: 16, core: 2. Of those that a mesh axis runs over, the one named last changes fastest.
Arguments:
- features: bfloat16 [128, 32, 32, 128], P('chan', 'gx', 'gy'), may hold values from -6 to 6
- weight: bfloat16 [27, 128, 128], replicated, may hold values from -0.109375 to 0.109375
- bias: float32 [128], P('chan'), may hold values from -3 to 3
- cotangent: bfloat16 [128, 32, 32, 128], P('chan', 'gx', 'gy'), may hold values from -6 to 6
Outputs:
- output: bfloat16 [128, 32, 32, 128], P('chan', 'gx', 'gy')
- input_grad: bfloat16 [128, 32, 32, 128], P('chan', 'gx', 'gy')
- weight_grad: float32 [27, 128, 128], P(None, None, 'chan')
- bias_grad: float32 [128], P('chan')
All inputs are finite; a program needn't handle non-finite values.
Results may differ from a plain program's by a relative error of at most 0.009.
Values may be sent and summed in bfloat16 or wider, within the bound.
No kernel may reach another device: no remote copies, remote signals or barrier semaphores. Data moves between devices by JAX's collectives and lax.ppermute only.
A program may use at most 64 MiB of HBM per device.

v0:
```python
import jax
import jax.numpy as jnp
from jax import lax
from jax.sharding import PartitionSpec as P


def with_halo(block, sides, width):
    for axis, dim in sides:
        count = lax.axis_size(axis)
        forward = [(i, i + 1) for i in range(count - 1)]
        forward.append((count - 1, 0))
        backward = [(target, source) for source, target in forward]
        low = lax.ppermute(
            lax.slice_in_dim(block, block.shape[dim] - width, None, axis=dim), axis, forward
        )
        high = lax.ppermute(lax.slice_in_dim(block, 0, width, axis=dim), axis, backward)
        block = jnp.concatenate([low, block, high], axis=dim)
    return block


def build_patches(padded, extent_x, extent_y):
    blocks = []
    for first in range(3):
        pieces = []
        for second in range(3):
            for third in range(3):
                window = padded[:, first : first + extent_x, second : second + extent_y, :]
                pieces.append(jnp.roll(window, 1 - third, axis=3))
        stacked = jnp.stack(pieces, axis=0)
        blocks.append(stacked.reshape(9 * padded.shape[0], -1))
    return blocks


def tap_sum(weight_rows, padded, sign, extent_x, extent_y, count):
    total = None
    depth = padded.shape[3]
    for first in range(3):
        start_x = 2 - first
        slab = padded[:, start_x : start_x + extent_x]
        zed = jnp.dot(
            weight_rows[first], slab.reshape(slab.shape[0], -1), preferred_element_type=jnp.float32
        )
        zed = zed.reshape(3, 3, count, extent_x, extent_y + 2, depth)
        for second in range(3):
            start_y = 2 - second
            for third in range(3):
                part = zed[second, third, :, :, start_y : start_y + extent_y, :]
                part = jnp.roll(part, -(third - 1) * sign, axis=3)
                total = part if total is None else total + part
    return total


def on_device(features, weight, bias, cotangent):
    chans, extent_x, extent_y, depth = features.shape
    width = weight.shape[1]
    cells = extent_x * extent_y * depth
    offset = lax.axis_index("chan") * chans
    padded = with_halo(features, (("gx", 1), ("gy", 2)), 1)
    patches = build_patches(padded, extent_x, extent_y)
    row_mats = []
    for first in range(3):
        block = lax.dynamic_slice_in_dim(weight[first * 9 : (first + 1) * 9], offset, chans, 2)
        row_mats.append(jnp.transpose(block, (1, 0, 2)).reshape(width, 9 * chans))
    total = jnp.zeros((chans * lax.axis_size("chan"), cells), jnp.float32)
    for rows_first in range(3):
        rows = row_mats[rows_first]
        total = total + jnp.dot(rows, patches[rows_first], preferred_element_type=jnp.float32)
    pre = lax.psum_scatter(total, "chan", scatter_dimension=0, tiled=True).reshape(
        chans, extent_x, extent_y, depth
    )
    pre = pre + bias[:, None, None, None]
    sigma = jax.nn.sigmoid(pre)
    output = (pre * sigma).astype(jnp.bfloat16)
    dpre = (cotangent.astype(jnp.float32) * sigma * (1.0 + pre * (1.0 - sigma))).astype(
        jnp.bfloat16
    )
    every = lax.all_gather(dpre, "chan", axis=0, tiled=True)
    grad_pad = with_halo(every, (("gx", 1), ("gy", 2)), 1)
    back_rows = []
    for first in range(3):
        block = lax.dynamic_slice_in_dim(weight[first * 9 : (first + 1) * 9], offset, chans, 2)
        back_rows.append(jnp.transpose(block, (0, 2, 1)).reshape(9 * chans, width))
    input_grad = tap_sum(back_rows, grad_pad, -1, extent_x, extent_y, chans).astype(jnp.bfloat16)
    inner = grad_pad[:, 1 : 1 + extent_x, 1 : 1 + extent_y, :].reshape(width, cells)
    weight_parts = []
    for first in range(3):
        product = lax.dot_general(
            inner, patches[first], (((1,), (1,)), ((), ())), preferred_element_type=jnp.float32
        )
        weight_parts.append(jnp.transpose(product.reshape(width, 9, chans), (1, 0, 2)))
    weight_local = jnp.concatenate(weight_parts, axis=0)
    bias_local = jnp.sum(dpre.astype(jnp.float32), axis=(1, 2, 3))
    weight_total, bias_total = lax.psum((weight_local, bias_local), ("gx", "gy"))
    scale = 1.0 / jnp.sqrt(
        jnp.float32(extent_x * lax.axis_size("gx") * extent_y * lax.axis_size("gy") * depth)
    )
    return (output, input_grad, weight_total * scale, bias_total * scale)


def solution(mesh):
    return jax.shard_map(
        on_device,
        mesh=mesh,
        in_specs=(P("chan", "gx", "gy", None), P(), P("chan"), P("chan", "gx", "gy", None)),
        out_specs=(
            P("chan", "gx", "gy", None),
            P("chan", "gx", "gy", None),
            P(None, None, "chan"),
            P("chan"),
        ),
        check_vma=False,
    )
```

profile of v0, /device:TPU:1, one launch (start us, length us, event | category | flops | bytes accessed | tf_op | source)
XLA Modules:
  0.0 685.1 jit_solution(10472216390885604797)
XLA Ops:
  7.2 0.8 fusion.85
  8.0 4.4 collective-permute-start
  12.4 9.5 %collective-permute-start.1 = (bf16[16,1,8,128]{3,0,2,1:T(8,128)(2,1)S(1)}, bf16[16,1,8,128]{3,0,2,1:T(8,128)(2,1)S(1)}, u32[]{:S(2)}, u32[]{:S(2)}) collective-permute-start(bf16[16,1,8,128]{3,0,2,1:T(8,128)(2,1)S(1)} %copy.79), channel_id=1, source_target_pairs={{4,0},{8,4},{12,8},{16,12},{20,16},{24,20},{28,24},{32,28},{36,32}... | collective-permute-start | bytes 98312 | tf_op jit(solution)/shard_map/ppermute | solution.py:16
  21.9 1.0 fusion.84
  22.9 1.0 fusion.83
  23.9 1.2 fusion.76
  25.6 0.8 copy.62
  26.4 0.8 copy.66
  27.2 0.8 copy.64
  28.2 4.0 collective-permute-start.2
  32.5 1.9 collective-permute-start.3
  35.8 1.8 collective-permute-done.3
  40.0 1.1 fusion.86
  41.5 0.4 copy-done.6
  41.9 1.3 convolution_add_fusion
  43.3 83.1 %reduce-scatter.2.cloned.1.call-done = f32[16,2048]{1,0:T(8,128)} async-done(((f32[128,2048]{1,0:T(8,128)}), f32[16,2048]{1,0:T(8,128)}) %reduce-scatter.2.cloned.1.call-update) | async-done | bytes 131088 | tf_op jit(solution)/shard_map/reduce_scatter | solution.py:68
  126.3 0.9 copy.67
  127.5 29.0 %all_gather.3 = bf16[128,2,8,128]{3,0,2,1:T(8,128)(2,1)S(1)} all-gather(bf16[16,2,8,128]{3,0,2,1:T(8,128)(2,1)S(1)} %get-tuple-element.13), channel_id=1, replica_groups=mesh['chan'=8,'gx'=16,'gy'=4] {'chan'}, dimensions={0}, use_global_device_ids=true | all-gather | bytes 589824 | tf_op jit(solution)/shard_map/all_gather | solution.py:77
  157.3 113.1 %psum.15 = f32[16]{0:T(128)S(1)} all-reduce(f32[16]{0:T(128)S(1)} %get-tuple-element.12), channel_id=1, replica_groups=mesh['chan'=8,'gx'=16,'gy'=4] {'gx','gy'}, use_global_device_ids=true, to_apply=%region_3.4 | all-reduce | flops 16 | bytes 128 | tf_op jit(solution)/shard_map/psum | solution.py:93
  270.4 0.5 broadcast_multiply_fusion.1
  270.9 1.9 collective-permute-start.5
  272.8 3.4 collective-permute-start.4
  276.5 0.7 pad_maximum_fusion.1
  277.2 0.6 copy.46
  277.9 5.8 collective-permute-done.4
  283.8 2.5 collective-permute-start.6
  286.4 2.3 collective-permute-start.7
  288.7 381.5 %all-reduce.2.cloned.1.call-done = f32[27,128,16]{1,2,0:T(8,128)} async-done(((f32[27,128,16]{1,2,0:T(8,128)}), f32[27,128,16]{1,2,0:T(8,128)}) %all-reduce.2.cloned.1.call-update) | async-done | bytes 221200 | tf_op jit(solution)/shard_map/psum | solution.py:93
  670.2 1.6 broadcast_multiply_fusion
  672.0 0.5 fusion.74
  676.9 0.8 fusion.11
  677.7 0.6 copy.47
  (115 shorter events, 10.8 us)
Async XLA Ops:
  7.2 119.2 %reduce-scatter.2.cloned.1.call-start = ((), (), s32[]{:S(2)}) async-start(), calls=%async_computation.1 | async-start | bytes 1179648 | tf_op jit(solution)/shard_map/reduce_scatter | solution.py:68
  8.0 19.9 %collective-permute-start = (bf16[16,1,8,128]{3,0,2,1:T(8,128)(2,1)S(1)}, bf16[16,1,8,128]{3,0,2,1:T(8,128)(2,1)S(1)}, u32[]{:S(2)}, u32[]{:S(2)}) collective-permute-start(bf16[16,1,8,128]{3,0,2,1:T(8,128)(2,1)S(1)} %copy.78), channel_id=1, source_target_pairs={{0,4},{4,8},{8,12},{12,16},{16,20},{20,24},{24,28},{28,32},{32,36}... | collective-permute-start | bytes 98312 | tf_op jit(solution)/shard_map/ppermute | solution.py:13
  12.4 15.6 %collective-permute-start.1 = (bf16[16,1,8,128]{3,0,2,1:T(8,128)(2,1)S(1)}, bf16[16,1,8,128]{3,0,2,1:T(8,128)(2,1)S(1)}, u32[]{:S(2)}, u32[]{:S(2)}) collective-permute-start(bf16[16,1,8,128]{3,0,2,1:T(8,128)(2,1)S(1)} %copy.79), channel_id=1, source_target_pairs={{4,0},{8,4},{12,8},{16,12},{20,16},{24,20},{28,24},{32,28},{36,32}... | collective-permute-start | bytes 98312 | tf_op jit(solution)/shard_map/ppermute | solution.py:16
  25.1 2.8 copy-start
  28.2 6.2 collective-permute-start.2
  32.5 5.1 collective-permute-start.3
  38.5 1.1 copy-start.1
  40.0 1.1 copy-start.4
  41.1 0.8 copy-start.6
  41.9 85.4 %copy-start.8 = (bf16[16,2,8,128]{3,2,1,0:T(8,128)(2,1)S(1)}, bf16[16,2,8,128]{3,2,1,0:T(8,128)(2,1)}, u32[]{:S(2)}) copy-start(bf16[16,2,8,128]{3,2,1,0:T(8,128)(2,1)} %param.7) | copy-start | bytes 196612
  41.9 85.4 %copy-start.9 = (f32[16]{0:T(128)S(1)}, f32[16]{0:T(128)}, u32[]{:S(2)}) copy-start(f32[16]{0:T(128)} %param.6) | copy-start | bytes 196
  43.2 113.4 %copy-start.2 = (bf16[9,16,2,8,128]{4,1,3,2,0:T(8,128)(2,1)S(1)}, bf16[9,16,2,8,128]{4,1,3,2,0:T(8,128)(2,1)}, u32[]{:S(2)}) copy-start(bf16[9,16,2,8,128]{4,1,3,2,0:T(8,128)(2,1)} %copy-done.1) | copy-start | bytes 1769476
  43.2 626.9 %all-reduce.2.cloned.1.call-start = ((), (), s32[]{:S(2)}) async-start(), calls=%async_computation.2 | async-start | bytes 442368 | tf_op jit(solution)/shard_map/psum | solution.py:93
  270.9 12.9 %collective-permute-start.5 = (bf16[128,1,8,128]{3,0,2,1:T(8,128)(2,1)S(1)}, bf16[128,1,8,128]{3,0,2,1:T(8,128)(2,1)S(1)}, u32[]{:S(2)}, u32[]{:S(2)}) collective-permute-start(bf16[128,1,8,128]{3,0,2,1:T(8,128)(2,1)S(1)} %get-tuple-element.40), channel_id=1, source_target_pairs={{4,0},{8,4},{12,8},{16,12},{20,16},{24,20},{28,24},{32,28},{36,32}... | collective-permute-start | bytes 786440 | tf_op jit(solution)/shard_map/ppermute | solution.py:16
  272.8 10.9 %collective-permute-start.4 = (bf16[128,1,8,128]{3,0,2,1:T(8,128)(2,1)S(1)}, bf16[128,1,8,128]{3,0,2,1:T(8,128)(2,1)S(1)}, u32[]{:S(2)}, u32[]{:S(2)}) collective-permute-start(bf16[128,1,8,128]{3,0,2,1:T(8,128)(2,1)S(1)} %get-tuple-element.41), channel_id=1, source_target_pairs={{0,4},{4,8},{8,12},{12,16},{16,20},{20,24},{24,28},{28,32},{32,36}... | collective-permute-start | bytes 786440 | tf_op jit(solution)/shard_map/ppermute | solution.py:13
  283.8 388.0 %collective-permute-start.6 = (bf16[128,4,1,128]{3,0,2,1:T(8,128)(2,1)S(1)}, bf16[128,4,1,128]{3,0,2,1:T(8,128)(2,1)S(1)}, u32[]{:S(2)}, u32[]{:S(2)}) collective-permute-start(bf16[128,4,1,128]{3,0,2,1:T(8,128)(2,1)S(1)} %get-tuple-element.35), channel_id=1, source_target_pairs={{0,1},{1,2},{2,3},{3,0},{4,5},{5,6},{6,7},{7,4},{8,9},{9,10},{10,1... | collective-permute-start | bytes 393224 | tf_op jit(solution)/shard_map/ppermute | solution.py:13
  286.4 385.4 %collective-permute-start.7 = (bf16[128,4,1,128]{3,0,2,1:T(8,128)(2,1)S(1)}, bf16[128,4,1,128]{3,0,2,1:T(8,128)(2,1)S(1)}, u32[]{:S(2)}, u32[]{:S(2)}) collective-permute-start(bf16[128,4,1,128]{3,0,2,1:T(8,128)(2,1)S(1)} %get-tuple-element.36), channel_id=1, source_target_pairs={{1,0},{2,1},{3,2},{0,3},{5,4},{6,5},{7,6},{4,7},{9,8},{10,9},{11,1... | collective-permute-start | bytes 393224 | tf_op jit(solution)/shard_map/ppermute | solution.py:16
  672.8 0.8 copy-start.3
  673.9 0.8 copy-start.7
  675.0 0.8 copy-start.5
Sparse Core Ops, SparseCore 0:
  43.3 82.9 reduce-scatter.1
  278.0 392.1 all-reduce.1
where the time goes:
time: 686 us; the launch traced here: 685 us
  waiting for transfers between devices  472 us (69%)
  blocking collectives  142 us (21%)
  starting transfers between devices  30 us (4%)
  local copies, waits for them, and re-layouts  14.9 us (2%)
  between operations  14.7 us (2%)
    psum x1, waiting for transfers between devices, on_device(): lax.psum((weight_local, bias_local), ('gx', 'gy'))  381 us
    psum x1, blocking collectives, on_device(): lax.psum((weight_local, bias_local), ('gx', 'gy'))  113 us
    reduce_scatter x1, waiting for transfers between devices, on_device(): lax.psum_scatter(total, 'chan', scatter_dimension=0, tiled=True)  83.1 us
    all_gather x1, blocking collectives, on_device(): every = lax.all_gather(dpre, 'chan', axis=0, tiled=True)  29 us
    ppermute x4, starting transfers between devices, with_halo(): lax.ppermute(lax.slice_in_dim(block, 0, width, axis=dim), axis, backward)  15.6 us
    ppermute x4, starting transfers between devices, with_halo(): lax.ppermute(lax.slice_in_dim(block, block.shape[dim] - width, None, axis...  14.3 us
  transfers between devices with their start and end apart: 10, of which 4 were waited for; matrix products, arithmetic and copies ran while one was open for 2% of the time, Pallas kernels for 0%

commit v1 on v0

v1 whole, which is shorter than its diff:
```python
import functools

import jax
import jax.numpy as jnp
from jax import lax
from jax.experimental import pallas as pl
from jax.experimental.pallas import tpu as pltpu
from jax.sharding import Mesh, PartitionSpec as P

BF = jnp.bfloat16
F32 = jnp.float32
LANE = 128
TAPS = 27


def conv_kernel(place, got, weight, own_weight, out_ref, sums_ref, inner_ref, moved, grad, patch, spread, act):
    chan = place[0]
    gy = place[1]
    peers, _, chans, _ = got.shape
    width = peers * chans
    own = pl.multiple_of(chan * chans, chans)

    def row(index):
        return jnp.concatenate([got[p, index] for p in range(peers)], axis=0)

    for x in range(4):
        for y in range(10):
            tile = row(x * 10 + y)
            lanes = slice(y * LANE, (y + 1) * LANE)
            wide = tile.astype(F32)
            moved[x, 0:width, lanes] = pltpu.roll(wide, 1, 1).astype(BF)
            moved[x, width : 2 * width, lanes] = tile
            moved[x, 2 * width : 3 * width, lanes] = pltpu.roll(wide, LANE - 1, 1).astype(BF)

    bias = jnp.sum(row(56).astype(F32), axis=1, keepdims=True)
    filters = jnp.concatenate([weight[t] for t in range(TAPS)], axis=1)
    half = 4
    for x in range(2):
        for part in range(8 // half):
            y0 = part * half
            span = half * LANE
            cells = jnp.concatenate(
                [moved[x + a, :, (b + y0) * LANE : (b + y0) * LANE + span] for a in range(3) for b in range(3)],
                axis=0,
            )
            pre = jnp.dot(filters, cells, preferred_element_type=F32) + bias
            sigma = jax.nn.sigmoid(pre)
            cot = jnp.concatenate([row(40 + x * 8 + y0 + y) for y in range(half)], axis=1).astype(F32)
            lanes = slice((x * 8 + y0) * LANE, (x * 8 + y0) * LANE + span)
            grad[:, lanes] = (cot * sigma * (1.0 + pre * (1.0 - sigma))).astype(BF)
            act[:, lanes] = (pre * sigma).astype(BF)
    for x in range(2):
        for y in range(8):
            lanes = slice((x * 8 + y) * LANE, (x * 8 + y + 1) * LANE)
            out_ref[x, y] = act[pl.ds(own, chans), lanes]

    for a in range(3):
        for b in range(3):
            for c in range(3):
                t = 9 * a + 3 * b + c
                for x in range(2):
                    patch[t * chans : (t + 1) * chans, x * 1024 : (x + 1) * 1024] = moved[
                        x + a, pl.ds(pl.multiple_of(c * width + own, chans), chans), b * LANE : (b + 8) * LANE
                    ]
    index = lax.broadcasted_iota(jnp.int32, (chans, 2048), 0)
    patch[TAPS * chans :, :] = jnp.where(index == 0, 1.0, 0.0).astype(BF)
    total = lax.dot_general(patch[...], grad[...], (((1,), (1,)), ((), ())), preferred_element_type=F32)
    quarter = total.shape[0] // 4
    for g in range(4):
        sums_ref[g, 0:quarter, :] = total[g * quarter : (g + 1) * quarter]
        sums_ref[g, quarter:, :] = jnp.zeros((4 * chans, LANE), F32)

    spread[...] = jnp.zeros(spread.shape, F32)
    for x in range(2):
        terms = jnp.dot(own_weight[...], grad[:, x * 1024 : (x + 1) * 1024], preferred_element_type=F32)
        for a in range(3):
            for b in range(3):
                for c in range(3):
                    t = 9 * a + 3 * b + c
                    spread[c, x + a, :, b * LANE : (b + 8) * LANE] += terms[t * chans : (t + 1) * chans]
    after = lax.rem(gy + 1, 4)
    before = lax.rem(gy + 3, 4)
    for x in range(4):
        for y in range(10):
            lanes = slice(y * LANE, (y + 1) * LANE)
            tile = (
                pltpu.roll(spread[0, x, :, lanes], LANE - 1, 1)
                + spread[1, x, :, lanes]
                + pltpu.roll(spread[2, x, :, lanes], 1, 1)
            )
            spot = slice(quarter + x * chans, quarter + (x + 1) * chans)
            if y == 0:
                sums_ref[before, spot, :] = tile
            elif y == 9:
                sums_ref[after, spot, :] = tile
            else:
                inner_ref[x, y - 1] = tile


def on_device(features, weight, bias, cotangent):
    chans, extent_x, extent_y, depth = features.shape
    width = weight.shape[1]
    peers = width // chans
    chan = lax.axis_index("chan")
    gy = lax.axis_index("gy")
    count_x = lax.axis_size("zh") * lax.axis_size("zl")
    count_y = lax.axis_size("gy")
    gx_axes = ("zh", "zl")
    up = [(i, (i + 1) % count_x) for i in range(count_x)]
    down = [(i, (i - 1) % count_x) for i in range(count_x)]
    after = lax.rem(gy + 1, count_y)
    before = lax.rem(gy + count_y - 1, count_y)
    slot = lax.broadcasted_iota(jnp.int32, (count_y, 1, 1, 1), 0)

    rows = jnp.transpose(features, (1, 2, 0, 3))
    low = lax.ppermute(rows[-1:], gx_axes, up)
    high = lax.ppermute(rows[:1], gx_axes, down)
    own_weight = lax.dynamic_slice_in_dim(weight, chan * chans, chans, 2)
    own_weight = jnp.transpose(own_weight, (0, 2, 1)).reshape(TAPS * chans, width)
    cot_rows = jnp.transpose(cotangent, (1, 2, 0, 3)).reshape(extent_x * extent_y, chans, depth)
    first = lax.reduce_precision(bias, 8, 7)
    second = lax.reduce_precision(bias - first, 8, 7)
    third = bias - first - second
    bias_row = jnp.stack([first, second, third], axis=1).astype(BF)
    bias_row = jnp.pad(bias_row, ((0, 0), (0, depth - 3)))[None]

    rows = jnp.concatenate([low, rows, high], axis=0)
    edges = jnp.where(slot == after, rows[None, :, -1], jnp.where(slot == before, rows[None, :, 0], 0)).astype(BF)
    edges = lax.all_to_all(edges, "gy", 0, 0)
    south = lax.dynamic_index_in_dim(edges, before, 0, keepdims=False)
    north = lax.dynamic_index_in_dim(edges, after, 0, keepdims=False)
    rows = jnp.concatenate([south[:, None], rows, north[:, None]], axis=1)
    parcel = jnp.concatenate([rows.reshape(-1, chans, depth), cot_rows, bias_row], axis=0)
    got = lax.all_to_all(jnp.broadcast_to(parcel, (peers,) + parcel.shape), "chan", 0, 0)

    cells = extent_x * extent_y * depth
    piece = (TAPS + 1) * chans // 4
    vmem = pl.BlockSpec(memory_space=pltpu.VMEM)
    output, sums, inner = pl.pallas_call(
        conv_kernel,
        out_shape=(
            jax.ShapeDtypeStruct((extent_x, extent_y, chans, depth), BF),
            jax.ShapeDtypeStruct((4, piece + 4 * chans, LANE), F32),
            jax.ShapeDtypeStruct((4, extent_y, chans, depth), F32),
        ),
        in_specs=[pl.BlockSpec(memory_space=pltpu.SMEM), vmem, vmem, vmem],
        out_specs=(vmem, vmem, vmem),
        scratch_shapes=[
            pltpu.VMEM((4, 3 * width, 10 * LANE), BF),
            pltpu.VMEM((width, cells), BF),
            pltpu.VMEM(((TAPS + 1) * chans, cells), BF),
            pltpu.VMEM((3, 4, chans, 10 * LANE), F32),
            pltpu.VMEM((width, cells), BF),
        ],
        compiler_params=pltpu.CompilerParams(vmem_limit_bytes=40 * 1024 * 1024),
    )(jnp.stack([chan, gy]).astype(jnp.int32), got, weight, own_weight)

    sums = lax.all_to_all(sums, "gy", 0, 0)
    edge = sums[:, piece:].reshape(4, 4, chans, depth)
    south = lax.dynamic_index_in_dim(edge, before, 0, keepdims=False)
    north = lax.dynamic_index_in_dim(edge, after, 0, keepdims=False)
    inner = jnp.concatenate([inner[:, :1] + south[:, None], inner[:, 1:-1], inner[:, -1:] + north[:, None]], axis=1)
    low = lax.ppermute(inner[-1:], gx_axes, up)
    high = lax.ppermute(inner[:1], gx_axes, down)
    scale = 1.0 / jnp.sqrt(jnp.float32(count_x * count_y * cells))
    part = jnp.sum(sums[:, :piece], axis=0).astype(BF)
    part = lax.all_to_all(jnp.broadcast_to(part, (4,) + part.shape), "zl", 0, 0)
    part = jnp.sum(part.astype(F32), axis=0).astype(BF)
    part = lax.all_to_all(jnp.broadcast_to(part, (4,) + part.shape), "zh", 0, 0)
    part = (jnp.sum(part.astype(F32), axis=0) * scale).astype(BF)
    part = lax.all_to_all(jnp.broadcast_to(part, (4,) + part.shape), "gy", 0, 0)
    whole = part.reshape((TAPS + 1) * chans, LANE).astype(F32)
    weight_grad = jnp.transpose(whole[: TAPS * chans].reshape(TAPS, chans, width), (0, 2, 1))
    bias_grad = lax.dynamic_slice_in_dim(whole[TAPS * chans], chan * chans, chans, 0)

    input_grad = jnp.concatenate([inner[1:2] + low, inner[2:3] + high], axis=0).astype(BF)
    return (
        jnp.transpose(output, (2, 0, 1, 3)),
        jnp.transpose(input_grad, (2, 0, 1, 3)),
        weight_grad,
        bias_grad,
    )


def solution(mesh):
    split = Mesh(mesh.devices.reshape(8, 4, 4, 4), ("chan", "zh", "zl", "gy"))
    block = P("chan", ("zh", "zl"), "gy", None)
    return jax.shard_map(
        on_device,
        mesh=split,
        in_specs=(block, P(), P("chan"), block),
        out_specs=(block, block, P(None, None, "chan"), P("chan")),
        check_vma=False,
    )
```

time: 686 us -> 119 us (0.17)
  waiting for transfers between devices: 472 us -> 41.8 us
  blocking collectives: 142 us -> 0 us
  starting transfers between devices: 30 us -> 58.9 us
  between operations: 14.7 us -> 0.81 us
    psum x1 -> x0, waiting for transfers between devices: 381 us -> none  [on_device(): lax.psum((weight_local, bias_local), ('gx', 'gy'))]
    psum x1 -> x0, blocking collectives: 113 us -> none  [on_device(): lax.psum((weight_local, bias_local), ('gx', 'gy'))]
    reduce_scatter x1 -> x0, waiting for transfers between devices: 83.1 us -> none  [on_device(): lax.psum_scatter(total, 'chan', scatter_dimension=0, tiled=True)]
    all_to_all x0 -> x6, waiting for transfers between devices: none -> 40.9 us  [the longest x1 23.3 us: on_device(): lax.all_to_all(jnp.broadcast_to(parcel, (peers,) + parcel.shape), 'chan',...]
    all_to_all x0 -> x6, starting transfers between devices: none -> 36 us  [the longest x1 9.55 us: on_device(): part = lax.all_to_all(jnp.broadcast_to(part, (4,) + part.shape), 'zh', 0, 0)]
    all_gather x1 -> x0, blocking collectives: 29 us -> none  [on_device(): every = lax.all_gather(dpre, 'chan', axis=0, tiled=True)]
    ppermute x8 -> x4, starting transfers between devices: 29.9 us -> 22.9 us  [the longest x1 9.5 us: on_device(): high = lax.ppermute(rows[:1], gx_axes, down)]
  transfers between devices with their start and end apart: 10 -> 10, of which waited for: 4 -> 8; matrix products, arithmetic and copies ran while one was open for 2% -> 5% of each run, Pallas kernels for 0% -> 0%
where the time goes in v1:
time: 119 us; the launch traced here: 118 us
  starting transfers between devices  58.9 us (49%)
  waiting for transfers between devices  41.8 us (35%)
  local copies, waits for them, and re-layouts  10.7 us (9%)
  Pallas kernels  4.48 us (4%)
  other arithmetic  1.69 us (1%)
    all_to_all x1, waiting for transfers between devices, on_device(): lax.all_to_all(jnp.broadcast_to(parcel, (peers,) + parcel.shape), 'chan',...  23.3 us
    all_to_all x1, starting transfers between devices, on_device(): part = lax.all_to_all(jnp.broadcast_to(part, (4,) + part.shape), 'zh', 0, 0)  9.55 us
    ppermute x1, starting transfers between devices, on_device(): high = lax.ppermute(rows[:1], gx_axes, down)  9.5 us
    all_to_all x1, starting transfers between devices, on_device(): part = lax.all_to_all(jnp.broadcast_to(part, (4,) + part.shape), 'gy', 0, 0)  7.33 us
    all_to_all x1, starting transfers between devices, on_device(): lax.all_to_all(jnp.broadcast_to(parcel, (peers,) + parcel.shape), 'chan',...  6.78 us
    all_to_all x1, waiting for transfers between devices, on_device(): sums = lax.all_to_all(sums, 'gy', 0, 0)  6.21 us
    ppermute x1, starting transfers between devices, on_device(): high = lax.ppermute(inner[:1], gx_axes, down)  5.69 us
    all_to_all x1, waiting for transfers between devices, on_device(): part = lax.all_to_all(jnp.broadcast_to(part, (4,) + part.shape), 'zh', 0, 0)  4.9 us
  transfers between devices with their start and end apart: 10, of which 8 were waited for; matrix products, arithmetic and copies ran while one was open for 5% of the time, Pallas kernels for 0%

profile of v1, /device:TPU:1, one launch (start us, length us, event | category | flops | bytes accessed | tf_op | source)
XLA Modules:
  0.0 118.3 jit_solution(15898667176007574444)
XLA Ops:
  0.6 0.9 copy.38
  1.5 4.4 %collective-permute-start = (bf16[1,8,16,128]{3,2,0,1:T(8,128)(2,1)S(1)}, bf16[1,8,16,128]{3,2,0,1:T(8,128)(2,1)S(1)}, u32[]{:S(2)}, u32[]{:S(2)}) collective-permute-start(bf16[1,8,16,128]{3,2,0,1:T(8,128)(2,1)S(1)} %get-tuple-element.34), channel_id=1, source_target_pairs={{0,4},{4,8},{8,12},{12,16},{16,20},{20,24},{24,28},{28,32},{32,36}... | collective-permute-start | bytes 98312 | tf_op jit(solution)/shard_map/ppermute | solution.py:116
  5.9 9.5 %collective-permute-start.1 = (bf16[1,8,16,128]{3,2,0,1:T(8,128)(2,1)S(1)}, bf16[1,8,16,128]{3,2,0,1:T(8,128)(2,1)S(1)}, u32[]{:S(2)}, u32[]{:S(2)}) collective-permute-start(bf16[1,8,16,128]{3,2,0,1:T(8,128)(2,1)S(1)} %get-tuple-element.35), channel_id=1, source_target_pairs={{0,60},{4,0},{8,4},{12,8},{16,12},{20,16},{24,20},{28,24},{32,28},... | collective-permute-start | bytes 98312 | tf_op jit(solution)/shard_map/ppermute | solution.py:117
  15.4 0.7 fusion.3
  16.4 0.7 select_select_fusion
  17.1 4.8 %all-to-all-start = ((bf16[4,4,16,128]{3,2,1,0:T(8,128)(2,1)}), bf16[4,4,16,128]{3,2,1,0:T(8,128)(2,1)S(1)}, u32[]{:S(2)}, u32[]{:S(2)}) async-start(bf16[4,4,16,128]{3,2,1,0:T(8,128)(2,1)} %select_select_fusion), calls=%async_computation | async-start | bytes 131072 | tf_op jit(solution)/shard_map/all_to_all | solution.py:129
  21.9 0.9 copy.32
  22.8 2.4 %all-to-all-done = bf16[4,4,16,128]{3,2,1,0:T(8,128)(2,1)S(1)} async-done(((bf16[4,4,16,128]{3,2,1,0:T(8,128)(2,1)}), bf16[4,4,16,128]{3,2,1,0:T(8,128)(2,1)S(1)}, u32[]{:S(2)}, u32[]{:S(2)}) %all-to-all-start) | async-done | bytes 65568 | tf_op jit(solution)/shard_map/all_to_all | solution.py:129
  25.3 1.5 %broadcast_in_dim.77 = bf16[8,57,16,128]{3,2,1,0:T(8,128)(2,1)} broadcast(bf16[57,16,128]{2,1,0:T(8,128)(2,1)S(1)} %pad_maximum_fusion.1), dimensions={1,2,3} | broadcast | bytes 2101248 | tf_op jit(solution)/shard_map/broadcast_in_dim | solution.py:134
  26.8 6.8 %all-to-all-start.1 = ((bf16[8,57,16,128]{3,2,1,0:T(8,128)(2,1)}), bf16[8,57,16,128]{3,2,1,0:T(8,128)(2,1)S(1)}, u32[]{:S(2)}, u32[]{:S(2)}) async-start(bf16[8,57,16,128]{3,2,1,0:T(8,128)(2,1)} %broadcast_in_dim.77), calls=%async_computation.1 | async-start | bytes 3735552 | tf_op jit(solution)/shard_map/all_to_all | solution.py:134
  33.6 1.3 %dynamic-slice_bitcast_fusion = bf16[27,16,128]{1,2,0:T(8,128)(2,1)} fusion(bf16[27,128,128]{2,1,0:T(8,128)(2,1)S(1)} %copy-done, s32[]{:T(128)S(6)} %select_n.26), kind=kLoop, calls=%fused_computation | loop fusion | bytes 221188 | tf_op jit(solution)/shard_map/transpose | solution.py:119
  34.8 1.4 %copy.34 = bf16[27,16,128]{2,1,0:T(8,128)(2,1)S(1)} copy(bf16[27,16,128]{1,2,0:T(8,128)(2,1)} %dynamic-slice_bitcast_fusion) | data formatting | bytes 221184 | tf_op jit(solution)/shard_map/transpose | solution.py:119
  36.3 23.3 %all-to-all-done.1.got = bf16[8,57,16,128]{3,2,1,0:T(8,128)(2,1)S(1)} async-done(((bf16[8,57,16,128]{3,2,1,0:T(8,128)(2,1)}), bf16[8,57,16,128]{3,2,1,0:T(8,128)(2,1)S(1)}, u32[]{:S(2)}, u32[]{:S(2)}) %all-to-all-start.1) | async-done | bytes 1867808 | tf_op jit(solution)/shard_map/all_to_all | solution.py:134
  59.6 4.5 %shard_map.75 = (bf16[2,8,16,128]{3,2,1,0:T(8,128)(2,1)S(1)}, f32[4,176,128]{2,1,0:T(8,128)}, f32[4,8,16,128]{3,2,1,0:T(8,128)S(1)}) custom-call(s32[2]{0:T(128)S(1)} %pad_add_fusion.place, bf16[8,57,16,128]{3,2,1,0:T(8,128)(2,1)S(1)} %all-to-all-done.1.got, bf16[27,128,128]{2,1,0:T(8,128)(2,1)S(1)} %copy-done, bf16[432,128]{1,0:T(8,128)(2,1)S(1)} %bitcast.43), custom_call_target="tpu_custom_call" | custom-call | tf_op jit(solution)/shard_map/pallas_call | solution.py:139
  64.1 4.3 %all-to-all-start.2 = ((f32[4,176,128]{2,1,0:T(8,128)}), f32[4,176,128]{2,1,0:T(8,128)S(1)}, u32[]{:S(2)}, u32[]{:S(2)}) async-start(f32[4,176,128]{2,1,0:T(8,128)} %get-tuple-element.9), calls=%async_computation.2 | async-start | bytes 720896 | tf_op jit(solution)/shard_map/all_to_all | solution.py:158
  68.4 6.2 %all-to-all-done.2 = f32[4,176,128]{2,1,0:T(8,128)S(1)} async-done(((f32[4,176,128]{2,1,0:T(8,128)}), f32[4,176,128]{2,1,0:T(8,128)S(1)}, u32[]{:S(2)}, u32[]{:S(2)}) %all-to-all-start.2) | async-done | bytes 360480 | tf_op jit(solution)/shard_map/all_to_all | solution.py:158
  74.6 0.7 broadcast_in_dim.80
  75.3 3.3 %all-to-all-start.3 = ((bf16[4,112,128]{2,1,0:T(8,128)(2,1)}), bf16[4,112,128]{2,1,0:T(8,128)(2,1)S(1)}, u32[]{:S(2)}, u32[]{:S(2)}) async-start(bf16[4,112,128]{2,1,0:T(8,128)(2,1)} %broadcast_in_dim.80), calls=%async_computation.3 | async-start | bytes 229376 | tf_op jit(solution)/shard_map/all_to_all | solution.py:167
  78.7 3.3 %collective-permute-start.2 = (f32[1,8,16,128]{3,2,1,0:T(8,128)S(1)}, f32[1,8,16,128]{3,2,1,0:T(8,128)S(1)}, u32[]{:S(2)}, u32[]{:S(2)}) collective-permute-start(f32[1,8,16,128]{3,2,1,0:T(8,128)S(1)} %slice.64), channel_id=1, source_target_pairs={{0,4},{4,8},{8,12},{12,16},{16,20},{20,24},{24,28},{28,32},{32,36}... | collective-permute-start | bytes 196616 | tf_op jit(solution)/shard_map/ppermute | solution.py:163
  82.0 1.3 %all-to-all-done.3 = bf16[4,112,128]{2,1,0:T(8,128)(2,1)S(1)} async-done(((bf16[4,112,128]{2,1,0:T(8,128)(2,1)}), bf16[4,112,128]{2,1,0:T(8,128)(2,1)S(1)}, u32[]{:S(2)}, u32[]{:S(2)}) %all-to-all-start.3) | async-done | bytes 114720 | tf_op jit(solution)/shard_map/all_to_all | solution.py:167
  83.4 0.7 broadcast_in_dim.81
  84.0 9.6 %all-to-all-start.4 = ((bf16[4,112,128]{2,1,0:T(8,128)(2,1)}), bf16[4,112,128]{2,1,0:T(8,128)(2,1)S(1)}, u32[]{:S(2)}, u32[]{:S(2)}) async-start(bf16[4,112,128]{2,1,0:T(8,128)(2,1)} %broadcast_in_dim.81), calls=%async_computation.4 | async-start | bytes 229376 | tf_op jit(solution)/shard_map/all_to_all | solution.py:169
  93.6 5.7 %collective-permute-start.3 = (f32[1,8,16,128]{3,2,1,0:T(8,128)S(1)}, f32[1,8,16,128]{3,2,1,0:T(8,128)S(1)}, u32[]{:S(2)}, u32[]{:S(2)}) collective-permute-start(f32[1,8,16,128]{3,2,1,0:T(8,128)S(1)} %get-tuple-element.29), channel_id=1, source_target_pairs={{0,60},{4,0},{8,4},{12,8},{16,12},{20,16},{24,20},{28,24},{32,28},... | collective-permute-start | bytes 196616 | tf_op jit(solution)/shard_map/ppermute | solution.py:164
  99.3 0.6 copy.35
  99.9 0.7 collective-permute-done.3
  100.6 4.9 %all-to-all-done.4 = bf16[4,112,128]{2,1,0:T(8,128)(2,1)S(1)} async-done(((bf16[4,112,128]{2,1,0:T(8,128)(2,1)}), bf16[4,112,128]{2,1,0:T(8,128)(2,1)S(1)}, u32[]{:S(2)}, u32[]{:S(2)}) %all-to-all-start.4) | async-done | bytes 114720 | tf_op jit(solution)/shard_map/all_to_all | solution.py:169
  105.6 0.7 broadcast_in_dim.82
  106.2 7.3 %all-to-all-start.5 = ((bf16[4,112,128]{2,1,0:T(8,128)(2,1)}), bf16[4,112,128]{2,1,0:T(8,128)(2,1)S(1)}, u32[]{:S(2)}, u32[]{:S(2)}) async-start(bf16[4,112,128]{2,1,0:T(8,128)(2,1)} %broadcast_in_dim.82), calls=%async_computation.5 | async-start | bytes 229376 | tf_op jit(solution)/shard_map/all_to_all | solution.py:171
  113.6 0.6 copy.36
  114.2 2.8 %all-to-all-done.5 = bf16[4,112,128]{2,1,0:T(8,128)(2,1)S(1)} async-done(((bf16[4,112,128]{2,1,0:T(8,128)(2,1)}), bf16[4,112,128]{2,1,0:T(8,128)(2,1)S(1)}, u32[]{:S(2)}, u32[]{:S(2)}) %all-to-all-start.5) | async-done | bytes 114720 | tf_op jit(solution)/shard_map/all_to_all | solution.py:171
  117.0 0.7 slice.68
  117.7 0.6 fusion.7
  (30 shorter events, 0.7 us)
Async XLA Ops:
  1.5 14.7 %collective-permute-start = (bf16[1,8,16,128]{3,2,0,1:T(8,128)(2,1)S(1)}, bf16[1,8,16,128]{3,2,0,1:T(8,128)(2,1)S(1)}, u32[]{:S(2)}, u32[]{:S(2)}) collective-permute-start(bf16[1,8,16,128]{3,2,0,1:T(8,128)(2,1)S(1)} %get-tuple-element.34), channel_id=1, source_target_pairs={{0,4},{4,8},{8,12},{12,16},{16,20},{20,24},{24,28},{28,32},{32,36}... | collective-permute-start | bytes 98312 | tf_op jit(solution)/shard_map/ppermute | solution.py:116
  5.9 10.5 %collective-permute-start.1 = (bf16[1,8,16,128]{3,2,0,1:T(8,128)(2,1)S(1)}, bf16[1,8,16,128]{3,2,0,1:T(8,128)(2,1)S(1)}, u32[]{:S(2)}, u32[]{:S(2)}) collective-permute-start(bf16[1,8,16,128]{3,2,0,1:T(8,128)(2,1)S(1)} %get-tuple-element.35), channel_id=1, source_target_pairs={{0,60},{4,0},{8,4},{12,8},{16,12},{20,16},{24,20},{28,24},{32,28},... | collective-permute-start | bytes 98312 | tf_op jit(solution)/shard_map/ppermute | solution.py:117
  17.1 8.0 %all-to-all-start = ((bf16[4,4,16,128]{3,2,1,0:T(8,128)(2,1)}), bf16[4,4,16,128]{3,2,1,0:T(8,128)(2,1)S(1)}, u32[]{:S(2)}, u32[]{:S(2)}) async-start(bf16[4,4,16,128]{3,2,1,0:T(8,128)(2,1)} %select_select_fusion), calls=%async_computation | async-start | bytes 131072 | tf_op jit(solution)/shard_map/all_to_all | solution.py:129
  26.8 6.8 %copy-start = (bf16[27,128,128]{2,1,0:T(8,128)(2,1)S(1)}, bf16[27,128,128]{2,1,0:T(8,128)(2,1)}, u32[]{:S(2)}) copy-start(bf16[27,128,128]{2,1,0:T(8,128)(2,1)} %weight.1) | copy-start | bytes 2654212
  26.8 32.9 %all-to-all-start.1 = ((bf16[8,57,16,128]{3,2,1,0:T(8,128)(2,1)}), bf16[8,57,16,128]{3,2,1,0:T(8,128)(2,1)S(1)}, u32[]{:S(2)}, u32[]{:S(2)}) async-start(bf16[8,57,16,128]{3,2,1,0:T(8,128)(2,1)} %broadcast_in_dim.77), calls=%async_computation.1 | async-start | bytes 3735552 | tf_op jit(solution)/shard_map/all_to_all | solution.py:134
  64.1 10.5 %all-to-all-start.2 = ((f32[4,176,128]{2,1,0:T(8,128)}), f32[4,176,128]{2,1,0:T(8,128)S(1)}, u32[]{:S(2)}, u32[]{:S(2)}) async-start(f32[4,176,128]{2,1,0:T(8,128)} %get-tuple-element.9), calls=%async_computation.2 | async-start | bytes 720896 | tf_op jit(solution)/shard_map/all_to_all | solution.py:158
  75.3 8.0 %all-to-all-start.3 = ((bf16[4,112,128]{2,1,0:T(8,128)(2,1)}), bf16[4,112,128]{2,1,0:T(8,128)(2,1)S(1)}, u32[]{:S(2)}, u32[]{:S(2)}) async-start(bf16[4,112,128]{2,1,0:T(8,128)(2,1)} %broadcast_in_dim.80), calls=%async_computation.3 | async-start | bytes 229376 | tf_op jit(solution)/shard_map/all_to_all | solution.py:167
  78.7 14.9 %collective-permute-start.2 = (f32[1,8,16,128]{3,2,1,0:T(8,128)S(1)}, f32[1,8,16,128]{3,2,1,0:T(8,128)S(1)}, u32[]{:S(2)}, u32[]{:S(2)}) collective-permute-start(f32[1,8,16,128]{3,2,1,0:T(8,128)S(1)} %slice.64), channel_id=1, source_target_pairs={{0,4},{4,8},{8,12},{12,16},{16,20},{20,24},{24,28},{28,32},{32,36}... | collective-permute-start | bytes 196616 | tf_op jit(solution)/shard_map/ppermute | solution.py:163
  84.0 21.5 %all-to-all-start.4 = ((bf16[4,112,128]{2,1,0:T(8,128)(2,1)}), bf16[4,112,128]{2,1,0:T(8,128)(2,1)S(1)}, u32[]{:S(2)}, u32[]{:S(2)}) async-start(bf16[4,112,128]{2,1,0:T(8,128)(2,1)} %broadcast_in_dim.81), calls=%async_computation.4 | async-start | bytes 229376 | tf_op jit(solution)/shard_map/all_to_all | solution.py:169
  93.6 7.0 %collective-permute-start.3 = (f32[1,8,16,128]{3,2,1,0:T(8,128)S(1)}, f32[1,8,16,128]{3,2,1,0:T(8,128)S(1)}, u32[]{:S(2)}, u32[]{:S(2)}) collective-permute-start(f32[1,8,16,128]{3,2,1,0:T(8,128)S(1)} %get-tuple-element.29), channel_id=1, source_target_pairs={{0,60},{4,0},{8,4},{12,8},{16,12},{20,16},{24,20},{28,24},{32,28},... | collective-permute-start | bytes 196616 | tf_op jit(solution)/shard_map/ppermute | solution.py:164
  106.2 10.8 %all-to-all-start.5 = ((bf16[4,112,128]{2,1,0:T(8,128)(2,1)}), bf16[4,112,128]{2,1,0:T(8,128)(2,1)S(1)}, u32[]{:S(2)}, u32[]{:S(2)}) async-start(bf16[4,112,128]{2,1,0:T(8,128)(2,1)} %broadcast_in_dim.82), calls=%async_computation.5 | async-start | bytes 229376 | tf_op jit(solution)/shard_map/all_to_all | solution.py:171

commit v2 on v1

v2 whole, which is shorter than its diff:
```python
import functools

import jax
import jax.numpy as jnp
from jax import lax
from jax.experimental import pallas as pl
from jax.experimental.pallas import tpu as pltpu
from jax.sharding import Mesh, PartitionSpec as P

BF = jnp.bfloat16
F32 = jnp.float32
LANE = 128
TAPS = 27


def pack_block(features, cotangent, out, first, last):
    peers = out.shape[0]
    extent_x, extent_y = features.shape[1:3]
    for array, start in ((features, 0), (cotangent, extent_x * extent_y)):
        for x in range(extent_x):
            rows = jnp.swapaxes(array[:, x].astype(F32), 0, 1).astype(BF)
            for p in range(peers):
                out[p, start + x * extent_y : start + (x + 1) * extent_y] = rows
            if start == 0 and x == 0:
                first[...] = rows
            if start == 0 and x == extent_x - 1:
                last[...] = rows


def pack_layer(low, high, south, north, bias, out):
    for p in range(out.shape[0]):
        out[p, 0:8] = low[...]
        out[p, 8:16] = high[...]
        out[p, 16:20] = south[...]
        out[p, 20:24] = north[...]
        out[p, 24:25] = bias[...]


def sum_parts(scale, parts, out):
    total = jnp.sum(parts[...].astype(F32), axis=0)
    if scale != 1.0:
        total = total * jnp.float32(scale)
    for p in range(out.shape[0]):
        out[p] = total.astype(BF)


def unpack_sums(place, parts, weight_out, bias_out):
    piece = parts.shape[1]
    rows, width = weight_out.shape
    chans = bias_out.shape[1]
    for n in range(parts.shape[0]):
        start = n * piece
        values = parts[n].astype(F32)
        if start + piece <= rows:
            weight_out[start : start + piece] = values
        elif start <= rows:
            if start < rows:
                weight_out[start:rows] = values[: rows - start]
            line = values[rows - start : rows - start + 1]
            bias_out[...] = pltpu.roll(line, lax.rem(width - place[0] * chans, width), 1)[:, :chans]


def conv_kernel(
    place, got, halo, weight, own_weight, out_ref, sums_ref, inner_ref, edge_ref, moved, grad, patch, spread, act
):
    chan = place[0]
    peers, _, chans, _ = got.shape
    width = peers * chans
    own = pl.multiple_of(chan * chans, chans)

    def row(index, ref=got):
        return jnp.concatenate([ref[p, index] for p in range(peers)], axis=0)

    def feature(x, y):
        if y == 0 or y == 9:
            return row(16 + (y // 9) * 4 + x, halo)
        if x == 0 or x == 3:
            return row((x // 3) * 8 + y - 1, halo)
        return row((x - 1) * 8 + y - 1)

    for x in range(4):
        for y in range(10):
            tile = feature(x, y)
            lanes = slice(y * LANE, (y + 1) * LANE)
            wide = tile.astype(F32)
            moved[x, 0:width, lanes] = pltpu.roll(wide, 1, 1).astype(BF)
            moved[x, width : 2 * width, lanes] = tile
            moved[x, 2 * width : 3 * width, lanes] = pltpu.roll(wide, LANE - 1, 1).astype(BF)

    bias = jnp.sum(row(24, halo).astype(F32), axis=1, keepdims=True)
    filters = jnp.concatenate([weight[t] for t in range(TAPS)], axis=1)
    half = 4
    for x in range(2):
        for part in range(8 // half):
            y0 = part * half
            span = half * LANE
            cells = jnp.concatenate(
                [moved[x + a, :, (b + y0) * LANE : (b + y0) * LANE + span] for a in range(3) for b in range(3)],
                axis=0,
            )
            pre = jnp.dot(filters, cells, preferred_element_type=F32) + bias
            sigma = jax.nn.sigmoid(pre)
            cot = jnp.concatenate([row(16 + x * 8 + y0 + y) for y in range(half)], axis=1).astype(F32)
            lanes = slice((x * 8 + y0) * LANE, (x * 8 + y0) * LANE + span)
            grad[:, lanes] = (cot * sigma * (1.0 + pre * (1.0 - sigma))).astype(BF)
            act[:, lanes] = (pre * sigma).astype(BF)
    for x in range(2):
        for y in range(8):
            lanes = slice((x * 8 + y) * LANE, (x * 8 + y + 1) * LANE)
            out_ref[x, y] = act[pl.ds(own, chans), lanes]

    for a in range(3):
        for b in range(3):
            for c in range(3):
                t = 9 * a + 3 * b + c
                for x in range(2):
                    patch[t * chans : (t + 1) * chans, x * 1024 : (x + 1) * 1024] = moved[
                        x + a, pl.ds(pl.multiple_of(c * width + own, chans), chans), b * LANE : (b + 8) * LANE
                    ]
    spare = patch.shape[0] - TAPS * chans
    index = lax.broadcasted_iota(jnp.int32, (spare, patch.shape[1]), 0)
    patch[TAPS * chans :, :] = jnp.where(index == 0, 1.0, 0.0).astype(BF)
    sums_ref[...] = lax.dot_general(
        patch[...], grad[...], (((1,), (1,)), ((), ())), preferred_element_type=F32
    ).astype(BF)

    spread[...] = jnp.zeros(spread.shape, F32)
    for x in range(2):
        terms = jnp.dot(own_weight[...], grad[:, x * 1024 : (x + 1) * 1024], preferred_element_type=F32)
        for a in range(3):
            for b in range(3):
                for c in range(3):
                    t = 9 * a + 3 * b + c
                    spread[c, x + a, :, b * LANE : (b + 8) * LANE] += terms[t * chans : (t + 1) * chans]
    for x in range(4):
        for y in range(10):
            lanes = slice(y * LANE, (y + 1) * LANE)
            tile = (
                pltpu.roll(spread[0, x, :, lanes], LANE - 1, 1)
                + spread[1, x, :, lanes]
                + pltpu.roll(spread[2, x, :, lanes], 1, 1)
            )
            if y == 0 or y == 9:
                edge_ref[y // 9, x] = tile
            else:
                inner_ref[x, y - 1] = tile


def on_device(features, weight, bias, cotangent):
    chans, extent_x, extent_y, depth = features.shape
    width = weight.shape[1]
    peers = width // chans
    chan = lax.axis_index("chan")
    count_x = lax.axis_size("zh") * lax.axis_size("zl")
    count_y = lax.axis_size("gy")
    gx_axes = ("zh", "zl")
    up = [(i, (i + 1) % count_x) for i in range(count_x)]
    down = [(i, (i - 1) % count_x) for i in range(count_x)]

    vmem = pl.BlockSpec(memory_space=pltpu.VMEM)
    smem = pl.BlockSpec(memory_space=pltpu.SMEM)

    def call(body, out_shape, *operands, specs=None):
        return pl.pallas_call(
            body,
            out_shape=out_shape,
            in_specs=specs or [vmem] * len(operands),
            out_specs=jax.tree.map(lambda _: vmem, out_shape),
            compiler_params=pltpu.CompilerParams(vmem_limit_bytes=16 * 1024 * 1024),
        )(*operands)

    plane = jax.ShapeDtypeStruct((extent_y, chans, depth), BF)
    parcel, x_first, x_last = call(
        pack_block,
        (jax.ShapeDtypeStruct((peers, 2 * extent_x * extent_y, chans, depth), BF), plane, plane),
        features,
        cotangent,
    )
    got = lax.all_to_all(parcel, "chan", 0, 0)

    low = lax.ppermute(x_last, gx_axes, up)
    high = lax.ppermute(x_first, gx_axes, down)
    right = [(i, (i + 1) % count_y) for i in range(count_y)]
    left = [(i, (i - 1) % count_y) for i in range(count_y)]
    south = lax.ppermute(jnp.stack([low[-1], x_first[-1], x_last[-1], high[-1]]), "gy", right)
    north = lax.ppermute(jnp.stack([low[0], x_first[0], x_last[0], high[0]]), "gy", left)
    first = lax.reduce_precision(bias, 8, 7)
    second = lax.reduce_precision(bias - first, 8, 7)
    third = bias - first - second
    bias_row = jnp.stack([first, second, third], axis=1).astype(BF)
    bias_row = jnp.pad(bias_row, ((0, 0), (0, depth - 3)))[None]
    parcel = call(
        pack_layer,
        jax.ShapeDtypeStruct((peers, 2 * extent_y + 9, chans, depth), BF),
        low,
        high,
        south,
        north,
        bias_row,
    )
    parcel, got = lax.optimization_barrier((parcel, got))
    halo = lax.all_to_all(parcel, "chan", 0, 0)
    own_weight = lax.dynamic_slice_in_dim(weight, chan * chans, chans, 2)
    own_weight = jnp.transpose(own_weight, (0, 2, 1)).reshape(TAPS * chans, width)

    cells = extent_x * extent_y * depth
    near = lax.axis_size("zl") * count_y
    piece = -(-(TAPS * chans + 1) // (near * 16)) * 16
    place = chan.astype(jnp.int32).reshape(1)
    output, sums, inner, edge = pl.pallas_call(
        conv_kernel,
        out_shape=(
            jax.ShapeDtypeStruct((extent_x, extent_y, chans, depth), BF),
            jax.ShapeDtypeStruct((near * piece, width), BF),
            jax.ShapeDtypeStruct((4, extent_y, chans, depth), F32),
            jax.ShapeDtypeStruct((2, 4, chans, depth), F32),
        ),
        in_specs=[smem, vmem, vmem, vmem, vmem],
        out_specs=(vmem, vmem, vmem, vmem),
        scratch_shapes=[
            pltpu.VMEM((4, 3 * width, 10 * LANE), BF),
            pltpu.VMEM((width, cells), BF),
            pltpu.VMEM((near * piece, cells), BF),
            pltpu.VMEM((3, 4, chans, 10 * LANE), F32),
            pltpu.VMEM((width, cells), BF),
        ],
        compiler_params=pltpu.CompilerParams(vmem_limit_bytes=40 * 1024 * 1024),
    )(place, got, halo, weight, own_weight)

    scale = 1.0 / float(count_x * count_y * cells) ** 0.5
    far = lax.axis_size("zh")
    part = lax.all_to_all(sums.reshape(near, piece, width), ("zl", "gy"), 0, 0)
    north = lax.ppermute(edge[0], "gy", left)
    south = lax.ppermute(edge[1], "gy", right)
    part = call(functools.partial(sum_parts, 1.0), jax.ShapeDtypeStruct((far, piece, width), BF), part)
    part = lax.all_to_all(part, "zh", 0, 0)
    inner = jnp.concatenate([inner[:, :1] + south[:, None], inner[:, 1:-1], inner[:, -1:] + north[:, None]], axis=1)
    low = lax.ppermute(inner[-1:], gx_axes, up)
    high = lax.ppermute(inner[:1], gx_axes, down)
    part, low, high = lax.optimization_barrier((part, low, high))
    part = call(functools.partial(sum_parts, scale), jax.ShapeDtypeStruct((near, piece, width), BF), part)
    part = lax.all_to_all(part, ("zl", "gy"), 0, 0)
    whole, bias_grad = call(
        unpack_sums,
        (jax.ShapeDtypeStruct((TAPS * chans, width), F32), jax.ShapeDtypeStruct((1, chans), F32)),
        place,
        part,
        specs=[smem, vmem],
    )
    weight_grad = jnp.transpose(whole.reshape(TAPS, chans, width), (0, 2, 1))
    input_grad = jnp.concatenate([inner[1:2] + low, inner[2:3] + high], axis=0).astype(BF)
    return (
        jnp.transpose(output, (2, 0, 1, 3)),
        jnp.transpose(input_grad, (2, 0, 1, 3)),
        weight_grad,
        bias_grad.reshape(chans),
    )


def solution(mesh):
    split = Mesh(mesh.devices.reshape(8, 4, 4, 4), ("chan", "zh", "zl", "gy"))
    block = P("chan", ("zh", "zl"), "gy", None)
    return jax.shard_map(
        on_device,
        mesh=split,
        in_specs=(block, P(), P("chan"), block),
        out_specs=(block, block, P(None, None, "chan"), P("chan")),
        check_vma=False,
    )
```

time: 119 us -> 112 us (0.941)
  waiting for transfers between devices: 41.8 us -> 30.2 us
  starting transfers between devices: 58.9 us -> 66.1 us
  local copies, waits for them, and re-layouts: 10.7 us -> 5.83 us
  Pallas kernels: 4.48 us -> 7.99 us
  other arithmetic: 1.69 us -> 0.09 us
    all_to_all x6 -> x5, waiting for transfers between devices: 40.9 us -> 18 us  [the longest x1 12.3 us: on_device(): halo = lax.all_to_all(parcel, 'chan', 0, 0)]
    ppermute x2 -> x6, starting transfers between devices: 13.9 us -> 24.4 us  [the longest x1 9.5 us: on_device(): high = lax.ppermute(x_first, gx_axes, down)]
    ppermute x2 -> x6, waiting for transfers between devices: 0.21 us -> 7.23 us  [the longest x1 3.27 us: on_device(): north = lax.ppermute(edge[0], 'gy', left)]
    ppermute x1, waiting for transfers between devices: 0.01 us -> 4.93 us  [on_device(): low = lax.ppermute(inner[-1:], gx_axes, up)]
    pallas_call x0 -> x5, Pallas kernels: none -> 4.1 us  [call(): pl.pallas_call(body, out_shape=out_shape, in_specs=specs or [vmem] * len(...]
    all_to_all x6 -> x5, starting transfers between devices: 36 us -> 32.5 us  [the longest x1 9.76 us: on_device(): part = lax.all_to_all(part, 'zh', 0, 0)]
    broadcast_in_dim x5 -> x0, local copies, waits for them, and re-layouts: 3.5 us -> none  [the longest x1 1.51 us: on_device(): jnp.broadcast_to(parcel, (peers,) + parcel.shape)]
    ppermute x1, starting transfers between devices: 5.69 us -> 7.29 us  [on_device(): high = lax.ppermute(inner[:1], gx_axes, down)]
  transfers between devices with their start and end apart: 10 -> 13, of which waited for: 8 -> 7; matrix products, arithmetic and copies ran while one was open for 5% -> 4% of each run, Pallas kernels for 0% -> 1%
where the time goes in v2:
time: 112 us; the launch traced here: 111 us
  starting transfers between devices  66.1 us (59%)
  waiting for transfers between devices  30.2 us (27%)
  Pallas kernels  7.99 us (7%)
  local copies, waits for them, and re-layouts  5.83 us (5%)
    all_to_all x1, waiting for transfers between devices, on_device(): halo = lax.all_to_all(parcel, 'chan', 0, 0)  12.3 us
    all_to_all x1, starting transfers between devices, on_device(): part = lax.all_to_all(part, 'zh', 0, 0)  9.76 us
    ppermute x1, starting transfers between devices, on_device(): high = lax.ppermute(x_first, gx_axes, down)  9.5 us
    all_to_all x1, starting transfers between devices, on_device(): halo = lax.all_to_all(parcel, 'chan', 0, 0)  7.67 us
    all_to_all x1, starting transfers between devices, on_device(): got = lax.all_to_all(parcel, 'chan', 0, 0)  7.48 us
    ppermute x1, starting transfers between devices, on_device(): high = lax.ppermute(inner[:1], gx_axes, down)  7.29 us
    all_to_all x1, waiting for transfers between devices, on_device(): part = lax.all_to_all(part, ('zl', 'gy'), 0, 0)  5.62 us
    ppermute x1, waiting for transfers between devices, on_device(): low = lax.ppermute(inner[-1:], gx_axes, up)  4.93 us
  transfers between devices with their start and end apart: 13, of which 7 were waited for; matrix products, arithmetic and copies ran while one was open for 4% of the time, Pallas kernels for 1%

profile of v2, /device:TPU:1, one launch (start us, length us, event | category | flops | bytes accessed | tf_op | source)
XLA Modules:
  0.0 111.1 jit_solution(259125733582682282)
XLA Ops:
  0.6 0.8 copy-done.1
  1.5 0.8 copy-done.2
  2.3 1.1 shard_map.75
  3.4 7.5 %all-to-all-start = ((bf16[8,32,16,128]{3,2,1,0:T(8,128)(2,1)}), bf16[8,32,16,128]{3,2,1,0:T(8,128)(2,1)S(1)}, u32[]{:S(2)}, u32[]{:S(2)}) async-start(bf16[8,32,16,128]{3,2,1,0:T(8,128)(2,1)} %get-tuple-element.20), calls=%async_computation | async-start | bytes 2097152 | tf_op jit(solution)/shard_map/all_to_all | solution.py:179
  10.9 3.5 %collective-permute-start = (bf16[8,16,128]{2,1,0:T(8,128)(2,1)S(1)}, bf16[8,16,128]{2,1,0:T(8,128)(2,1)S(1)}, u32[]{:S(2)}, u32[]{:S(2)}) collective-permute-start(bf16[8,16,128]{2,1,0:T(8,128)(2,1)S(1)} %get-tuple-element.18), channel_id=1, source_target_pairs={{0,4},{4,8},{8,12},{12,16},{16,20},{20,24},{24,28},{28,32},{32,36}... | collective-permute-start | bytes 98312 | tf_op jit(solution)/shard_map/ppermute | solution.py:181
  14.4 9.5 %collective-permute-start.1 = (bf16[8,16,128]{2,1,0:T(8,128)(2,1)S(1)}, bf16[8,16,128]{2,1,0:T(8,128)(2,1)S(1)}, u32[]{:S(2)}, u32[]{:S(2)}) collective-permute-start(bf16[8,16,128]{2,1,0:T(8,128)(2,1)S(1)} %get-tuple-element.19), channel_id=1, source_target_pairs={{0,60},{4,0},{8,4},{12,8},{16,12},{20,16},{24,20},{28,24},{32,28},... | collective-permute-start | bytes 98312 | tf_op jit(solution)/shard_map/ppermute | solution.py:182
  24.1 0.8 collective-permute-done.1.high
  24.9 4.0 %collective-permute-start.2 = (bf16[4,16,128]{2,1,0:T(8,128)(2,1)S(1)}, bf16[4,16,128]{2,1,0:T(8,128)(2,1)S(1)}, u32[]{:S(2)}, u32[]{:S(2)}) collective-permute-start(bf16[4,16,128]{2,1,0:T(8,128)(2,1)S(1)} %pad_maximum_fusion.1), channel_id=1, source_target_pairs={{0,1},{1,2},{2,3},{3,0},{4,5},{5,6},{6,7},{7,4},{8,9},{9,10},{10,1... | collective-permute-start | bytes 49160 | tf_op jit(solution)/shard_map/ppermute | solution.py:185
  29.0 1.9 %collective-permute-start.3 = (bf16[4,16,128]{2,1,0:T(8,128)(2,1)S(1)}, bf16[4,16,128]{2,1,0:T(8,128)(2,1)S(1)}, u32[]{:S(2)}, u32[]{:S(2)}) collective-permute-start(bf16[4,16,128]{2,1,0:T(8,128)(2,1)S(1)} %pad_maximum_fusion.2), channel_id=1, source_target_pairs={{0,3},{1,0},{2,1},{3,2},{4,7},{5,4},{6,5},{7,6},{8,11},{9,8},{10,9... | collective-permute-start | bytes 49160 | tf_op jit(solution)/shard_map/ppermute | solution.py:186
  30.9 3.1 %collective-permute-done.3.north = bf16[4,16,128]{2,1,0:T(8,128)(2,1)S(1)} collective-permute-done((bf16[4,16,128]{2,1,0:T(8,128)(2,1)S(1)}, bf16[4,16,128]{2,1,0:T(8,128)(2,1)S(1)}, u32[]{:S(2)}, u32[]{:S(2)}) %collective-permute-start.3) | collective-permute-done | bytes 16416 | tf_op jit(solution)/shard_map/ppermute | solution.py:186
  34.0 1.0 shard_map.76
  35.0 7.7 %all-to-all-start.1 = ((bf16[8,25,16,128]{3,2,1,0:T(8,128)(2,1)}), bf16[8,25,16,128]{3,2,1,0:T(8,128)(2,1)S(1)}, u32[]{:S(2)}, u32[]{:S(2)}) async-start(bf16[8,25,16,128]{3,2,1,0:T(8,128)(2,1)} %shard_map.76), calls=%async_computation.1 | async-start | bytes 1638400 | tf_op jit(solution)/shard_map/all_to_all | solution.py:202
  42.7 1.3 %dynamic-slice_bitcast_fusion = bf16[27,16,128]{1,2,0:T(8,128)(2,1)} fusion(bf16[27,128,128]{2,1,0:T(8,128)(2,1)S(1)} %copy-done, s32[]{:T(128)S(6)} %select_n.3), kind=kLoop, calls=%fused_computation | loop fusion | bytes 221188 | tf_op jit(solution)/shard_map/transpose | solution.py:204
  44.0 1.4 %copy.19 = bf16[27,16,128]{2,1,0:T(8,128)(2,1)S(1)} copy(bf16[27,16,128]{1,2,0:T(8,128)(2,1)} %dynamic-slice_bitcast_fusion) | data formatting | bytes 221184 | tf_op jit(solution)/shard_map/transpose | solution.py:204
  45.4 12.3 %all-to-all-done.1.halo = bf16[8,25,16,128]{3,2,1,0:T(8,128)(2,1)S(1)} async-done(((bf16[8,25,16,128]{3,2,1,0:T(8,128)(2,1)}), bf16[8,25,16,128]{3,2,1,0:T(8,128)(2,1)S(1)}, u32[]{:S(2)}, u32[]{:S(2)}) %all-to-all-start.1) | async-done | bytes 819232 | tf_op jit(solution)/shard_map/all_to_all | solution.py:202
  57.8 3.9 %shard_map.77 = (bf16[2,8,16,128]{3,2,1,0:T(8,128)(2,1)S(1)}, bf16[512,128]{1,0:T(8,128)(2,1)}, f32[4,8,16,128]{3,2,1,0:T(8,128)S(1)}, f32[2,4,16,128]{3,2,1,0:T(8,128)S(1)}) custom-call(s32[1]{0:T(128)} %bitcast.place, bf16[8,32,16,128]{3,2,1,0:T(8,128)(2,1)S(1)} %all-to-all-done.got, bf16[8,25,16,128]{3,2,1,0:T(8,128)(2,1)S(1)} %all-to-all-done.1.halo, ...), custom_call_target="tpu_custom_call" | custom-call | tf_op jit(solution)/shard_map/pallas_call | solution.py:210
  61.6 3.7 %all-to-all-start.2 = ((bf16[16,32,128]{2,1,0:T(8,128)(2,1)}), bf16[16,32,128]{2,1,0:T(8,128)(2,1)S(1)}, u32[]{:S(2)}, u32[]{:S(2)}) async-start(bf16[16,32,128]{2,1,0:T(8,128)(2,1)} %bitcast.14), calls=%async_computation.2 | async-start | bytes 262144 | tf_op jit(solution)/shard_map/all_to_all | solution.py:232
  65.3 3.5 %collective-permute-start.4 = (f32[4,16,128]{2,1,0:T(8,128)S(1)}, f32[4,16,128]{2,1,0:T(8,128)S(1)}, u32[]{:S(2)}, u32[]{:S(2)}) collective-permute-start(f32[4,16,128]{2,1,0:T(8,128)S(1)} %get-tuple-element.46), channel_id=1, source_target_pairs={{0,1},{1,2},{2,3},{3,0},{4,5},{5,6},{6,7},{7,4},{8,9},{9,10},{10,1... | collective-permute-start | bytes 98312 | tf_op jit(solution)/shard_map/ppermute | solution.py:234
  68.9 1.9 %collective-permute-start.5 = (f32[4,16,128]{2,1,0:T(8,128)S(1)}, f32[4,16,128]{2,1,0:T(8,128)S(1)}, u32[]{:S(2)}, u32[]{:S(2)}) collective-permute-start(f32[4,16,128]{2,1,0:T(8,128)S(1)} %get-tuple-element.47), channel_id=1, source_target_pairs={{0,3},{1,0},{2,1},{3,2},{4,7},{5,4},{6,5},{7,6},{8,11},{9,8},{10,9... | collective-permute-start | bytes 98312 | tf_op jit(solution)/shard_map/ppermute | solution.py:233
  70.9 3.3 %collective-permute-done.5 = f32[4,16,128]{2,1,0:T(8,128)S(1)} collective-permute-done((f32[4,16,128]{2,1,0:T(8,128)S(1)}, f32[4,16,128]{2,1,0:T(8,128)S(1)}, u32[]{:S(2)}, u32[]{:S(2)}) %collective-permute-start.5) | collective-permute-done | bytes 32800 | tf_op jit(solution)/shard_map/ppermute | solution.py:233
  74.2 0.6 shard_map.78
  74.8 9.8 %all-to-all-start.3 = ((bf16[4,32,128]{2,1,0:T(8,128)(2,1)}), bf16[4,32,128]{2,1,0:T(8,128)(2,1)S(1)}, u32[]{:S(2)}, u32[]{:S(2)}) async-start(bf16[4,32,128]{2,1,0:T(8,128)(2,1)} %shard_map.78), calls=%async_computation.3 | async-start | bytes 65536 | tf_op jit(solution)/shard_map/all_to_all | solution.py:236
  84.6 7.3 %collective-permute-start.7 = (f32[1,8,16,128]{3,2,1,0:T(8,128)S(1)}, f32[1,8,16,128]{3,2,1,0:T(8,128)S(1)}, u32[]{:S(2)}, u32[]{:S(2)}) collective-permute-start(f32[1,8,16,128]{3,2,1,0:T(8,128)S(1)} %get-tuple-element.42), channel_id=1, source_target_pairs={{0,60},{4,0},{8,4},{12,8},{16,12},{20,16},{24,20},{28,24},{32,28},... | collective-permute-start | bytes 196616 | tf_op jit(solution)/shard_map/ppermute | solution.py:239
  91.9 1.9 %collective-permute-start.6 = (f32[1,8,16,128]{3,2,1,0:T(8,128)S(1)}, f32[1,8,16,128]{3,2,1,0:T(8,128)S(1)}, u32[]{:S(2)}, u32[]{:S(2)}) collective-permute-start(f32[1,8,16,128]{3,2,1,0:T(8,128)S(1)} %get-tuple-element.43), channel_id=1, source_target_pairs={{0,4},{4,8},{8,12},{12,16},{16,20},{20,24},{24,28},{28,32},{32,36}... | collective-permute-start | bytes 196616 | tf_op jit(solution)/shard_map/ppermute | solution.py:238
  93.8 0.1 collective-permute-done.7
  93.9 4.9 %collective-permute-done.6 = f32[1,8,16,128]{3,2,1,0:T(8,128)S(1)} collective-permute-done((f32[1,8,16,128]{3,2,1,0:T(8,128)S(1)}, f32[1,8,16,128]{3,2,1,0:T(8,128)S(1)}, u32[]{:S(2)}, u32[]{:S(2)}) %collective-permute-start.6) | collective-permute-done | bytes 65568 | tf_op jit(solution)/shard_map/ppermute | solution.py:238
  98.9 0.7 shard_map.79
  99.5 3.9 %all-to-all-start.4 = ((bf16[16,32,128]{2,1,0:T(8,128)(2,1)}), bf16[16,32,128]{2,1,0:T(8,128)(2,1)S(1)}, u32[]{:S(2)}, u32[]{:S(2)}) async-start(bf16[16,32,128]{2,1,0:T(8,128)(2,1)} %shard_map.79), calls=%async_computation.4 | async-start | bytes 262144 | tf_op jit(solution)/shard_map/all_to_all | solution.py:242
  103.5 0.6 copy.24
  104.2 0.6 copy.25
  104.8 5.6 %all-to-all-done.4.parts = bf16[16,32,128]{2,1,0:T(8,128)(2,1)S(1)} async-done(((bf16[16,32,128]{2,1,0:T(8,128)(2,1)}), bf16[16,32,128]{2,1,0:T(8,128)(2,1)S(1)}, u32[]{:S(2)}, u32[]{:S(2)}) %all-to-all-start.4) | async-done | bytes 131104 | tf_op jit(solution)/shard_map/all_to_all | solution.py:242
  110.4 0.7 shard_map.80
  (28 shorter events, 0.3 us)
Async XLA Ops:
  0.6 0.8 copy-start.1
  1.5 0.8 copy-start.2
  3.4 31.6 %all-to-all-start = ((bf16[8,32,16,128]{3,2,1,0:T(8,128)(2,1)}), bf16[8,32,16,128]{3,2,1,0:T(8,128)(2,1)S(1)}, u32[]{:S(2)}, u32[]{:S(2)}) async-start(bf16[8,32,16,128]{3,2,1,0:T(8,128)(2,1)} %get-tuple-element.20), calls=%async_computation | async-start | bytes 2097152 | tf_op jit(solution)/shard_map/all_to_all | solution.py:179
  10.9 13.2 %collective-permute-start = (bf16[8,16,128]{2,1,0:T(8,128)(2,1)S(1)}, bf16[8,16,128]{2,1,0:T(8,128)(2,1)S(1)}, u32[]{:S(2)}, u32[]{:S(2)}) collective-permute-start(bf16[8,16,128]{2,1,0:T(8,128)(2,1)S(1)} %get-tuple-element.18), channel_id=1, source_target_pairs={{0,4},{4,8},{8,12},{12,16},{16,20},{20,24},{24,28},{28,32},{32,36}... | collective-permute-start | bytes 98312 | tf_op jit(solution)/shard_map/ppermute | solution.py:181
  14.4 9.5 %copy-start.3 = (f32[16]{0:T(128)S(1)}, f32[16]{0:T(128)}, u32[]{:S(2)}) copy-start(f32[16]{0:T(128)} %param.6) | copy-start | bytes 196
  14.4 10.5 %collective-permute-start.1 = (bf16[8,16,128]{2,1,0:T(8,128)(2,1)S(1)}, bf16[8,16,128]{2,1,0:T(8,128)(2,1)S(1)}, u32[]{:S(2)}, u32[]{:S(2)}) collective-permute-start(bf16[8,16,128]{2,1,0:T(8,128)(2,1)S(1)} %get-tuple-element.19), channel_id=1, source_target_pairs={{0,60},{4,0},{8,4},{12,8},{16,12},{20,16},{24,20},{28,24},{32,28},... | collective-permute-start | bytes 98312 | tf_op jit(solution)/shard_map/ppermute | solution.py:182
  24.9 6.0 %collective-permute-start.2 = (bf16[4,16,128]{2,1,0:T(8,128)(2,1)S(1)}, bf16[4,16,128]{2,1,0:T(8,128)(2,1)S(1)}, u32[]{:S(2)}, u32[]{:S(2)}) collective-permute-start(bf16[4,16,128]{2,1,0:T(8,128)(2,1)S(1)} %pad_maximum_fusion.1), channel_id=1, source_target_pairs={{0,1},{1,2},{2,3},{3,0},{4,5},{5,6},{6,7},{7,4},{8,9},{9,10},{10,1... | collective-permute-start | bytes 49160 | tf_op jit(solution)/shard_map/ppermute | solution.py:185
  29.0 5.1 %collective-permute-start.3 = (bf16[4,16,128]{2,1,0:T(8,128)(2,1)S(1)}, bf16[4,16,128]{2,1,0:T(8,128)(2,1)S(1)}, u32[]{:S(2)}, u32[]{:S(2)}) collective-permute-start(bf16[4,16,128]{2,1,0:T(8,128)(2,1)S(1)} %pad_maximum_fusion.2), channel_id=1, source_target_pairs={{0,3},{1,0},{2,1},{3,2},{4,7},{5,4},{6,5},{7,6},{8,11},{9,8},{10,9... | collective-permute-start | bytes 49160 | tf_op jit(solution)/shard_map/ppermute | solution.py:186
  35.0 7.7 %copy-start = (bf16[27,128,128]{2,1,0:T(8,128)(2,1)S(1)}, bf16[27,128,128]{2,1,0:T(8,128)(2,1)}, u32[]{:S(2)}) copy-start(bf16[27,128,128]{2,1,0:T(8,128)(2,1)} %weight.1) | copy-start | bytes 2654212
  35.0 22.7 %all-to-all-start.1 = ((bf16[8,25,16,128]{3,2,1,0:T(8,128)(2,1)}), bf16[8,25,16,128]{3,2,1,0:T(8,128)(2,1)S(1)}, u32[]{:S(2)}, u32[]{:S(2)}) async-start(bf16[8,25,16,128]{3,2,1,0:T(8,128)(2,1)} %shard_map.76), calls=%async_computation.1 | async-start | bytes 1638400 | tf_op jit(solution)/shard_map/all_to_all | solution.py:202
  61.6 12.5 %all-to-all-start.2 = ((bf16[16,32,128]{2,1,0:T(8,128)(2,1)}), bf16[16,32,128]{2,1,0:T(8,128)(2,1)S(1)}, u32[]{:S(2)}, u32[]{:S(2)}) async-start(bf16[16,32,128]{2,1,0:T(8,128)(2,1)} %bitcast.14), calls=%async_computation.2 | async-start | bytes 262144 | tf_op jit(solution)/shard_map/all_to_all | solution.py:232
  65.3 5.5 %collective-permute-start.4 = (f32[4,16,128]{2,1,0:T(8,128)S(1)}, f32[4,16,128]{2,1,0:T(8,128)S(1)}, u32[]{:S(2)}, u32[]{:S(2)}) collective-permute-start(f32[4,16,128]{2,1,0:T(8,128)S(1)} %get-tuple-element.46), channel_id=1, source_target_pairs={{0,1},{1,2},{2,3},{3,0},{4,5},{5,6},{6,7},{7,4},{8,9},{9,10},{10,1... | collective-permute-start | bytes 98312 | tf_op jit(solution)/shard_map/ppermute | solution.py:234
  68.9 5.2 %collective-permute-start.5 = (f32[4,16,128]{2,1,0:T(8,128)S(1)}, f32[4,16,128]{2,1,0:T(8,128)S(1)}, u32[]{:S(2)}, u32[]{:S(2)}) collective-permute-start(f32[4,16,128]{2,1,0:T(8,128)S(1)} %get-tuple-element.47), channel_id=1, source_target_pairs={{0,3},{1,0},{2,1},{3,2},{4,7},{5,4},{6,5},{7,6},{8,11},{9,8},{10,9... | collective-permute-start | bytes 98312 | tf_op jit(solution)/shard_map/ppermute | solution.py:233
  74.8 24.1 %all-to-all-start.3 = ((bf16[4,32,128]{2,1,0:T(8,128)(2,1)}), bf16[4,32,128]{2,1,0:T(8,128)(2,1)S(1)}, u32[]{:S(2)}, u32[]{:S(2)}) async-start(bf16[4,32,128]{2,1,0:T(8,128)(2,1)} %shard_map.78), calls=%async_computation.3 | async-start | bytes 65536 | tf_op jit(solution)/shard_map/all_to_all | solution.py:236
  84.6 9.3 %collective-permute-start.7 = (f32[1,8,16,128]{3,2,1,0:T(8,128)S(1)}, f32[1,8,16,128]{3,2,1,0:T(8,128)S(1)}, u32[]{:S(2)}, u32[]{:S(2)}) collective-permute-start(f32[1,8,16,128]{3,2,1,0:T(8,128)S(1)} %get-tuple-element.42), channel_id=1, source_target_pairs={{0,60},{4,0},{8,4},{12,8},{16,12},{20,16},{24,20},{28,24},{32,28},... | collective-permute-start | bytes 196616 | tf_op jit(solution)/shard_map/ppermute | solution.py:239
  91.9 7.0 %collective-permute-start.6 = (f32[1,8,16,128]{3,2,1,0:T(8,128)S(1)}, f32[1,8,16,128]{3,2,1,0:T(8,128)S(1)}, u32[]{:S(2)}, u32[]{:S(2)}) collective-permute-start(f32[1,8,16,128]{3,2,1,0:T(8,128)S(1)} %get-tuple-element.43), channel_id=1, source_target_pairs={{0,4},{4,8},{8,12},{12,16},{16,20},{20,24},{24,28},{28,32},{32,36}... | collective-permute-start | bytes 196616 | tf_op jit(solution)/shard_map/ppermute | solution.py:238
  99.5 10.9 %all-to-all-start.4 = ((bf16[16,32,128]{2,1,0:T(8,128)(2,1)}), bf16[16,32,128]{2,1,0:T(8,128)(2,1)S(1)}, u32[]{:S(2)}, u32[]{:S(2)}) async-start(bf16[16,32,128]{2,1,0:T(8,128)(2,1)} %shard_map.79), calls=%async_computation.4 | async-start | bytes 262144 | tf_op jit(solution)/shard_map/all_to_all | solution.py:242

commit v3 on v2

v3 whole, which is shorter than its diff:
```python
import functools

import jax
import jax.numpy as jnp
from jax import lax
from jax.experimental import pallas as pl
from jax.experimental.pallas import tpu as pltpu
from jax.sharding import Mesh, PartitionSpec as P

BF = jnp.bfloat16
F32 = jnp.float32
LANE = 128
TAPS = 27


def pack_block(features_hbm, cotangent_hbm, bias_hbm, out, x_send, y_send, features, cotangent, bias, arrived):
    copies = [
        pltpu.make_async_copy(source, target, arrived.at[n])
        for n, (source, target) in enumerate(
            ((features_hbm, features), (cotangent_hbm, cotangent), (bias_hbm, bias))
        )
    ]
    for copy in copies:
        copy.start()
    for copy in copies:
        copy.wait()
    cells = 2 * 8
    for x in range(2):
        rows = jnp.swapaxes(features[:, x].astype(F32), 0, 1).astype(BF)
        x_send[x * 8 : (x + 1) * 8] = rows
        y_send[2 * x : 2 * x + 2] = rows[0:2]
        for p in range(out.shape[0]):
            out[p, x * 8 : (x + 1) * 8] = rows
    x_send[cells:] = jnp.swapaxes(cotangent[:, 0].astype(F32), 0, 1).astype(BF)
    rows = jnp.swapaxes(cotangent[:, 1].astype(F32), 0, 1).astype(BF)
    y_send[4:5] = rows[0:1]
    chans = bias.shape[1]
    line = lax.broadcasted_iota(jnp.int32, (chans, chans), 0)
    lane = lax.broadcasted_iota(jnp.int32, (chans, chans), 1)
    column = jnp.sum(jnp.where(line == lane, jnp.broadcast_to(bias[...], (chans, chans)), 0.0), axis=1, keepdims=True)
    first = column.astype(BF).astype(F32)
    second = (column - first).astype(BF).astype(F32)
    third = column - first - second
    lane = lax.broadcasted_iota(jnp.int32, (chans, LANE), 1)
    parts = jnp.where(lane == 0, first, jnp.where(lane == 1, second, jnp.where(lane == 2, third, 0.0)))
    for p in range(out.shape[0]):
        out[p, cells] = parts.astype(BF)
        out[p, cells + 1 :] = rows[1:]


def pack_edge(own, from_x, out):
    out[0:4] = own[0:4]
    out[4:6] = from_x[0:2]
    out[6:8] = from_x[8:10]
    out[8:9] = own[4:5]
    out[9:10] = from_x[16:17]


def pack_layer(from_x, from_y, out):
    for p in range(out.shape[0]):
        out[p, 0:16] = from_x[0:16]
        out[p, 16:23] = from_x[17:24]
        out[p, 23:33] = from_y[...]


def add_edge(inner, from_y, keep, send):
    for plane in range(6):
        grad_plane = plane < 4
        rows = 2 if grad_plane else 1
        start = 2 * plane if grad_plane else 8 + plane - 4
        values = inner[plane]
        added = from_y[start : start + rows].astype(F32)
        values = jnp.concatenate([values[0:rows] + added, values[rows:]], axis=0)
        if plane in (0, 1, 4):
            keep[min(plane, 2)] = values
        else:
            send[min(plane - 2, 2)] = values.astype(BF)


def finish(keep, from_x, output, input_grad):
    for x in range(2):
        input_grad[:, x] = jnp.swapaxes(keep[x] + from_x[x].astype(F32), 0, 1).astype(BF)
    output[:, 0] = jnp.swapaxes(from_x[2].astype(F32), 0, 1).astype(BF)
    output[:, 1] = jnp.swapaxes(keep[2], 0, 1).astype(BF)


def sum_parts(scale, parts, out):
    total = jnp.sum(parts[...].astype(F32), axis=0)
    if scale != 1.0:
        total = total * jnp.float32(scale)
    for p in range(out.shape[0]):
        out[p] = total.astype(BF)


def unpack_sums(place, parts, weight_out, bias_out):
    piece = parts.shape[1]
    rows, width = weight_out.shape
    chans = bias_out.shape[1]
    for n in range(parts.shape[0]):
        start = n * piece
        values = parts[n].astype(F32)
        if start + piece <= rows:
            weight_out[start : start + piece] = values
        elif start <= rows:
            if start < rows:
                weight_out[start:rows] = values[: rows - start]
            line = values[rows - start : rows - start + 1]
            bias_out[...] = pltpu.roll(line, lax.rem(width - place[0] * chans, width), 1)[:, :chans]


def conv_kernel(place, got, layer, weight, own_weight, sums_ref, inner_ref, edge_ref, moved, grad, patch, spread, act):
    chan = place[0]
    peers, _, chans, _ = got.shape
    width = peers * chans
    own = pl.multiple_of(chan * chans, chans)

    def row(ref, index):
        return jnp.concatenate([ref[p, index] for p in range(peers)], axis=0)

    def feature(x, y):
        if y >= 8:
            return row(layer, 23 + 2 * x + y - 8)
        return row(got, x * 8 + y) if x < 2 else row(layer, (x - 2) * 8 + y)

    def cotangent(x, y):
        if y == 7:
            return row(layer, 31 + x)
        return row(layer, 16 + y) if x else row(got, 17 + y)

    for x in range(4):
        for y in range(10):
            tile = feature(x, y)
            lanes = slice(y * LANE, (y + 1) * LANE)
            wide = tile.astype(F32)
            moved[x, 0:width, lanes] = pltpu.roll(wide, 1, 1).astype(BF)
            moved[x, width : 2 * width, lanes] = tile
            moved[x, 2 * width : 3 * width, lanes] = pltpu.roll(wide, LANE - 1, 1).astype(BF)

    bias = jnp.sum(row(got, 16).astype(F32), axis=1, keepdims=True)
    filters = jnp.concatenate([weight[t] for t in range(TAPS)], axis=1)
    half = 4
    for x in range(2):
        for part in range(8 // half):
            y0 = part * half
            span = half * LANE
            cells = jnp.concatenate(
                [moved[x + a, :, (b + y0) * LANE : (b + y0) * LANE + span] for a in range(3) for b in range(3)],
                axis=0,
            )
            pre = jnp.dot(filters, cells, preferred_element_type=F32) + bias
            sigma = jax.nn.sigmoid(pre)
            cot = jnp.concatenate([cotangent(x, y0 + y) for y in range(half)], axis=1).astype(F32)
            lanes = slice((x * 8 + y0) * LANE, (x * 8 + y0) * LANE + span)
            grad[:, lanes] = (cot * sigma * (1.0 + pre * (1.0 - sigma))).astype(BF)
            act[:, lanes] = (pre * sigma).astype(BF)
    for x in range(2):
        inner_ref[4 + x, 0] = jnp.zeros((chans, LANE), F32)
        for y in range(8):
            lanes = slice((x * 8 + y) * LANE, (x * 8 + y + 1) * LANE)
            tile = act[pl.ds(own, chans), lanes]
            if y == 7:
                edge_ref[8 + x] = tile
            else:
                inner_ref[4 + x, y + 1] = tile.astype(F32)

    for a in range(3):
        for b in range(3):
            for c in range(3):
                t = 9 * a + 3 * b + c
                for x in range(2):
                    patch[t * chans : (t + 1) * chans, x * 1024 : (x + 1) * 1024] = moved[
                        x + a, pl.ds(pl.multiple_of(c * width + own, chans), chans), b * LANE : (b + 8) * LANE
                    ]
    spare = patch.shape[0] - TAPS * chans
    index = lax.broadcasted_iota(jnp.int32, (spare, patch.shape[1]), 0)
    patch[TAPS * chans :, :] = jnp.where(index == 0, 1.0, 0.0).astype(BF)
    sums_ref[...] = lax.dot_general(
        patch[...], grad[...], (((1,), (1,)), ((), ())), preferred_element_type=F32
    ).astype(BF)

    spread[...] = jnp.zeros(spread.shape, F32)
    for x in range(2):
        terms = jnp.dot(own_weight[...], grad[:, x * 1024 : (x + 1) * 1024], preferred_element_type=F32)
        for a in range(3):
            for b in range(3):
                for c in range(3):
                    t = 9 * a + 3 * b + c
                    spread[c, x + a, :, b * LANE : (b + 8) * LANE] += terms[t * chans : (t + 1) * chans]
    for x in range(4):
        for y in range(10):
            lanes = slice(y * LANE, (y + 1) * LANE)
            tile = (
                pltpu.roll(spread[0, x, :, lanes], LANE - 1, 1)
                + spread[1, x, :, lanes]
                + pltpu.roll(spread[2, x, :, lanes], 1, 1)
            )
            if y >= 8:
                edge_ref[2 * x + y - 8] = tile.astype(BF)
            else:
                inner_ref[x, y] = tile


def on_device(features, weight, bias, cotangent):
    chans, extent_x, extent_y, depth = features.shape
    width = weight.shape[1]
    peers = width // chans
    chan = lax.axis_index("chan")
    count_x = lax.axis_size("zh") * lax.axis_size("zl")
    count_y = lax.axis_size("gy")
    gx_axes = ("zh", "zl")
    up = [(i, (i + 1) % count_x) for i in range(count_x)]
    down = [(i, (i - 1) % count_x) for i in range(count_x)]

    vmem = pl.BlockSpec(memory_space=pltpu.VMEM)
    smem = pl.BlockSpec(memory_space=pltpu.SMEM)

    def call(body, out_shape, *operands, specs=None):
        return pl.pallas_call(
            body,
            out_shape=out_shape,
            in_specs=specs or [vmem] * len(operands),
            out_specs=jax.tree.map(lambda _: vmem, out_shape),
            compiler_params=pltpu.CompilerParams(vmem_limit_bytes=16 * 1024 * 1024),
        )(*operands)

    def rows_of(*shape, dtype=BF):
        return jax.ShapeDtypeStruct((*shape, chans, depth), dtype)

    anywhere = pl.BlockSpec(memory_space=pl.ANY)
    parcel, x_send, y_send = pl.pallas_call(
        pack_block,
        out_shape=(rows_of(peers, 24), rows_of(24), rows_of(5)),
        in_specs=[anywhere] * 3,
        out_specs=(vmem,) * 3,
        scratch_shapes=[
            pltpu.VMEM(features.shape, BF),
            pltpu.VMEM(features.shape, BF),
            pltpu.VMEM((1, chans), F32),
            pltpu.SemaphoreType.DMA((3,)),
        ],
        compiler_params=pltpu.CompilerParams(vmem_limit_bytes=60 * 1024 * 1024),
    )(features, cotangent, bias.reshape(1, chans))
    got = lax.all_to_all(parcel, "chan", 0, 0)

    forth = [(i, (i + 1) % count_y) for i in range(count_y)]
    back = [(i, (i - 1) % count_y) for i in range(count_y)]
    from_x = lax.ppermute(x_send, gx_axes, down)
    from_y = lax.ppermute(call(pack_edge, rows_of(10), y_send, from_x), "gy", back)
    parcel = call(pack_layer, rows_of(peers, 33), from_x, from_y)
    parcel, got = lax.optimization_barrier((parcel, got))
    layer = lax.all_to_all(parcel, "chan", 0, 0)
    own_weight = lax.dynamic_slice_in_dim(weight, chan * chans, chans, 2)
    own_weight = jnp.transpose(own_weight, (0, 2, 1)).reshape(TAPS * chans, width)

    cells = extent_x * extent_y * depth
    near = lax.axis_size("zl") * count_y
    piece = -(-(TAPS * chans + 1) // (near * 16)) * 16
    place = chan.astype(jnp.int32).reshape(1)
    sums, inner, edge = pl.pallas_call(
        conv_kernel,
        out_shape=(
            jax.ShapeDtypeStruct((near * piece, width), BF),
            rows_of(6, extent_y, dtype=F32),
            rows_of(10),
        ),
        in_specs=[smem, vmem, vmem, vmem, vmem],
        out_specs=(vmem, vmem, vmem),
        scratch_shapes=[
            pltpu.VMEM((4, 3 * width, 10 * LANE), BF),
            pltpu.VMEM((width, cells), BF),
            pltpu.VMEM((near * piece, cells), BF),
            pltpu.VMEM((3, 4, chans, 10 * LANE), F32),
            pltpu.VMEM((width, cells), BF),
        ],
        compiler_params=pltpu.CompilerParams(vmem_limit_bytes=40 * 1024 * 1024),
    )(place, got, layer, weight, own_weight)

    scale = 1.0 / float(count_x * count_y * cells) ** 0.5
    far = lax.axis_size("zh")
    run = lax.axis_size("zl")
    middle = [[((i + 1) % run) * count_y + j for i in range(run) for j in range(count_y)]]
    part = lax.all_to_all(sums.reshape(near, piece, width), ("zl", "gy"), 0, 0, axis_index_groups=middle)
    from_y = lax.ppermute(edge, "gy", forth)
    part = call(functools.partial(sum_parts, 1.0), jax.ShapeDtypeStruct((far, piece, width), BF), part)
    part = lax.all_to_all(part, "zh", 0, 0, axis_index_groups=[[(i + far // 2) % far for i in range(far)]])
    keep, send = call(add_edge, (rows_of(3, extent_y, dtype=F32), rows_of(3, extent_y)), inner, from_y)
    part, send = lax.optimization_barrier((part, send))
    from_x = lax.ppermute(send, gx_axes, up)
    part = call(functools.partial(sum_parts, scale), jax.ShapeDtypeStruct((near, piece, width), BF), part)
    part = lax.all_to_all(part, ("zl", "gy"), 0, 0, axis_index_groups=middle)
    whole, bias_grad = call(
        unpack_sums,
        (jax.ShapeDtypeStruct((TAPS * chans, width), F32), jax.ShapeDtypeStruct((1, chans), F32)),
        place,
        part,
        specs=[smem, vmem],
    )
    weight_grad = jnp.transpose(whole.reshape(TAPS, chans, width), (0, 2, 1))
    block = jax.ShapeDtypeStruct(features.shape, BF)
    output, input_grad = call(finish, (block, block), keep, from_x)
    return output, input_grad, weight_grad, bias_grad.reshape(chans)


def solution(mesh):
    split = Mesh(mesh.devices.reshape(8, 8, 2, 4), ("chan", "zh", "zl", "gy"))
    block = P("chan", ("zh", "zl"), "gy", None)
    return jax.shard_map(
        on_device,
        mesh=split,
        in_specs=(block, P(), P("chan"), block),
        out_specs=(block, block, P(None, None, "chan"), P("chan")),
        check_vma=False,
    )
```

time: 112 us -> 99 us (0.88)
  starting transfers between devices: 66.1 us -> 53.1 us
  blocking collectives: 0 us -> 6.89 us
  waiting for transfers between devices: 30.2 us -> 25.8 us
  local copies, waits for them, and re-layouts: 5.83 us -> 2.73 us
  Pallas kernels: 7.99 us -> 9.12 us
    ppermute x8 -> x4, starting transfers between devices: 33.6 us -> 20.1 us  [the longest x1 11.1 us: on_device(): from_x = lax.ppermute(x_send, gx_axes, down)]
    all_to_all x0 -> x1, blocking collectives: none -> 6.89 us  [on_device(): lax.all_to_all(sums.reshape(near, piece, width), ('zl', 'gy'), 0, 0, axis...]
    unnamed x10 -> x6, local copies, waits for them, and re-layouts: 2.98 us -> 0.02 us
    ppermute x8 -> x4, waiting for transfers between devices: 12.3 us -> 9.8 us  [the longest x1 5.15 us: on_device(): from_x = lax.ppermute(send, gx_axes, up)]
    all_to_all x4 -> x3, waiting for transfers between devices: 18 us -> 16 us  [the longest x1 15.1 us: on_device(): layer = lax.all_to_all(parcel, 'chan', 0, 0)]
    pallas_call x1 -> x2, Pallas kernels: 3.89 us -> 5.2 us  [the longest x1 3.28 us: on_device(): pl.pallas_call(conv_kernel, out_shape=(jax.ShapeDtypeStruct((near * piece...]
    all_to_all x4 -> x3, starting transfers between devices: 25.1 us -> 25.4 us  [the longest x1 12.3 us: on_device(): lax.all_to_all(part, 'zh', 0, 0, axis_index_groups=[[(i + far // 2) % far...]
    pallas_call x5 -> x7, Pallas kernels: 4.1 us -> 3.93 us  [call(): pl.pallas_call(body, out_shape=out_shape, in_specs=specs or [vmem] * len(...]
  transfers between devices with their start and end apart: 13 -> 8, of which waited for: 7 -> 6; matrix products, arithmetic and copies ran while one was open for 4% -> 3% of each run, Pallas kernels for 1% -> 2%
where the time goes in v3:
time: 99 us; the launch traced here: 98.3 us
  starting transfers between devices  53.1 us (54%)
  waiting for transfers between devices  25.8 us (26%)
  Pallas kernels  9.12 us (9%)
  blocking collectives  6.89 us (7%)
  local copies, waits for them, and re-layouts  2.73 us (3%)
    all_to_all x1, waiting for transfers between devices, on_device(): layer = lax.all_to_all(parcel, 'chan', 0, 0)  15.1 us
    all_to_all x1, starting transfers between devices, on_device(): lax.all_to_all(part, 'zh', 0, 0, axis_index_groups=[[(i + far // 2) % far...  12.3 us
    ppermute x1, starting transfers between devices, on_device(): from_x = lax.ppermute(x_send, gx_axes, down)  11.1 us
    all_to_all x1, starting transfers between devices, on_device(): layer = lax.all_to_all(parcel, 'chan', 0, 0)  7.65 us
    all_to_all x1, starting transfers between devices, on_device(): got = lax.all_to_all(parcel, 'chan', 0, 0)  7.62 us
    all_to_all x1, blocking collectives, on_device(): lax.all_to_all(sums.reshape(near, piece, width), ('zl', 'gy'), 0, 0, axis...  6.89 us
    all_to_all x1, starting transfers between devices, on_device(): part = lax.all_to_all(part, ('zl', 'gy'), 0, 0, axis_index_groups=middle)  5.5 us
    ppermute x1, waiting for transfers between devices, on_device(): from_x = lax.ppermute(send, gx_axes, up)  5.15 us
  transfers between devices with their start and end apart: 8, of which 6 were waited for; matrix products, arithmetic and copies ran while one was open for 3% of the time, Pallas kernels for 2%

profile of v3, /device:TPU:1, one launch (start us, length us, event | category | flops | bytes accessed | tf_op | source)
XLA Modules:
  0.0 98.3 jit_solution(6599730111516516748)
XLA Ops:
  0.6 1.9 %shard_map.75 = (bf16[8,24,16,128]{3,2,1,0:T(8,128)(2,1)}, bf16[24,16,128]{2,1,0:T(8,128)(2,1)}, bf16[5,16,128]{2,1,0:T(8,128)(2,1)}) custom-call(bf16[16,2,8,128]{3,2,1,0:T(8,128)(2,1)} %features_hbm.1, bf16[16,2,8,128]{3,2,1,0:T(8,128)(2,1)} %cotangent_hbm.1, f32[1,16]{1,0:T(1,128)} %bitcast.12), custom_call_target="tpu_custom_call" | custom-call | tf_op jit(solution)/shard_map/pallas_call | solution.py:230
  2.6 0.0 copy-start.2
  2.6 0.0 copy-start.1
  2.6 7.6 %all-to-all-start = ((bf16[8,24,16,128]{3,2,1,0:T(8,128)(2,1)}), bf16[8,24,16,128]{3,2,1,0:T(8,128)(2,1)S(1)}, u32[]{:S(2)}, u32[]{:S(2)}) async-start(bf16[8,24,16,128]{3,2,1,0:T(8,128)(2,1)} %get-tuple-element.22), calls=%async_computation | async-start | bytes 1572864 | tf_op jit(solution)/shard_map/all_to_all | solution.py:243
  10.2 0.0 copy-done.2
  10.2 11.1 %collective-permute-start = (bf16[24,16,128]{2,1,0:T(8,128)(2,1)S(1)}, bf16[24,16,128]{2,1,0:T(8,128)(2,1)S(1)}, u32[]{:S(2)}, u32[]{:S(2)}) collective-permute-start(bf16[24,16,128]{2,1,0:T(8,128)(2,1)S(1)} %copy-done.2), channel_id=1, source_target_pairs={{0,60},{4,0},{8,4},{12,8},{16,12},{20,16},{24,20},{28,24},{32,28},... | collective-permute-start | bytes 294920 | tf_op jit(solution)/shard_map/ppermute | solution.py:247
  21.3 1.6 %collective-permute-done.from_x = bf16[24,16,128]{2,1,0:T(8,128)(2,1)S(1)} collective-permute-done((bf16[24,16,128]{2,1,0:T(8,128)(2,1)S(1)}, bf16[24,16,128]{2,1,0:T(8,128)(2,1)S(1)}, u32[]{:S(2)}, u32[]{:S(2)}) %collective-permute-start) | collective-permute-done | bytes 98336 | tf_op jit(solution)/shard_map/ppermute | solution.py:247
  23.0 0.0 copy-done.1
  23.0 3.7 %collective-permute-start.1 = (bf16[10,16,128]{2,1,0:T(8,128)(2,1)S(1)}, bf16[10,16,128]{2,1,0:T(8,128)(2,1)S(1)}, u32[]{:S(2)}, u32[]{:S(2)}) collective-permute-start(bf16[10,16,128]{2,1,0:T(8,128)(2,1)S(1)} %shard_map.76), channel_id=1, source_target_pairs={{0,3},{1,0},{2,1},{3,2},{4,7},{5,4},{6,5},{7,6},{8,11},{9,8},{10,9... | collective-permute-start | bytes 122888 | tf_op jit(solution)/shard_map/ppermute | solution.py:248
  26.7 2.0 %collective-permute-done.1.from_y = bf16[10,16,128]{2,1,0:T(8,128)(2,1)S(1)} collective-permute-done((bf16[10,16,128]{2,1,0:T(8,128)(2,1)S(1)}, bf16[10,16,128]{2,1,0:T(8,128)(2,1)S(1)}, u32[]{:S(2)}, u32[]{:S(2)}) %collective-permute-start.1) | collective-permute-done | bytes 40992 | tf_op jit(solution)/shard_map/ppermute | solution.py:248
  28.6 1.1 %shard_map.77 = bf16[8,33,16,128]{3,2,1,0:T(8,128)(2,1)} custom-call(bf16[24,16,128]{2,1,0:T(8,128)(2,1)S(1)} %collective-permute-done.from_x, bf16[10,16,128]{2,1,0:T(8,128)(2,1)S(1)} %collective-permute-done.1.from_y), custom_call_target="tpu_custom_call" | custom-call | tf_op jit(solution)/shard_map/pallas_call | solution.py:218
  29.8 0.0 copy-start
  29.8 0.0 all-to-all-done.got
  29.8 7.7 %all-to-all-start.1 = ((bf16[8,33,16,128]{3,2,1,0:T(8,128)(2,1)}), bf16[8,33,16,128]{3,2,1,0:T(8,128)(2,1)S(1)}, u32[]{:S(2)}, u32[]{:S(2)}) async-start(bf16[8,33,16,128]{3,2,1,0:T(8,128)(2,1)} %shard_map.77), calls=%async_computation.1 | async-start | bytes 2162688 | tf_op jit(solution)/shard_map/all_to_all | solution.py:251
  37.4 0.0 copy-done
  37.4 1.3 %dynamic-slice_bitcast_fusion = bf16[27,16,128]{1,2,0:T(8,128)(2,1)} fusion(bf16[27,128,128]{2,1,0:T(8,128)(2,1)S(1)} %copy-done, s32[]{:T(128)S(6)} %select_n.3), kind=kLoop, calls=%fused_computation | loop fusion | bytes 221188 | tf_op jit(solution)/shard_map/transpose | solution.py:253
  38.7 1.4 %copy.8 = bf16[27,16,128]{2,1,0:T(8,128)(2,1)S(1)} copy(bf16[27,16,128]{1,2,0:T(8,128)(2,1)} %dynamic-slice_bitcast_fusion) | data formatting | bytes 221184 | tf_op jit(solution)/shard_map/transpose | solution.py:253
  40.1 15.1 %all-to-all-done.1.layer = bf16[8,33,16,128]{3,2,1,0:T(8,128)(2,1)S(1)} async-done(((bf16[8,33,16,128]{3,2,1,0:T(8,128)(2,1)}), bf16[8,33,16,128]{3,2,1,0:T(8,128)(2,1)S(1)}, u32[]{:S(2)}, u32[]{:S(2)}) %all-to-all-start.1) | async-done | bytes 1081376 | tf_op jit(solution)/shard_map/all_to_all | solution.py:251
  55.2 3.3 %shard_map.78 = (bf16[512,128]{1,0:T(8,128)(2,1)S(1)}, f32[6,8,16,128]{3,2,1,0:T(8,128)S(1)}, bf16[10,16,128]{2,1,0:T(8,128)(2,1)S(1)}) custom-call(s32[1]{0:T(128)} %bitcast.place, bf16[8,24,16,128]{3,2,1,0:T(8,128)(2,1)S(1)} %all-to-all-done.got, bf16[8,33,16,128]{3,2,1,0:T(8,128)(2,1)S(1)} %all-to-all-done.1.layer, bf16[27,128,128]{2,1,0:T(8,128)(2,1)S(1)} %copy-done, ...), custom_call_target="tpu_custom_call" | custom-call | tf_op jit(solution)/shard_map/pallas_call | solution.py:259
  58.5 6.9 %all_to_all.25.parts = bf16[8,64,128]{2,1,0:T(8,128)(2,1)S(1)} all-to-all(bf16[8,64,128]{2,1,0:T(8,128)(2,1)S(1)} %bitcast.11), channel_id=1, replica_groups={{4,5,6,7,0,1,2,3},{12,13,14,15,8,9,10,11},{20,21,22,23,16,17,18,19},{28..., dimensions={0} | all-to-all | bytes 262144 | tf_op jit(solution)/shard_map/all_to_all | solution.py:282
  65.4 0.7 shard_map.80
  66.1 12.3 %all-to-all-start.3 = ((bf16[8,64,128]{2,1,0:T(8,128)(2,1)}), bf16[8,64,128]{2,1,0:T(8,128)(2,1)S(1)}, u32[]{:S(2)}, u32[]{:S(2)}) async-start(bf16[8,64,128]{2,1,0:T(8,128)(2,1)} %shard_map.80), calls=%async_computation.3 | async-start | bytes 262144 | tf_op jit(solution)/shard_map/all_to_all | solution.py:285
  78.3 3.3 %collective-permute-start.2 = (bf16[10,16,128]{2,1,0:T(8,128)(2,1)S(1)}, bf16[10,16,128]{2,1,0:T(8,128)(2,1)S(1)}, u32[]{:S(2)}, u32[]{:S(2)}) collective-permute-start(bf16[10,16,128]{2,1,0:T(8,128)(2,1)S(1)} %get-tuple-element.26), channel_id=1, source_target_pairs={{0,1},{1,2},{2,3},{3,0},{4,5},{5,6},{6,7},{7,4},{8,9},{9,10},{10,1... | collective-permute-start | bytes 122888 | tf_op jit(solution)/shard_map/ppermute | solution.py:283
  81.6 1.1 %collective-permute-done.2.from_y = bf16[10,16,128]{2,1,0:T(8,128)(2,1)S(1)} collective-permute-done((bf16[10,16,128]{2,1,0:T(8,128)(2,1)S(1)}, bf16[10,16,128]{2,1,0:T(8,128)(2,1)S(1)}, u32[]{:S(2)}, u32[]{:S(2)}) %collective-permute-start.2) | collective-permute-done | bytes 40992 | tf_op jit(solution)/shard_map/ppermute | solution.py:283
  82.7 0.9 all-to-all-done.3.parts
  83.6 0.7 shard_map.82
  84.3 5.5 %all-to-all-start.4 = ((bf16[8,64,128]{2,1,0:T(8,128)(2,1)}), bf16[8,64,128]{2,1,0:T(8,128)(2,1)S(1)}, u32[]{:S(2)}, u32[]{:S(2)}) async-start(bf16[8,64,128]{2,1,0:T(8,128)(2,1)} %shard_map.82), calls=%async_computation.4 | async-start | bytes 262144 | tf_op jit(solution)/shard_map/all_to_all | solution.py:290
  89.8 2.0 %collective-permute-start.3 = (bf16[3,8,16,128]{3,2,1,0:T(8,128)(2,1)S(1)}, bf16[3,8,16,128]{3,2,1,0:T(8,128)(2,1)S(1)}, u32[]{:S(2)}, u32[]{:S(2)}) collective-permute-start(bf16[3,8,16,128]{3,2,1,0:T(8,128)(2,1)S(1)} %get-tuple-element.30), channel_id=1, source_target_pairs={{0,4},{4,8},{8,12},{12,16},{16,20},{20,24},{24,28},{28,32},{32,36}... | collective-permute-start | bytes 294920 | tf_op jit(solution)/shard_map/ppermute | solution.py:288
  91.8 5.1 %collective-permute-done.3.from_x = bf16[3,8,16,128]{3,2,1,0:T(8,128)(2,1)S(1)} collective-permute-done((bf16[3,8,16,128]{3,2,1,0:T(8,128)(2,1)S(1)}, bf16[3,8,16,128]{3,2,1,0:T(8,128)(2,1)S(1)}, u32[]{:S(2)}, u32[]{:S(2)}) %collective-permute-start.3) | collective-permute-done | bytes 98336 | tf_op jit(solution)/shard_map/ppermute | solution.py:288
  96.9 0.7 shard_map.81
  97.6 0.0 all-to-all-done.4.parts
  97.6 0.7 shard_map.83
  (2 shorter events, 0.0 us)
Async XLA Ops:
  2.6 7.7 %copy-start.2 = (bf16[24,16,128]{2,1,0:T(8,128)(2,1)S(1)}, bf16[24,16,128]{2,1,0:T(8,128)(2,1)}, u32[]{:S(2)}) copy-start(bf16[24,16,128]{2,1,0:T(8,128)(2,1)} %get-tuple-element.20) | copy-start | bytes 294916
  2.6 20.4 %copy-start.1 = (bf16[5,16,128]{2,1,0:T(8,128)(2,1)S(1)}, bf16[5,16,128]{2,1,0:T(8,128)(2,1)}, u32[]{:S(2)}) copy-start(bf16[5,16,128]{2,1,0:T(8,128)(2,1)} %get-tuple-element.21.own) | copy-start | bytes 61444
  2.6 27.2 %all-to-all-start = ((bf16[8,24,16,128]{3,2,1,0:T(8,128)(2,1)}), bf16[8,24,16,128]{3,2,1,0:T(8,128)(2,1)S(1)}, u32[]{:S(2)}, u32[]{:S(2)}) async-start(bf16[8,24,16,128]{3,2,1,0:T(8,128)(2,1)} %get-tuple-element.22), calls=%async_computation | async-start | bytes 1572864 | tf_op jit(solution)/shard_map/all_to_all | solution.py:243
  10.2 12.7 %collective-permute-start = (bf16[24,16,128]{2,1,0:T(8,128)(2,1)S(1)}, bf16[24,16,128]{2,1,0:T(8,128)(2,1)S(1)}, u32[]{:S(2)}, u32[]{:S(2)}) collective-permute-start(bf16[24,16,128]{2,1,0:T(8,128)(2,1)S(1)} %copy-done.2), channel_id=1, source_target_pairs={{0,60},{4,0},{8,4},{12,8},{16,12},{20,16},{24,20},{28,24},{32,28},... | collective-permute-start | bytes 294920 | tf_op jit(solution)/shard_map/ppermute | solution.py:247
  23.0 5.7 %collective-permute-start.1 = (bf16[10,16,128]{2,1,0:T(8,128)(2,1)S(1)}, bf16[10,16,128]{2,1,0:T(8,128)(2,1)S(1)}, u32[]{:S(2)}, u32[]{:S(2)}) collective-permute-start(bf16[10,16,128]{2,1,0:T(8,128)(2,1)S(1)} %shard_map.76), channel_id=1, source_target_pairs={{0,3},{1,0},{2,1},{3,2},{4,7},{5,4},{6,5},{7,6},{8,11},{9,8},{10,9... | collective-permute-start | bytes 122888 | tf_op jit(solution)/shard_map/ppermute | solution.py:248
  29.8 7.7 %copy-start = (bf16[27,128,128]{2,1,0:T(8,128)(2,1)S(1)}, bf16[27,128,128]{2,1,0:T(8,128)(2,1)}, u32[]{:S(2)}) copy-start(bf16[27,128,128]{2,1,0:T(8,128)(2,1)} %weight.1) | copy-start | bytes 2654212
  29.8 25.5 %all-to-all-start.1 = ((bf16[8,33,16,128]{3,2,1,0:T(8,128)(2,1)}), bf16[8,33,16,128]{3,2,1,0:T(8,128)(2,1)S(1)}, u32[]{:S(2)}, u32[]{:S(2)}) async-start(bf16[8,33,16,128]{3,2,1,0:T(8,128)(2,1)} %shard_map.77), calls=%async_computation.1 | async-start | bytes 2162688 | tf_op jit(solution)/shard_map/all_to_all | solution.py:251
  66.1 17.6 %all-to-all-start.3 = ((bf16[8,64,128]{2,1,0:T(8,128)(2,1)}), bf16[8,64,128]{2,1,0:T(8,128)(2,1)S(1)}, u32[]{:S(2)}, u32[]{:S(2)}) async-start(bf16[8,64,128]{2,1,0:T(8,128)(2,1)} %shard_map.80), calls=%async_computation.3 | async-start | bytes 262144 | tf_op jit(solution)/shard_map/all_to_all | solution.py:285
  78.3 4.4 %collective-permute-start.2 = (bf16[10,16,128]{2,1,0:T(8,128)(2,1)S(1)}, bf16[10,16,128]{2,1,0:T(8,128)(2,1)S(1)}, u32[]{:S(2)}, u32[]{:S(2)}) collective-permute-start(bf16[10,16,128]{2,1,0:T(8,128)(2,1)S(1)} %get-tuple-element.26), channel_id=1, source_target_pairs={{0,1},{1,2},{2,3},{3,0},{4,5},{5,6},{6,7},{7,4},{8,9},{9,10},{10,1... | collective-permute-start | bytes 122888 | tf_op jit(solution)/shard_map/ppermute | solution.py:283
  84.3 13.3 %all-to-all-start.4 = ((bf16[8,64,128]{2,1,0:T(8,128)(2,1)}), bf16[8,64,128]{2,1,0:T(8,128)(2,1)S(1)}, u32[]{:S(2)}, u32[]{:S(2)}) async-start(bf16[8,64,128]{2,1,0:T(8,128)(2,1)} %shard_map.82), calls=%async_computation.4 | async-start | bytes 262144 | tf_op jit(solution)/shard_map/all_to_all | solution.py:290
  89.8 7.1 %collective-permute-start.3 = (bf16[3,8,16,128]{3,2,1,0:T(8,128)(2,1)S(1)}, bf16[3,8,16,128]{3,2,1,0:T(8,128)(2,1)S(1)}, u32[]{:S(2)}, u32[]{:S(2)}) collective-permute-start(bf16[3,8,16,128]{3,2,1,0:T(8,128)(2,1)S(1)} %get-tuple-element.30), channel_id=1, source_target_pairs={{0,4},{4,8},{8,12},{12,16},{16,20},{20,24},{24,28},{28,32},{32,36}... | collective-permute-start | bytes 294920 | tf_op jit(solution)/shard_map/ppermute | solution.py:288

commit v4 on v3

--- a/solution.py
+++ b/solution.py
@@ -28,12 +28,11 @@
     for x in range(2):
         rows = jnp.swapaxes(features[:, x].astype(F32), 0, 1).astype(BF)
         x_send[x * 8 : (x + 1) * 8] = rows
-        y_send[2 * x : 2 * x + 2] = rows[0:2]
         for p in range(out.shape[0]):
             out[p, x * 8 : (x + 1) * 8] = rows
     x_send[cells:] = jnp.swapaxes(cotangent[:, 0].astype(F32), 0, 1).astype(BF)
     rows = jnp.swapaxes(cotangent[:, 1].astype(F32), 0, 1).astype(BF)
-    y_send[4:5] = rows[0:1]
+    y_send[...] = rows[0:1]
     chans = bias.shape[1]
     line = lax.broadcasted_iota(jnp.int32, (chans, chans), 0)
     lane = lax.broadcasted_iota(jnp.int32, (chans, chans), 1)
@@ -49,18 +48,17 @@
 
 
 def pack_edge(own, from_x, out):
-    out[0:4] = own[0:4]
-    out[4:6] = from_x[0:2]
-    out[6:8] = from_x[8:10]
-    out[8:9] = own[4:5]
-    out[9:10] = from_x[16:17]
+    out[0:2] = from_x[0:2]
+    out[2:4] = from_x[8:10]
+    out[4:5] = own[...]
+    out[5:6] = from_x[16:17]
 
 
 def pack_layer(from_x, from_y, out):
     for p in range(out.shape[0]):
-        out[p, 0:16] = from_x[0:16]
-        out[p, 16:23] = from_x[17:24]
-        out[p, 23:33] = from_y[...]
+        out[p, 0:8] = from_x[0:8]
+        out[p, 8:15] = from_x[17:24]
+        out[p, 15:21] = from_y[...]
 
 
 def add_edge(inner, from_y, keep, send):
@@ -108,7 +106,7 @@
             bias_out[...] = pltpu.roll(line, lax.rem(width - place[0] * chans, width), 1)[:, :chans]
 
 
-def conv_kernel(place, got, layer, weight, own_weight, sums_ref, inner_ref, edge_ref, moved, grad, patch, spread, act):
+def conv_kernel(place, got, layer, beside, across, weight, own_weight, sums_ref, inner_ref, edge_ref, moved, grad, patch, spread, act):
     chan = place[0]
     peers, _, chans, _ = got.shape
     width = peers * chans
@@ -119,13 +117,13 @@
 
     def feature(x, y):
         if y >= 8:
-            return row(layer, 23 + 2 * x + y - 8)
-        return row(got, x * 8 + y) if x < 2 else row(layer, (x - 2) * 8 + y)
+            return row(beside, 2 * x + y - 8) if x < 2 else row(layer, 15 + 2 * (x - 2) + y - 8)
+        return row((got, got, layer, across)[x], 8 * (x % 2) * (x < 2) + y)
 
     def cotangent(x, y):
         if y == 7:
-            return row(layer, 31 + x)
-        return row(layer, 16 + y) if x else row(got, 17 + y)
+            return row(layer, 19 + x)
+        return row(layer, 8 + y) if x else row(got, 17 + y)
 
     for x in range(4):
         for y in range(10):
@@ -229,7 +227,7 @@
     anywhere = pl.BlockSpec(memory_space=pl.ANY)
     parcel, x_send, y_send = pl.pallas_call(
         pack_block,
-        out_shape=(rows_of(peers, 24), rows_of(24), rows_of(5)),
+        out_shape=(rows_of(peers, 24), rows_of(24), rows_of(1)),
         in_specs=[anywhere] * 3,
         out_specs=(vmem,) * 3,
         scratch_shapes=[
@@ -245,16 +243,18 @@
     forth = [(i, (i + 1) % count_y) for i in range(count_y)]
     back = [(i, (i - 1) % count_y) for i in range(count_y)]
     from_x = lax.ppermute(x_send, gx_axes, down)
-    from_y = lax.ppermute(call(pack_edge, rows_of(10), y_send, from_x), "gy", back)
-    parcel = call(pack_layer, rows_of(peers, 33), from_x, from_y)
+    from_y = lax.ppermute(call(pack_edge, rows_of(6), y_send, from_x), "gy", back)
+    parcel = call(pack_layer, rows_of(peers, 21), from_x, from_y)
     parcel, got = lax.optimization_barrier((parcel, got))
     layer = lax.all_to_all(parcel, "chan", 0, 0)
+    across = lax.ppermute(got[:, 8:16], gx_axes, down)
+    beside = lax.ppermute(jnp.concatenate([got[:, 0:2], got[:, 8:10]], axis=1), "gy", back)
     own_weight = lax.dynamic_slice_in_dim(weight, chan * chans, chans, 2)
     own_weight = jnp.transpose(own_weight, (0, 2, 1)).reshape(TAPS * chans, width)
 
     cells = extent_x * extent_y * depth
     near = lax.axis_size("zl") * count_y
-    piece = -(-(TAPS * chans + 1) // (near * 16)) * 16
+    piece = -(-(TAPS * chans + 1) // (near * 8)) * 8
     place = chan.astype(jnp.int32).reshape(1)
     sums, inner, edge = pl.pallas_call(
         conv_kernel,
@@ -263,7 +263,7 @@
             rows_of(6, extent_y, dtype=F32),
             rows_of(10),
         ),
-        in_specs=[smem, vmem, vmem, vmem, vmem],
+        in_specs=[smem] + [vmem] * 6,
         out_specs=(vmem, vmem, vmem),
         scratch_shapes=[
             pltpu.VMEM((4, 3 * width, 10 * LANE), BF),
@@ -273,7 +273,7 @@
             pltpu.VMEM((width, cells), BF),
         ],
         compiler_params=pltpu.CompilerParams(vmem_limit_bytes=40 * 1024 * 1024),
-    )(place, got, layer, weight, own_weight)
+    )(place, got, layer, beside, across, weight, own_weight)
 
     scale = 1.0 / float(count_x * count_y * cells) ** 0.5
     far = lax.axis_size("zh")
@@ -295,6 +295,7 @@
         part,
         specs=[smem, vmem],
     )
+    whole, from_x = lax.optimization_barrier((whole, from_x))
     weight_grad = jnp.transpose(whole.reshape(TAPS, chans, width), (0, 2, 1))
     block = jax.ShapeDtypeStruct(features.shape, BF)
     output, input_grad = call(finish, (block, block), keep, from_x)

time: 99 us -> 93.8 us (0.947)
  waiting for transfers between devices: 25.8 us -> 13.1 us
  starting transfers between devices: 53.1 us -> 60.7 us
    all_to_all x1, waiting for transfers between devices: 15.1 us -> 1.15 us  [on_device(): layer = lax.all_to_all(parcel, 'chan', 0, 0)]
    ppermute x1 -> x3, starting transfers between devices: 3.71 us -> 10.9 us  [the longest x1 5.24 us: on_device(): across = lax.ppermute(got[:, 8:16], gx_axes, down)]
    ppermute x1, waiting for transfers between devices: 5.15 us -> 2.76 us  [on_device(): from_x = lax.ppermute(send, gx_axes, up)]
    ppermute x1 -> x3, waiting for transfers between devices: 1.95 us -> 4.29 us  [the longest x1 2.51 us: on_device(): lax.ppermute(jnp.concatenate([got[:, 0:2], got[:, 8:10]], axis=1), 'gy',...]
    all_to_all x1, waiting for transfers between devices: 0.01 us -> 1.68 us  [on_device(): part = lax.all_to_all(part, ('zl', 'gy'), 0, 0, axis_index_groups=middle)]
  transfers between devices with their start and end apart: 8 -> 10, of which waited for: 6 -> 8; matrix products, arithmetic and copies ran while one was open for 3% -> 3% of each run, Pallas kernels for 2% -> 2%
where the time goes in v4:
time: 93.8 us; the launch traced here: 93.1 us
  starting transfers between devices  60.7 us (65%)
  waiting for transfers between devices  13.1 us (14%)
  Pallas kernels  8.84 us (9%)
  blocking collectives  6.84 us (7%)
  local copies, waits for them, and re-layouts  2.76 us (3%)
    all_to_all x1, starting transfers between devices, on_device(): lax.all_to_all(part, 'zh', 0, 0, axis_index_groups=[[(i + far // 2) % far...  12.3 us
    ppermute x1, starting transfers between devices, on_device(): from_x = lax.ppermute(x_send, gx_axes, down)  11.1 us
    all_to_all x1, starting transfers between devices, on_device(): layer = lax.all_to_all(parcel, 'chan', 0, 0)  7.65 us
    all_to_all x1, starting transfers between devices, on_device(): got = lax.all_to_all(parcel, 'chan', 0, 0)  7.62 us
    all_to_all x1, blocking collectives, on_device(): lax.all_to_all(sums.reshape(near, piece, width), ('zl', 'gy'), 0, 0, axis...  6.84 us
    all_to_all x1, starting transfers between devices, on_device(): part = lax.all_to_all(part, ('zl', 'gy'), 0, 0, axis_index_groups=middle)  6 us
    ppermute x1, starting transfers between devices, on_device(): across = lax.ppermute(got[:, 8:16], gx_axes, down)  5.24 us
    pallas_call x7, Pallas kernels, call(): pl.pallas_call(body, out_shape=out_shape, in_specs=specs or [vmem] * len(...  3.72 us
  transfers between devices with their start and end apart: 10, of which 8 were waited for; matrix products, arithmetic and copies ran while one was open for 3% of the time, Pallas kernels for 2%

profile of v4, /device:TPU:1, one launch (start us, length us, event | category | flops | bytes accessed | tf_op | source)
XLA Modules:
  0.0 93.1 jit_solution(7881277097169176547)
XLA Ops:
  0.6 1.9 %shard_map.75 = (bf16[8,24,16,128]{3,2,1,0:T(8,128)(2,1)}, bf16[24,16,128]{2,1,0:T(8,128)(2,1)}, bf16[1,16,128]{2,1,0:T(8,128)(2,1)}) custom-call(bf16[16,2,8,128]{3,2,1,0:T(8,128)(2,1)} %features_hbm.1, bf16[16,2,8,128]{3,2,1,0:T(8,128)(2,1)} %cotangent_hbm.1, f32[1,16]{1,0:T(1,128)} %bitcast.12), custom_call_target="tpu_custom_call" | custom-call | tf_op jit(solution)/shard_map/pallas_call | solution.py:228
  2.5 0.0 copy-start.2
  2.5 0.0 copy-start.1
  2.6 7.6 %all-to-all-start = ((bf16[8,24,16,128]{3,2,1,0:T(8,128)(2,1)}), bf16[8,24,16,128]{3,2,1,0:T(8,128)(2,1)S(1)}, u32[]{:S(2)}, u32[]{:S(2)}) async-start(bf16[8,24,16,128]{3,2,1,0:T(8,128)(2,1)} %get-tuple-element.24), calls=%async_computation | async-start | bytes 1572864 | tf_op jit(solution)/shard_map/all_to_all | solution.py:241
  10.2 11.1 %collective-permute-start = (bf16[24,16,128]{2,1,0:T(8,128)(2,1)S(1)}, bf16[24,16,128]{2,1,0:T(8,128)(2,1)S(1)}, u32[]{:S(2)}, u32[]{:S(2)}) collective-permute-start(bf16[24,16,128]{2,1,0:T(8,128)(2,1)S(1)} %copy-done.2), channel_id=1, source_target_pairs={{0,60},{4,0},{8,4},{12,8},{16,12},{20,16},{24,20},{28,24},{32,28},... | collective-permute-start | bytes 294920 | tf_op jit(solution)/shard_map/ppermute | solution.py:245
  21.3 1.6 %collective-permute-done.from_x = bf16[24,16,128]{2,1,0:T(8,128)(2,1)S(1)} collective-permute-done((bf16[24,16,128]{2,1,0:T(8,128)(2,1)S(1)}, bf16[24,16,128]{2,1,0:T(8,128)(2,1)S(1)}, u32[]{:S(2)}, u32[]{:S(2)}) %collective-permute-start) | collective-permute-done | bytes 98336 | tf_op jit(solution)/shard_map/ppermute | solution.py:245
  22.9 3.7 %collective-permute-start.1 = (bf16[6,16,128]{2,1,0:T(8,128)(2,1)S(1)}, bf16[6,16,128]{2,1,0:T(8,128)(2,1)S(1)}, u32[]{:S(2)}, u32[]{:S(2)}) collective-permute-start(bf16[6,16,128]{2,1,0:T(8,128)(2,1)S(1)} %shard_map.76), channel_id=1, source_target_pairs={{0,3},{1,0},{2,1},{3,2},{4,7},{5,4},{6,5},{7,6},{8,11},{9,8},{10,9... | collective-permute-start | bytes 73736 | tf_op jit(solution)/shard_map/ppermute | solution.py:246
  26.7 1.8 %collective-permute-done.1.from_y = bf16[6,16,128]{2,1,0:T(8,128)(2,1)S(1)} collective-permute-done((bf16[6,16,128]{2,1,0:T(8,128)(2,1)S(1)}, bf16[6,16,128]{2,1,0:T(8,128)(2,1)S(1)}, u32[]{:S(2)}, u32[]{:S(2)}) %collective-permute-start.1) | collective-permute-done | bytes 24608 | tf_op jit(solution)/shard_map/ppermute | solution.py:246
  28.4 1.0 %shard_map.77 = bf16[8,21,16,128]{3,2,1,0:T(8,128)(2,1)} custom-call(bf16[24,16,128]{2,1,0:T(8,128)(2,1)S(1)} %collective-permute-done.from_x, bf16[6,16,128]{2,1,0:T(8,128)(2,1)S(1)} %collective-permute-done.1.from_y), custom_call_target="tpu_custom_call" | custom-call | tf_op jit(solution)/shard_map/pallas_call | solution.py:216
  29.4 0.0 all-to-all-done.got
  29.4 7.7 %all-to-all-start.1 = ((bf16[8,21,16,128]{3,2,1,0:T(8,128)(2,1)}), bf16[8,21,16,128]{3,2,1,0:T(8,128)(2,1)S(1)}, u32[]{:S(2)}, u32[]{:S(2)}) async-start(bf16[8,21,16,128]{3,2,1,0:T(8,128)(2,1)} %shard_map.77), calls=%async_computation.1 | async-start | bytes 1376256 | tf_op jit(solution)/shard_map/all_to_all | solution.py:249
  37.1 5.2 %collective-permute-start.3 = (bf16[8,8,16,128]{3,2,1,0:T(8,128)(2,1)S(1)}, bf16[8,8,16,128]{3,2,1,0:T(8,128)(2,1)S(1)}, u32[]{:S(2)}, u32[]{:S(2)}) collective-permute-start(bf16[8,8,16,128]{3,2,1,0:T(8,128)(2,1)S(1)} %slice.11), channel_id=1, source_target_pairs={{0,60},{4,0},{8,4},{12,8},{16,12},{20,16},{24,20},{28,24},{32,28},... | collective-permute-start | bytes 786440 | tf_op jit(solution)/shard_map/ppermute | solution.py:250
  42.4 1.9 %collective-permute-start.2 = (bf16[8,4,16,128]{3,2,1,0:T(8,128)(2,1)S(1)}, bf16[8,4,16,128]{3,2,1,0:T(8,128)(2,1)S(1)}, u32[]{:S(2)}, u32[]{:S(2)}) collective-permute-start(bf16[8,4,16,128]{3,2,1,0:T(8,128)(2,1)S(1)} %pad_maximum_fusion), channel_id=1, source_target_pairs={{0,3},{1,0},{2,1},{3,2},{4,7},{5,4},{6,5},{7,6},{8,11},{9,8},{10,9... | collective-permute-start | bytes 393224 | tf_op jit(solution)/shard_map/ppermute | solution.py:251
  44.3 1.3 %dynamic-slice_bitcast_fusion = bf16[27,16,128]{1,2,0:T(8,128)(2,1)} fusion(bf16[27,128,128]{2,1,0:T(8,128)(2,1)S(1)} %copy-done, s32[]{:T(128)S(6)} %select_n.3), kind=kLoop, calls=%fused_computation | loop fusion | bytes 221188 | tf_op jit(solution)/shard_map/transpose | solution.py:253
  45.6 1.4 %copy.8 = bf16[27,16,128]{2,1,0:T(8,128)(2,1)S(1)} copy(bf16[27,16,128]{1,2,0:T(8,128)(2,1)} %dynamic-slice_bitcast_fusion) | data formatting | bytes 221184 | tf_op jit(solution)/shard_map/transpose | solution.py:253
  47.0 2.5 %collective-permute-done.2.beside = bf16[8,4,16,128]{3,2,1,0:T(8,128)(2,1)S(1)} collective-permute-done((bf16[8,4,16,128]{3,2,1,0:T(8,128)(2,1)S(1)}, bf16[8,4,16,128]{3,2,1,0:T(8,128)(2,1)S(1)}, u32[]{:S(2)}, u32[]{:S(2)}) %collective-permute-start.2) | collective-permute-done | bytes 131104 | tf_op jit(solution)/shard_map/ppermute | solution.py:251
  49.5 0.0 collective-permute-done.3.across
  49.5 1.2 %all-to-all-done.1.layer = bf16[8,21,16,128]{3,2,1,0:T(8,128)(2,1)S(1)} async-done(((bf16[8,21,16,128]{3,2,1,0:T(8,128)(2,1)}), bf16[8,21,16,128]{3,2,1,0:T(8,128)(2,1)S(1)}, u32[]{:S(2)}, u32[]{:S(2)}) %all-to-all-start.1) | async-done | bytes 688160 | tf_op jit(solution)/shard_map/all_to_all | solution.py:249
  50.7 3.2 %shard_map.78 = (bf16[448,128]{1,0:T(8,128)(2,1)S(1)}, f32[6,8,16,128]{3,2,1,0:T(8,128)S(1)}, bf16[10,16,128]{2,1,0:T(8,128)(2,1)S(1)}) custom-call(s32[1]{0:T(128)} %bitcast.place, bf16[8,24,16,128]{3,2,1,0:T(8,128)(2,1)S(1)} %all-to-all-done.got, bf16[8,21,16,128]{3,2,1,0:T(8,128)(2,1)S(1)} %all-to-all-done.1.layer, ...), custom_call_target="tpu_custom_call" | custom-call | tf_op jit(solution)/shard_map/pallas_call | solution.py:259
  53.9 6.8 %all_to_all.25.parts = bf16[8,56,128]{2,1,0:T(8,128)(2,1)S(1)} all-to-all(bf16[8,56,128]{2,1,0:T(8,128)(2,1)S(1)} %bitcast.11), channel_id=1, replica_groups={{4,5,6,7,0,1,2,3},{12,13,14,15,8,9,10,11},{20,21,22,23,16,17,18,19},{28..., dimensions={0} | all-to-all | bytes 229376 | tf_op jit(solution)/shard_map/all_to_all | solution.py:282
  60.8 0.7 shard_map.80
  61.4 12.3 %all-to-all-start.3 = ((bf16[8,56,128]{2,1,0:T(8,128)(2,1)}), bf16[8,56,128]{2,1,0:T(8,128)(2,1)S(1)}, u32[]{:S(2)}, u32[]{:S(2)}) async-start(bf16[8,56,128]{2,1,0:T(8,128)(2,1)} %shard_map.80), calls=%async_computation.3 | async-start | bytes 229376 | tf_op jit(solution)/shard_map/all_to_all | solution.py:285
  73.7 3.2 %collective-permute-start.4 = (bf16[10,16,128]{2,1,0:T(8,128)(2,1)S(1)}, bf16[10,16,128]{2,1,0:T(8,128)(2,1)S(1)}, u32[]{:S(2)}, u32[]{:S(2)}) collective-permute-start(bf16[10,16,128]{2,1,0:T(8,128)(2,1)S(1)} %get-tuple-element.28), channel_id=1, source_target_pairs={{0,1},{1,2},{2,3},{3,0},{4,5},{5,6},{6,7},{7,4},{8,9},{9,10},{10,1... | collective-permute-start | bytes 122888 | tf_op jit(solution)/shard_map/ppermute | solution.py:283
  76.9 1.1 %collective-permute-done.4.from_y = bf16[10,16,128]{2,1,0:T(8,128)(2,1)S(1)} collective-permute-done((bf16[10,16,128]{2,1,0:T(8,128)(2,1)S(1)}, bf16[10,16,128]{2,1,0:T(8,128)(2,1)S(1)}, u32[]{:S(2)}, u32[]{:S(2)}) %collective-permute-start.4) | collective-permute-done | bytes 40992 | tf_op jit(solution)/shard_map/ppermute | solution.py:283
  78.0 0.6 all-to-all-done.3.parts
  78.6 0.7 shard_map.81
  79.3 6.0 %all-to-all-start.4 = ((bf16[8,56,128]{2,1,0:T(8,128)(2,1)}), bf16[8,56,128]{2,1,0:T(8,128)(2,1)S(1)}, u32[]{:S(2)}, u32[]{:S(2)}) async-start(bf16[8,56,128]{2,1,0:T(8,128)(2,1)} %shard_map.81), calls=%async_computation.4 | async-start | bytes 229376 | tf_op jit(solution)/shard_map/all_to_all | solution.py:290
  85.3 2.0 %collective-permute-start.5 = (bf16[3,8,16,128]{3,2,1,0:T(8,128)(2,1)S(1)}, bf16[3,8,16,128]{3,2,1,0:T(8,128)(2,1)S(1)}, u32[]{:S(2)}, u32[]{:S(2)}) collective-permute-start(bf16[3,8,16,128]{3,2,1,0:T(8,128)(2,1)S(1)} %get-tuple-element.34), channel_id=1, source_target_pairs={{0,4},{4,8},{8,12},{12,16},{16,20},{20,24},{24,28},{28,32},{32,36}... | collective-permute-start | bytes 294920 | tf_op jit(solution)/shard_map/ppermute | solution.py:288
  87.2 1.7 %all-to-all-done.4.parts = bf16[8,56,128]{2,1,0:T(8,128)(2,1)S(1)} async-done(((bf16[8,56,128]{2,1,0:T(8,128)(2,1)}), bf16[8,56,128]{2,1,0:T(8,128)(2,1)S(1)}, u32[]{:S(2)}, u32[]{:S(2)}) %all-to-all-start.4) | async-done | bytes 114720 | tf_op jit(solution)/shard_map/all_to_all | solution.py:290
  88.9 0.7 shard_map.82
  89.6 2.8 %collective-permute-done.5.from_x = bf16[3,8,16,128]{3,2,1,0:T(8,128)(2,1)S(1)} collective-permute-done((bf16[3,8,16,128]{3,2,1,0:T(8,128)(2,1)S(1)}, bf16[3,8,16,128]{3,2,1,0:T(8,128)(2,1)S(1)}, u32[]{:S(2)}, u32[]{:S(2)}) %collective-permute-start.5) | collective-permute-done | bytes 98336 | tf_op jit(solution)/shard_map/ppermute | solution.py:288
  92.4 0.7 shard_map.83
  (9 shorter events, 0.1 us)
Async XLA Ops:
  2.5 7.7 %copy-start.2 = (bf16[24,16,128]{2,1,0:T(8,128)(2,1)S(1)}, bf16[24,16,128]{2,1,0:T(8,128)(2,1)}, u32[]{:S(2)}) copy-start(bf16[24,16,128]{2,1,0:T(8,128)(2,1)} %get-tuple-element.22) | copy-start | bytes 294916
  2.5 20.4 %copy-start.1 = (bf16[1,16,128]{2,1,0:T(8,128)(2,1)S(1)}, bf16[1,16,128]{2,1,0:T(8,128)(2,1)}, u32[]{:S(2)}) copy-start(bf16[1,16,128]{2,1,0:T(8,128)(2,1)} %get-tuple-element.23.own) | copy-start | bytes 12292
  2.6 26.8 %all-to-all-start = ((bf16[8,24,16,128]{3,2,1,0:T(8,128)(2,1)}), bf16[8,24,16,128]{3,2,1,0:T(8,128)(2,1)S(1)}, u32[]{:S(2)}, u32[]{:S(2)}) async-start(bf16[8,24,16,128]{3,2,1,0:T(8,128)(2,1)} %get-tuple-element.24), calls=%async_computation | async-start | bytes 1572864 | tf_op jit(solution)/shard_map/all_to_all | solution.py:241
  10.2 12.7 %collective-permute-start = (bf16[24,16,128]{2,1,0:T(8,128)(2,1)S(1)}, bf16[24,16,128]{2,1,0:T(8,128)(2,1)S(1)}, u32[]{:S(2)}, u32[]{:S(2)}) collective-permute-start(bf16[24,16,128]{2,1,0:T(8,128)(2,1)S(1)} %copy-done.2), channel_id=1, source_target_pairs={{0,60},{4,0},{8,4},{12,8},{16,12},{20,16},{24,20},{28,24},{32,28},... | collective-permute-start | bytes 294920 | tf_op jit(solution)/shard_map/ppermute | solution.py:245
  22.9 5.5 %collective-permute-start.1 = (bf16[6,16,128]{2,1,0:T(8,128)(2,1)S(1)}, bf16[6,16,128]{2,1,0:T(8,128)(2,1)S(1)}, u32[]{:S(2)}, u32[]{:S(2)}) collective-permute-start(bf16[6,16,128]{2,1,0:T(8,128)(2,1)S(1)} %shard_map.76), channel_id=1, source_target_pairs={{0,3},{1,0},{2,1},{3,2},{4,7},{5,4},{6,5},{7,6},{8,11},{9,8},{10,9... | collective-permute-start | bytes 73736 | tf_op jit(solution)/shard_map/ppermute | solution.py:246
  29.4 14.9 %copy-start = (bf16[27,128,128]{2,1,0:T(8,128)(2,1)S(1)}, bf16[27,128,128]{2,1,0:T(8,128)(2,1)}, u32[]{:S(2)}) copy-start(bf16[27,128,128]{2,1,0:T(8,128)(2,1)} %weight.1) | copy-start | bytes 2654212
  29.4 21.3 %all-to-all-start.1 = ((bf16[8,21,16,128]{3,2,1,0:T(8,128)(2,1)}), bf16[8,21,16,128]{3,2,1,0:T(8,128)(2,1)S(1)}, u32[]{:S(2)}, u32[]{:S(2)}) async-start(bf16[8,21,16,128]{3,2,1,0:T(8,128)(2,1)} %shard_map.77), calls=%async_computation.1 | async-start | bytes 1376256 | tf_op jit(solution)/shard_map/all_to_all | solution.py:249
  37.1 12.5 %collective-permute-start.3 = (bf16[8,8,16,128]{3,2,1,0:T(8,128)(2,1)S(1)}, bf16[8,8,16,128]{3,2,1,0:T(8,128)(2,1)S(1)}, u32[]{:S(2)}, u32[]{:S(2)}) collective-permute-start(bf16[8,8,16,128]{3,2,1,0:T(8,128)(2,1)S(1)} %slice.11), channel_id=1, source_target_pairs={{0,60},{4,0},{8,4},{12,8},{16,12},{20,16},{24,20},{28,24},{32,28},... | collective-permute-start | bytes 786440 | tf_op jit(solution)/shard_map/ppermute | solution.py:250
  42.4 7.2 %collective-permute-start.2 = (bf16[8,4,16,128]{3,2,1,0:T(8,128)(2,1)S(1)}, bf16[8,4,16,128]{3,2,1,0:T(8,128)(2,1)S(1)}, u32[]{:S(2)}, u32[]{:S(2)}) collective-permute-start(bf16[8,4,16,128]{3,2,1,0:T(8,128)(2,1)S(1)} %pad_maximum_fusion), channel_id=1, source_target_pairs={{0,3},{1,0},{2,1},{3,2},{4,7},{5,4},{6,5},{7,6},{8,11},{9,8},{10,9... | collective-permute-start | bytes 393224 | tf_op jit(solution)/shard_map/ppermute | solution.py:251
  61.4 17.2 %all-to-all-start.3 = ((bf16[8,56,128]{2,1,0:T(8,128)(2,1)}), bf16[8,56,128]{2,1,0:T(8,128)(2,1)S(1)}, u32[]{:S(2)}, u32[]{:S(2)}) async-start(bf16[8,56,128]{2,1,0:T(8,128)(2,1)} %shard_map.80), calls=%async_computation.3 | async-start | bytes 229376 | tf_op jit(solution)/shard_map/all_to_all | solution.py:285
  73.7 4.3 %collective-permute-start.4 = (bf16[10,16,128]{2,1,0:T(8,128)(2,1)S(1)}, bf16[10,16,128]{2,1,0:T(8,128)(2,1)S(1)}, u32[]{:S(2)}, u32[]{:S(2)}) collective-permute-start(bf16[10,16,128]{2,1,0:T(8,128)(2,1)S(1)} %get-tuple-element.28), channel_id=1, source_target_pairs={{0,1},{1,2},{2,3},{3,0},{4,5},{5,6},{6,7},{7,4},{8,9},{9,10},{10,1... | collective-permute-start | bytes 122888 | tf_op jit(solution)/shard_map/ppermute | solution.py:283
  79.3 9.6 %all-to-all-start.4 = ((bf16[8,56,128]{2,1,0:T(8,128)(2,1)}), bf16[8,56,128]{2,1,0:T(8,128)(2,1)S(1)}, u32[]{:S(2)}, u32[]{:S(2)}) async-start(bf16[8,56,128]{2,1,0:T(8,128)(2,1)} %shard_map.81), calls=%async_computation.4 | async-start | bytes 229376 | tf_op jit(solution)/shard_map/all_to_all | solution.py:290
  85.3 7.1 %collective-permute-start.5 = (bf16[3,8,16,128]{3,2,1,0:T(8,128)(2,1)S(1)}, bf16[3,8,16,128]{3,2,1,0:T(8,128)(2,1)S(1)}, u32[]{:S(2)}, u32[]{:S(2)}) collective-permute-start(bf16[3,8,16,128]{3,2,1,0:T(8,128)(2,1)S(1)} %get-tuple-element.34), channel_id=1, source_target_pairs={{0,4},{4,8},{8,12},{12,16},{16,20},{20,24},{24,28},{28,32},{32,36}... | collective-permute-start | bytes 294920 | tf_op jit(solution)/shard_map/ppermute | solution.py:288

commit v5 on v4

--- a/solution.py
+++ b/solution.py
@@ -56,9 +56,9 @@
 
 def pack_layer(from_x, from_y, out):
     for p in range(out.shape[0]):
-        out[p, 0:8] = from_x[0:8]
-        out[p, 8:15] = from_x[17:24]
-        out[p, 15:21] = from_y[...]
+        out[p, 0:6] = from_x[0:6]
+        out[p, 6:13] = from_x[17:24]
+        out[p, 13:19] = from_y[...]
 
 
 def add_edge(inner, from_y, keep, send):
@@ -117,13 +117,15 @@
 
     def feature(x, y):
         if y >= 8:
-            return row(beside, 2 * x + y - 8) if x < 2 else row(layer, 15 + 2 * (x - 2) + y - 8)
-        return row((got, got, layer, across)[x], 8 * (x % 2) * (x < 2) + y)
+            return row(beside, 2 * x + y - 8) if x < 2 else row(layer, 13 + 2 * (x - 2) + y - 8)
+        if x < 2:
+            return row(got, x * 8 + y)
+        return row(layer, y) if x == 2 and y < 6 else row(across, (x - 2) * 8 + y - 6)
 
     def cotangent(x, y):
         if y == 7:
-            return row(layer, 19 + x)
-        return row(layer, 8 + y) if x else row(got, 17 + y)
+            return row(layer, 17 + x)
+        return row(layer, 6 + y) if x else row(got, 17 + y)
 
     for x in range(4):
         for y in range(10):
@@ -244,10 +246,10 @@
     back = [(i, (i - 1) % count_y) for i in range(count_y)]
     from_x = lax.ppermute(x_send, gx_axes, down)
     from_y = lax.ppermute(call(pack_edge, rows_of(6), y_send, from_x), "gy", back)
-    parcel = call(pack_layer, rows_of(peers, 21), from_x, from_y)
+    parcel = call(pack_layer, rows_of(peers, 19), from_x, from_y)
     parcel, got = lax.optimization_barrier((parcel, got))
     layer = lax.all_to_all(parcel, "chan", 0, 0)
-    across = lax.ppermute(got[:, 8:16], gx_axes, down)
+    across = lax.ppermute(got[:, 6:16], gx_axes, down)
     beside = lax.ppermute(jnp.concatenate([got[:, 0:2], got[:, 8:10]], axis=1), "gy", back)
     own_weight = lax.dynamic_slice_in_dim(weight, chan * chans, chans, 2)
     own_weight = jnp.transpose(own_weight, (0, 2, 1)).reshape(TAPS * chans, width)
@@ -282,7 +284,7 @@
     part = lax.all_to_all(sums.reshape(near, piece, width), ("zl", "gy"), 0, 0, axis_index_groups=middle)
     from_y = lax.ppermute(edge, "gy", forth)
     part = call(functools.partial(sum_parts, 1.0), jax.ShapeDtypeStruct((far, piece, width), BF), part)
-    part = lax.all_to_all(part, "zh", 0, 0, axis_index_groups=[[(i + far // 2) % far for i in range(far)]])
+    part = lax.all_to_all(part, "zh", 0, 0, axis_index_groups=[[(i + far // 2 + 1) % far for i in range(far)]])
     keep, send = call(add_edge, (rows_of(3, extent_y, dtype=F32), rows_of(3, extent_y)), inner, from_y)
     part, send = lax.optimization_barrier((part, send))
     from_x = lax.ppermute(send, gx_axes, up)

time: 93.8 us -> 92 us (0.981)
  starting transfers between devices: 60.7 us -> 58.4 us
    all_to_all x1, starting transfers between devices: 12.3 us -> 10.5 us  [on_device(): lax.all_to_all(part, 'zh', 0, 0, axis_index_groups=[[(i + far // 2 + 1) %...]
    all_to_all x1, waiting for transfers between devices: 0.56 us -> 2.03 us  [on_device(): lax.all_to_all(part, 'zh', 0, 0, axis_index_groups=[[(i + far // 2 + 1) %...]
    all_to_all x1, waiting for transfers between devices: 1.15 us -> 0.07 us  [on_device(): layer = lax.all_to_all(parcel, 'chan', 0, 0)]
  transfers between devices with their start and end apart: 10 -> 10, of which waited for: 8 -> 9; matrix products, arithmetic and copies ran while one was open for 3% -> 3% of each run, Pallas kernels for 2% -> 2%
where the time goes in v5:
time: 92 us; the launch traced here: 91.3 us
  starting transfers between devices  58.4 us (63%)
  waiting for transfers between devices  13.8 us (15%)
  Pallas kernels  8.83 us (10%)
  blocking collectives  6.77 us (7%)
  local copies, waits for them, and re-layouts  2.76 us (3%)
    ppermute x1, starting transfers between devices, on_device(): from_x = lax.ppermute(x_send, gx_axes, down)  11.1 us
    all_to_all x1, starting transfers between devices, on_device(): lax.all_to_all(part, 'zh', 0, 0, axis_index_groups=[[(i + far // 2 + 1) %...  10.5 us
    all_to_all x1, starting transfers between devices, on_device(): got = lax.all_to_all(parcel, 'chan', 0, 0)  7.62 us
    all_to_all x1, starting transfers between devices, on_device(): layer = lax.all_to_all(parcel, 'chan', 0, 0)  7.52 us
    all_to_all x1, blocking collectives, on_device(): lax.all_to_all(sums.reshape(near, piece, width), ('zl', 'gy'), 0, 0, axis...  6.77 us
    all_to_all x1, starting transfers between devices, on_device(): part = lax.all_to_all(part, ('zl', 'gy'), 0, 0, axis_index_groups=middle)  5.41 us
    ppermute x1, starting transfers between devices, on_device(): across = lax.ppermute(got[:, 6:16], gx_axes, down)  5.37 us
    ppermute x1, starting transfers between devices, on_device(): lax.ppermute(call(pack_edge, rows_of(6), y_send, from_x), 'gy', back)  3.71 us
  transfers between devices with their start and end apart: 10, of which 9 were waited for; matrix products, arithmetic and copies ran while one was open for 3% of the time, Pallas kernels for 2%

profile of v5, /device:TPU:1, one launch (start us, length us, event | category | flops | bytes accessed | tf_op | source)
XLA Modules:
  0.0 91.3 jit_solution(6619604910218033777)
XLA Ops:
  0.6 1.9 %shard_map.75 = (bf16[8,24,16,128]{3,2,1,0:T(8,128)(2,1)}, bf16[24,16,128]{2,1,0:T(8,128)(2,1)}, bf16[1,16,128]{2,1,0:T(8,128)(2,1)}) custom-call(bf16[16,2,8,128]{3,2,1,0:T(8,128)(2,1)} %features_hbm.1, bf16[16,2,8,128]{3,2,1,0:T(8,128)(2,1)} %cotangent_hbm.1, f32[1,16]{1,0:T(1,128)} %bitcast.12), custom_call_target="tpu_custom_call" | custom-call | tf_op jit(solution)/shard_map/pallas_call | solution.py:230
  2.5 0.0 copy-start.2
  2.5 0.0 copy-start.1
  2.6 7.6 %all-to-all-start = ((bf16[8,24,16,128]{3,2,1,0:T(8,128)(2,1)}), bf16[8,24,16,128]{3,2,1,0:T(8,128)(2,1)S(1)}, u32[]{:S(2)}, u32[]{:S(2)}) async-start(bf16[8,24,16,128]{3,2,1,0:T(8,128)(2,1)} %get-tuple-element.24), calls=%async_computation | async-start | bytes 1572864 | tf_op jit(solution)/shard_map/all_to_all | solution.py:243
  10.2 11.1 %collective-permute-start = (bf16[24,16,128]{2,1,0:T(8,128)(2,1)S(1)}, bf16[24,16,128]{2,1,0:T(8,128)(2,1)S(1)}, u32[]{:S(2)}, u32[]{:S(2)}) collective-permute-start(bf16[24,16,128]{2,1,0:T(8,128)(2,1)S(1)} %copy-done.2), channel_id=1, source_target_pairs={{0,60},{4,0},{8,4},{12,8},{16,12},{20,16},{24,20},{28,24},{32,28},... | collective-permute-start | bytes 294920 | tf_op jit(solution)/shard_map/ppermute | solution.py:247
  21.3 1.6 %collective-permute-done.from_x = bf16[24,16,128]{2,1,0:T(8,128)(2,1)S(1)} collective-permute-done((bf16[24,16,128]{2,1,0:T(8,128)(2,1)S(1)}, bf16[24,16,128]{2,1,0:T(8,128)(2,1)S(1)}, u32[]{:S(2)}, u32[]{:S(2)}) %collective-permute-start) | collective-permute-done | bytes 98336 | tf_op jit(solution)/shard_map/ppermute | solution.py:247
  22.9 3.7 %collective-permute-start.1 = (bf16[6,16,128]{2,1,0:T(8,128)(2,1)S(1)}, bf16[6,16,128]{2,1,0:T(8,128)(2,1)S(1)}, u32[]{:S(2)}, u32[]{:S(2)}) collective-permute-start(bf16[6,16,128]{2,1,0:T(8,128)(2,1)S(1)} %shard_map.76), channel_id=1, source_target_pairs={{0,3},{1,0},{2,1},{3,2},{4,7},{5,4},{6,5},{7,6},{8,11},{9,8},{10,9... | collective-permute-start | bytes 73736 | tf_op jit(solution)/shard_map/ppermute | solution.py:248
  26.7 1.8 %collective-permute-done.1.from_y = bf16[6,16,128]{2,1,0:T(8,128)(2,1)S(1)} collective-permute-done((bf16[6,16,128]{2,1,0:T(8,128)(2,1)S(1)}, bf16[6,16,128]{2,1,0:T(8,128)(2,1)S(1)}, u32[]{:S(2)}, u32[]{:S(2)}) %collective-permute-start.1) | collective-permute-done | bytes 24608 | tf_op jit(solution)/shard_map/ppermute | solution.py:248
  28.4 0.9 %shard_map.77 = bf16[8,19,16,128]{3,2,1,0:T(8,128)(2,1)} custom-call(bf16[24,16,128]{2,1,0:T(8,128)(2,1)S(1)} %collective-permute-done.from_x, bf16[6,16,128]{2,1,0:T(8,128)(2,1)S(1)} %collective-permute-done.1.from_y), custom_call_target="tpu_custom_call" | custom-call | tf_op jit(solution)/shard_map/pallas_call | solution.py:218
  29.4 0.0 all-to-all-done.got
  29.4 7.5 %all-to-all-start.1 = ((bf16[8,19,16,128]{3,2,1,0:T(8,128)(2,1)}), bf16[8,19,16,128]{3,2,1,0:T(8,128)(2,1)S(1)}, u32[]{:S(2)}, u32[]{:S(2)}) async-start(bf16[8,19,16,128]{3,2,1,0:T(8,128)(2,1)} %shard_map.77), calls=%async_computation.1 | async-start | bytes 1245184 | tf_op jit(solution)/shard_map/all_to_all | solution.py:251
  36.9 5.4 %collective-permute-start.3 = (bf16[8,10,16,128]{3,2,1,0:T(8,128)(2,1)S(1)}, bf16[8,10,16,128]{3,2,1,0:T(8,128)(2,1)S(1)}, u32[]{:S(2)}, u32[]{:S(2)}) collective-permute-start(bf16[8,10,16,128]{3,2,1,0:T(8,128)(2,1)S(1)} %slice.11), channel_id=1, source_target_pairs={{0,60},{4,0},{8,4},{12,8},{16,12},{20,16},{24,20},{28,24},{32,28},... | collective-permute-start | bytes 983048 | tf_op jit(solution)/shard_map/ppermute | solution.py:252
  42.4 1.9 %collective-permute-start.2 = (bf16[8,4,16,128]{3,2,1,0:T(8,128)(2,1)S(1)}, bf16[8,4,16,128]{3,2,1,0:T(8,128)(2,1)S(1)}, u32[]{:S(2)}, u32[]{:S(2)}) collective-permute-start(bf16[8,4,16,128]{3,2,1,0:T(8,128)(2,1)S(1)} %pad_maximum_fusion), channel_id=1, source_target_pairs={{0,3},{1,0},{2,1},{3,2},{4,7},{5,4},{6,5},{7,6},{8,11},{9,8},{10,9... | collective-permute-start | bytes 393224 | tf_op jit(solution)/shard_map/ppermute | solution.py:253
  44.3 1.3 %dynamic-slice_bitcast_fusion = bf16[27,16,128]{1,2,0:T(8,128)(2,1)} fusion(bf16[27,128,128]{2,1,0:T(8,128)(2,1)S(1)} %copy-done, s32[]{:T(128)S(6)} %select_n.3), kind=kLoop, calls=%fused_computation | loop fusion | bytes 221188 | tf_op jit(solution)/shard_map/transpose | solution.py:255
  45.6 1.4 %copy.8 = bf16[27,16,128]{2,1,0:T(8,128)(2,1)S(1)} copy(bf16[27,16,128]{1,2,0:T(8,128)(2,1)} %dynamic-slice_bitcast_fusion) | data formatting | bytes 221184 | tf_op jit(solution)/shard_map/transpose | solution.py:255
  47.0 1.9 %collective-permute-done.2.beside = bf16[8,4,16,128]{3,2,1,0:T(8,128)(2,1)S(1)} collective-permute-done((bf16[8,4,16,128]{3,2,1,0:T(8,128)(2,1)S(1)}, bf16[8,4,16,128]{3,2,1,0:T(8,128)(2,1)S(1)}, u32[]{:S(2)}, u32[]{:S(2)}) %collective-permute-start.2) | collective-permute-done | bytes 131104 | tf_op jit(solution)/shard_map/ppermute | solution.py:253
  48.9 0.8 collective-permute-done.3.across
  49.8 0.1 all-to-all-done.1.layer
  49.8 3.2 %shard_map.78 = (bf16[448,128]{1,0:T(8,128)(2,1)S(1)}, f32[6,8,16,128]{3,2,1,0:T(8,128)S(1)}, bf16[10,16,128]{2,1,0:T(8,128)(2,1)S(1)}) custom-call(s32[1]{0:T(128)} %bitcast.place, bf16[8,24,16,128]{3,2,1,0:T(8,128)(2,1)S(1)} %all-to-all-done.got, bf16[8,19,16,128]{3,2,1,0:T(8,128)(2,1)S(1)} %all-to-all-done.1.layer, ...), custom_call_target="tpu_custom_call" | custom-call | tf_op jit(solution)/shard_map/pallas_call | solution.py:261
  53.1 6.8 %all_to_all.25.parts = bf16[8,56,128]{2,1,0:T(8,128)(2,1)S(1)} all-to-all(bf16[8,56,128]{2,1,0:T(8,128)(2,1)S(1)} %bitcast.11), channel_id=1, replica_groups={{4,5,6,7,0,1,2,3},{12,13,14,15,8,9,10,11},{20,21,22,23,16,17,18,19},{28..., dimensions={0} | all-to-all | bytes 229376 | tf_op jit(solution)/shard_map/all_to_all | solution.py:284
  59.8 0.7 shard_map.80
  60.5 10.5 %all-to-all-start.3 = ((bf16[8,56,128]{2,1,0:T(8,128)(2,1)}), bf16[8,56,128]{2,1,0:T(8,128)(2,1)S(1)}, u32[]{:S(2)}, u32[]{:S(2)}) async-start(bf16[8,56,128]{2,1,0:T(8,128)(2,1)} %shard_map.80), calls=%async_computation.3 | async-start | bytes 229376 | tf_op jit(solution)/shard_map/all_to_all | solution.py:287
  71.0 3.2 %collective-permute-start.4 = (bf16[10,16,128]{2,1,0:T(8,128)(2,1)S(1)}, bf16[10,16,128]{2,1,0:T(8,128)(2,1)S(1)}, u32[]{:S(2)}, u32[]{:S(2)}) collective-permute-start(bf16[10,16,128]{2,1,0:T(8,128)(2,1)S(1)} %get-tuple-element.28), channel_id=1, source_target_pairs={{0,1},{1,2},{2,3},{3,0},{4,5},{5,6},{6,7},{7,4},{8,9},{9,10},{10,1... | collective-permute-start | bytes 122888 | tf_op jit(solution)/shard_map/ppermute | solution.py:285
  74.3 1.1 %collective-permute-done.4.from_y = bf16[10,16,128]{2,1,0:T(8,128)(2,1)S(1)} collective-permute-done((bf16[10,16,128]{2,1,0:T(8,128)(2,1)S(1)}, bf16[10,16,128]{2,1,0:T(8,128)(2,1)S(1)}, u32[]{:S(2)}, u32[]{:S(2)}) %collective-permute-start.4) | collective-permute-done | bytes 40992 | tf_op jit(solution)/shard_map/ppermute | solution.py:285
  75.4 2.0 %all-to-all-done.3.parts = bf16[8,56,128]{2,1,0:T(8,128)(2,1)S(1)} async-done(((bf16[8,56,128]{2,1,0:T(8,128)(2,1)}), bf16[8,56,128]{2,1,0:T(8,128)(2,1)S(1)}, u32[]{:S(2)}, u32[]{:S(2)}) %all-to-all-start.3) | async-done | bytes 114720 | tf_op jit(solution)/shard_map/all_to_all | solution.py:287
  77.4 0.7 shard_map.81
  78.1 5.4 %all-to-all-start.4 = ((bf16[8,56,128]{2,1,0:T(8,128)(2,1)}), bf16[8,56,128]{2,1,0:T(8,128)(2,1)S(1)}, u32[]{:S(2)}, u32[]{:S(2)}) async-start(bf16[8,56,128]{2,1,0:T(8,128)(2,1)} %shard_map.81), calls=%async_computation.4 | async-start | bytes 229376 | tf_op jit(solution)/shard_map/all_to_all | solution.py:292
  83.5 2.0 %collective-permute-start.5 = (bf16[3,8,16,128]{3,2,1,0:T(8,128)(2,1)S(1)}, bf16[3,8,16,128]{3,2,1,0:T(8,128)(2,1)S(1)}, u32[]{:S(2)}, u32[]{:S(2)}) collective-permute-start(bf16[3,8,16,128]{3,2,1,0:T(8,128)(2,1)S(1)} %get-tuple-element.34), channel_id=1, source_target_pairs={{0,4},{4,8},{8,12},{12,16},{16,20},{20,24},{24,28},{28,32},{32,36}... | collective-permute-start | bytes 294920 | tf_op jit(solution)/shard_map/ppermute | solution.py:290
  85.5 1.7 %all-to-all-done.4.parts = bf16[8,56,128]{2,1,0:T(8,128)(2,1)S(1)} async-done(((bf16[8,56,128]{2,1,0:T(8,128)(2,1)}), bf16[8,56,128]{2,1,0:T(8,128)(2,1)S(1)}, u32[]{:S(2)}, u32[]{:S(2)}) %all-to-all-start.4) | async-done | bytes 114720 | tf_op jit(solution)/shard_map/all_to_all | solution.py:292
  87.1 0.7 shard_map.82
  87.8 2.8 %collective-permute-done.5.from_x = bf16[3,8,16,128]{3,2,1,0:T(8,128)(2,1)S(1)} collective-permute-done((bf16[3,8,16,128]{3,2,1,0:T(8,128)(2,1)S(1)}, bf16[3,8,16,128]{3,2,1,0:T(8,128)(2,1)S(1)}, u32[]{:S(2)}, u32[]{:S(2)}) %collective-permute-start.5) | collective-permute-done | bytes 98336 | tf_op jit(solution)/shard_map/ppermute | solution.py:290
  90.6 0.7 shard_map.83
  (9 shorter events, 0.1 us)
Async XLA Ops:
  2.5 7.7 %copy-start.2 = (bf16[24,16,128]{2,1,0:T(8,128)(2,1)S(1)}, bf16[24,16,128]{2,1,0:T(8,128)(2,1)}, u32[]{:S(2)}) copy-start(bf16[24,16,128]{2,1,0:T(8,128)(2,1)} %get-tuple-element.22) | copy-start | bytes 294916
  2.5 20.4 %copy-start.1 = (bf16[1,16,128]{2,1,0:T(8,128)(2,1)S(1)}, bf16[1,16,128]{2,1,0:T(8,128)(2,1)}, u32[]{:S(2)}) copy-start(bf16[1,16,128]{2,1,0:T(8,128)(2,1)} %get-tuple-element.23.own) | copy-start | bytes 12292
  2.6 26.8 %all-to-all-start = ((bf16[8,24,16,128]{3,2,1,0:T(8,128)(2,1)}), bf16[8,24,16,128]{3,2,1,0:T(8,128)(2,1)S(1)}, u32[]{:S(2)}, u32[]{:S(2)}) async-start(bf16[8,24,16,128]{3,2,1,0:T(8,128)(2,1)} %get-tuple-element.24), calls=%async_computation | async-start | bytes 1572864 | tf_op jit(solution)/shard_map/all_to_all | solution.py:243
  10.2 12.7 %collective-permute-start = (bf16[24,16,128]{2,1,0:T(8,128)(2,1)S(1)}, bf16[24,16,128]{2,1,0:T(8,128)(2,1)S(1)}, u32[]{:S(2)}, u32[]{:S(2)}) collective-permute-start(bf16[24,16,128]{2,1,0:T(8,128)(2,1)S(1)} %copy-done.2), channel_id=1, source_target_pairs={{0,60},{4,0},{8,4},{12,8},{16,12},{20,16},{24,20},{28,24},{32,28},... | collective-permute-start | bytes 294920 | tf_op jit(solution)/shard_map/ppermute | solution.py:247
  22.9 5.5 %collective-permute-start.1 = (bf16[6,16,128]{2,1,0:T(8,128)(2,1)S(1)}, bf16[6,16,128]{2,1,0:T(8,128)(2,1)S(1)}, u32[]{:S(2)}, u32[]{:S(2)}) collective-permute-start(bf16[6,16,128]{2,1,0:T(8,128)(2,1)S(1)} %shard_map.76), channel_id=1, source_target_pairs={{0,3},{1,0},{2,1},{3,2},{4,7},{5,4},{6,5},{7,6},{8,11},{9,8},{10,9... | collective-permute-start | bytes 73736 | tf_op jit(solution)/shard_map/ppermute | solution.py:248
  29.4 20.4 %all-to-all-start.1 = ((bf16[8,19,16,128]{3,2,1,0:T(8,128)(2,1)}), bf16[8,19,16,128]{3,2,1,0:T(8,128)(2,1)S(1)}, u32[]{:S(2)}, u32[]{:S(2)}) async-start(bf16[8,19,16,128]{3,2,1,0:T(8,128)(2,1)} %shard_map.77), calls=%async_computation.1 | async-start | bytes 1245184 | tf_op jit(solution)/shard_map/all_to_all | solution.py:251
  36.9 7.4 %copy-start = (bf16[27,128,128]{2,1,0:T(8,128)(2,1)S(1)}, bf16[27,128,128]{2,1,0:T(8,128)(2,1)}, u32[]{:S(2)}) copy-start(bf16[27,128,128]{2,1,0:T(8,128)(2,1)} %weight.1) | copy-start | bytes 2654212
  36.9 12.8 %collective-permute-start.3 = (bf16[8,10,16,128]{3,2,1,0:T(8,128)(2,1)S(1)}, bf16[8,10,16,128]{3,2,1,0:T(8,128)(2,1)S(1)}, u32[]{:S(2)}, u32[]{:S(2)}) collective-permute-start(bf16[8,10,16,128]{3,2,1,0:T(8,128)(2,1)S(1)} %slice.11), channel_id=1, source_target_pairs={{0,60},{4,0},{8,4},{12,8},{16,12},{20,16},{24,20},{28,24},{32,28},... | collective-permute-start | bytes 983048 | tf_op jit(solution)/shard_map/ppermute | solution.py:252
  42.4 6.6 %collective-permute-start.2 = (bf16[8,4,16,128]{3,2,1,0:T(8,128)(2,1)S(1)}, bf16[8,4,16,128]{3,2,1,0:T(8,128)(2,1)S(1)}, u32[]{:S(2)}, u32[]{:S(2)}) collective-permute-start(bf16[8,4,16,128]{3,2,1,0:T(8,128)(2,1)S(1)} %pad_maximum_fusion), channel_id=1, source_target_pairs={{0,3},{1,0},{2,1},{3,2},{4,7},{5,4},{6,5},{7,6},{8,11},{9,8},{10,9... | collective-permute-start | bytes 393224 | tf_op jit(solution)/shard_map/ppermute | solution.py:253
  60.5 16.9 %all-to-all-start.3 = ((bf16[8,56,128]{2,1,0:T(8,128)(2,1)}), bf16[8,56,128]{2,1,0:T(8,128)(2,1)S(1)}, u32[]{:S(2)}, u32[]{:S(2)}) async-start(bf16[8,56,128]{2,1,0:T(8,128)(2,1)} %shard_map.80), calls=%async_computation.3 | async-start | bytes 229376 | tf_op jit(solution)/shard_map/all_to_all | solution.py:287
  71.0 4.3 %collective-permute-start.4 = (bf16[10,16,128]{2,1,0:T(8,128)(2,1)S(1)}, bf16[10,16,128]{2,1,0:T(8,128)(2,1)S(1)}, u32[]{:S(2)}, u32[]{:S(2)}) collective-permute-start(bf16[10,16,128]{2,1,0:T(8,128)(2,1)S(1)} %get-tuple-element.28), channel_id=1, source_target_pairs={{0,1},{1,2},{2,3},{3,0},{4,5},{5,6},{6,7},{7,4},{8,9},{9,10},{10,1... | collective-permute-start | bytes 122888 | tf_op jit(solution)/shard_map/ppermute | solution.py:285
  78.1 9.1 %all-to-all-start.4 = ((bf16[8,56,128]{2,1,0:T(8,128)(2,1)}), bf16[8,56,128]{2,1,0:T(8,128)(2,1)S(1)}, u32[]{:S(2)}, u32[]{:S(2)}) async-start(bf16[8,56,128]{2,1,0:T(8,128)(2,1)} %shard_map.81), calls=%async_computation.4 | async-start | bytes 229376 | tf_op jit(solution)/shard_map/all_to_all | solution.py:292
  83.5 7.1 %collective-permute-start.5 = (bf16[3,8,16,128]{3,2,1,0:T(8,128)(2,1)S(1)}, bf16[3,8,16,128]{3,2,1,0:T(8,128)(2,1)S(1)}, u32[]{:S(2)}, u32[]{:S(2)}) collective-permute-start(bf16[3,8,16,128]{3,2,1,0:T(8,128)(2,1)S(1)} %get-tuple-element.34), channel_id=1, source_target_pairs={{0,4},{4,8},{8,12},{12,16},{16,20},{20,24},{24,28},{28,32},{32,36}... | collective-permute-start | bytes 294920 | tf_op jit(solution)/shard_map/ppermute | solution.py:290

commit v6 on v5

--- a/solution.py
+++ b/solution.py
@@ -27,10 +27,13 @@
     cells = 2 * 8
     for x in range(2):
         rows = jnp.swapaxes(features[:, x].astype(F32), 0, 1).astype(BF)
-        x_send[x * 8 : (x + 1) * 8] = rows
+        if x == 0:
+            x_send[0:6] = rows[0:6]
+        else:
+            x_send[6:8] = rows[0:2]
         for p in range(out.shape[0]):
             out[p, x * 8 : (x + 1) * 8] = rows
-    x_send[cells:] = jnp.swapaxes(cotangent[:, 0].astype(F32), 0, 1).astype(BF)
+    x_send[8:16] = jnp.swapaxes(cotangent[:, 0].astype(F32), 0, 1).astype(BF)
     rows = jnp.swapaxes(cotangent[:, 1].astype(F32), 0, 1).astype(BF)
     y_send[...] = rows[0:1]
     chans = bias.shape[1]
@@ -49,15 +52,15 @@
 
 def pack_edge(own, from_x, out):
     out[0:2] = from_x[0:2]
-    out[2:4] = from_x[8:10]
+    out[2:4] = from_x[6:8]
     out[4:5] = own[...]
-    out[5:6] = from_x[16:17]
+    out[5:6] = from_x[8:9]
 
 
 def pack_layer(from_x, from_y, out):
     for p in range(out.shape[0]):
         out[p, 0:6] = from_x[0:6]
-        out[p, 6:13] = from_x[17:24]
+        out[p, 6:13] = from_x[9:16]
         out[p, 13:19] = from_y[...]
 
 
@@ -229,7 +232,7 @@
     anywhere = pl.BlockSpec(memory_space=pl.ANY)
     parcel, x_send, y_send = pl.pallas_call(
         pack_block,
-        out_shape=(rows_of(peers, 24), rows_of(24), rows_of(1)),
+        out_shape=(rows_of(peers, 24), rows_of(16), rows_of(1)),
         in_specs=[anywhere] * 3,
         out_specs=(vmem,) * 3,
         scratch_shapes=[

time: 92 us -> 91.7 us (level)
  no operation moved by 1% of the time
where the time goes in v6:
time: 91.7 us; the launch traced here: 90.9 us
  starting transfers between devices  58.3 us (64%)
  waiting for transfers between devices  13.5 us (15%)
  Pallas kernels  8.81 us (10%)
  blocking collectives  6.78 us (7%)
  local copies, waits for them, and re-layouts  2.76 us (3%)
    ppermute x1, starting transfers between devices, on_device(): from_x = lax.ppermute(x_send, gx_axes, down)  11.1 us
    all_to_all x1, starting transfers between devices, on_device(): lax.all_to_all(part, 'zh', 0, 0, axis_index_groups=[[(i + far // 2 + 1) %...  10.5 us
    all_to_all x1, starting transfers between devices, on_device(): got = lax.all_to_all(parcel, 'chan', 0, 0)  7.62 us
    all_to_all x1, starting transfers between devices, on_device(): layer = lax.all_to_all(parcel, 'chan', 0, 0)  7.52 us
    all_to_all x1, blocking collectives, on_device(): lax.all_to_all(sums.reshape(near, piece, width), ('zl', 'gy'), 0, 0, axis...  6.78 us
    all_to_all x1, starting transfers between devices, on_device(): part = lax.all_to_all(part, ('zl', 'gy'), 0, 0, axis_index_groups=middle)  5.41 us
    ppermute x1, starting transfers between devices, on_device(): across = lax.ppermute(got[:, 6:16], gx_axes, down)  5.33 us
    ppermute x1, starting transfers between devices, on_device(): lax.ppermute(call(pack_edge, rows_of(6), y_send, from_x), 'gy', back)  3.71 us
  transfers between devices with their start and end apart: 10, of which 9 were waited for; matrix products, arithmetic and copies ran while one was open for 3% of the time, Pallas kernels for 2%

profile of v6, /device:TPU:1, one launch (start us, length us, event | category | flops | bytes accessed | tf_op | source)
XLA Modules:
  0.0 90.9 jit_solution(4288452395765395898)
XLA Ops:
  0.6 1.9 %shard_map.75 = (bf16[8,24,16,128]{3,2,1,0:T(8,128)(2,1)}, bf16[16,16,128]{2,1,0:T(8,128)(2,1)}, bf16[1,16,128]{2,1,0:T(8,128)(2,1)}) custom-call(bf16[16,2,8,128]{3,2,1,0:T(8,128)(2,1)} %features_hbm.1, bf16[16,2,8,128]{3,2,1,0:T(8,128)(2,1)} %cotangent_hbm.1, f32[1,16]{1,0:T(1,128)} %bitcast.12), custom_call_target="tpu_custom_call" | custom-call | tf_op jit(solution)/shard_map/pallas_call | solution.py:233
  2.5 0.0 copy-start.2
  2.5 0.0 copy-start.1
  2.5 7.6 %all-to-all-start = ((bf16[8,24,16,128]{3,2,1,0:T(8,128)(2,1)}), bf16[8,24,16,128]{3,2,1,0:T(8,128)(2,1)S(1)}, u32[]{:S(2)}, u32[]{:S(2)}) async-start(bf16[8,24,16,128]{3,2,1,0:T(8,128)(2,1)} %get-tuple-element.24), calls=%async_computation | async-start | bytes 1572864 | tf_op jit(solution)/shard_map/all_to_all | solution.py:246
  10.2 11.1 %collective-permute-start = (bf16[16,16,128]{2,1,0:T(8,128)(2,1)S(1)}, bf16[16,16,128]{2,1,0:T(8,128)(2,1)S(1)}, u32[]{:S(2)}, u32[]{:S(2)}) collective-permute-start(bf16[16,16,128]{2,1,0:T(8,128)(2,1)S(1)} %copy-done.2), channel_id=1, source_target_pairs={{0,60},{4,0},{8,4},{12,8},{16,12},{20,16},{24,20},{28,24},{32,28},... | collective-permute-start | bytes 196616 | tf_op jit(solution)/shard_map/ppermute | solution.py:250
  21.3 1.3 %collective-permute-done.from_x = bf16[16,16,128]{2,1,0:T(8,128)(2,1)S(1)} collective-permute-done((bf16[16,16,128]{2,1,0:T(8,128)(2,1)S(1)}, bf16[16,16,128]{2,1,0:T(8,128)(2,1)S(1)}, u32[]{:S(2)}, u32[]{:S(2)}) %collective-permute-start) | collective-permute-done | bytes 65568 | tf_op jit(solution)/shard_map/ppermute | solution.py:250
  22.6 3.7 %collective-permute-start.1 = (bf16[6,16,128]{2,1,0:T(8,128)(2,1)S(1)}, bf16[6,16,128]{2,1,0:T(8,128)(2,1)S(1)}, u32[]{:S(2)}, u32[]{:S(2)}) collective-permute-start(bf16[6,16,128]{2,1,0:T(8,128)(2,1)S(1)} %shard_map.76), channel_id=1, source_target_pairs={{0,3},{1,0},{2,1},{3,2},{4,7},{5,4},{6,5},{7,6},{8,11},{9,8},{10,9... | collective-permute-start | bytes 73736 | tf_op jit(solution)/shard_map/ppermute | solution.py:251
  26.3 1.8 %collective-permute-done.1.from_y = bf16[6,16,128]{2,1,0:T(8,128)(2,1)S(1)} collective-permute-done((bf16[6,16,128]{2,1,0:T(8,128)(2,1)S(1)}, bf16[6,16,128]{2,1,0:T(8,128)(2,1)S(1)}, u32[]{:S(2)}, u32[]{:S(2)}) %collective-permute-start.1) | collective-permute-done | bytes 24608 | tf_op jit(solution)/shard_map/ppermute | solution.py:251
  28.1 0.9 %shard_map.77 = bf16[8,19,16,128]{3,2,1,0:T(8,128)(2,1)} custom-call(bf16[16,16,128]{2,1,0:T(8,128)(2,1)S(1)} %collective-permute-done.from_x, bf16[6,16,128]{2,1,0:T(8,128)(2,1)S(1)} %collective-permute-done.1.from_y), custom_call_target="tpu_custom_call" | custom-call | tf_op jit(solution)/shard_map/pallas_call | solution.py:221
  29.1 0.0 all-to-all-done.got
  29.1 7.5 %all-to-all-start.1 = ((bf16[8,19,16,128]{3,2,1,0:T(8,128)(2,1)}), bf16[8,19,16,128]{3,2,1,0:T(8,128)(2,1)S(1)}, u32[]{:S(2)}, u32[]{:S(2)}) async-start(bf16[8,19,16,128]{3,2,1,0:T(8,128)(2,1)} %shard_map.77), calls=%async_computation.1 | async-start | bytes 1245184 | tf_op jit(solution)/shard_map/all_to_all | solution.py:254
  36.6 5.3 %collective-permute-start.3 = (bf16[8,10,16,128]{3,2,1,0:T(8,128)(2,1)S(1)}, bf16[8,10,16,128]{3,2,1,0:T(8,128)(2,1)S(1)}, u32[]{:S(2)}, u32[]{:S(2)}) collective-permute-start(bf16[8,10,16,128]{3,2,1,0:T(8,128)(2,1)S(1)} %slice.11), channel_id=1, source_target_pairs={{0,60},{4,0},{8,4},{12,8},{16,12},{20,16},{24,20},{28,24},{32,28},... | collective-permute-start | bytes 983048 | tf_op jit(solution)/shard_map/ppermute | solution.py:255
  42.0 1.9 %collective-permute-start.2 = (bf16[8,4,16,128]{3,2,1,0:T(8,128)(2,1)S(1)}, bf16[8,4,16,128]{3,2,1,0:T(8,128)(2,1)S(1)}, u32[]{:S(2)}, u32[]{:S(2)}) collective-permute-start(bf16[8,4,16,128]{3,2,1,0:T(8,128)(2,1)S(1)} %pad_maximum_fusion), channel_id=1, source_target_pairs={{0,3},{1,0},{2,1},{3,2},{4,7},{5,4},{6,5},{7,6},{8,11},{9,8},{10,9... | collective-permute-start | bytes 393224 | tf_op jit(solution)/shard_map/ppermute | solution.py:256
  43.9 1.3 %dynamic-slice_bitcast_fusion = bf16[27,16,128]{1,2,0:T(8,128)(2,1)} fusion(bf16[27,128,128]{2,1,0:T(8,128)(2,1)S(1)} %copy-done, s32[]{:T(128)S(6)} %select_n.3), kind=kLoop, calls=%fused_computation | loop fusion | bytes 221188 | tf_op jit(solution)/shard_map/transpose | solution.py:258
  45.2 1.4 %copy.8 = bf16[27,16,128]{2,1,0:T(8,128)(2,1)S(1)} copy(bf16[27,16,128]{1,2,0:T(8,128)(2,1)} %dynamic-slice_bitcast_fusion) | data formatting | bytes 221184 | tf_op jit(solution)/shard_map/transpose | solution.py:258
  46.6 1.9 %collective-permute-done.2.beside = bf16[8,4,16,128]{3,2,1,0:T(8,128)(2,1)S(1)} collective-permute-done((bf16[8,4,16,128]{3,2,1,0:T(8,128)(2,1)S(1)}, bf16[8,4,16,128]{3,2,1,0:T(8,128)(2,1)S(1)}, u32[]{:S(2)}, u32[]{:S(2)}) %collective-permute-start.2) | collective-permute-done | bytes 131104 | tf_op jit(solution)/shard_map/ppermute | solution.py:256
  48.6 0.8 collective-permute-done.3.across
  49.4 0.1 all-to-all-done.1.layer
  49.5 3.2 %shard_map.78 = (bf16[448,128]{1,0:T(8,128)(2,1)S(1)}, f32[6,8,16,128]{3,2,1,0:T(8,128)S(1)}, bf16[10,16,128]{2,1,0:T(8,128)(2,1)S(1)}) custom-call(s32[1]{0:T(128)} %bitcast.place, bf16[8,24,16,128]{3,2,1,0:T(8,128)(2,1)S(1)} %all-to-all-done.got, bf16[8,19,16,128]{3,2,1,0:T(8,128)(2,1)S(1)} %all-to-all-done.1.layer, ...), custom_call_target="tpu_custom_call" | custom-call | tf_op jit(solution)/shard_map/pallas_call | solution.py:264
  52.7 6.8 %all_to_all.25.parts = bf16[8,56,128]{2,1,0:T(8,128)(2,1)S(1)} all-to-all(bf16[8,56,128]{2,1,0:T(8,128)(2,1)S(1)} %bitcast.11), channel_id=1, replica_groups={{4,5,6,7,0,1,2,3},{12,13,14,15,8,9,10,11},{20,21,22,23,16,17,18,19},{28..., dimensions={0} | all-to-all | bytes 229376 | tf_op jit(solution)/shard_map/all_to_all | solution.py:287
  59.5 0.7 shard_map.80
  60.2 10.5 %all-to-all-start.3 = ((bf16[8,56,128]{2,1,0:T(8,128)(2,1)}), bf16[8,56,128]{2,1,0:T(8,128)(2,1)S(1)}, u32[]{:S(2)}, u32[]{:S(2)}) async-start(bf16[8,56,128]{2,1,0:T(8,128)(2,1)} %shard_map.80), calls=%async_computation.3 | async-start | bytes 229376 | tf_op jit(solution)/shard_map/all_to_all | solution.py:290
  70.7 3.2 %collective-permute-start.4 = (bf16[10,16,128]{2,1,0:T(8,128)(2,1)S(1)}, bf16[10,16,128]{2,1,0:T(8,128)(2,1)S(1)}, u32[]{:S(2)}, u32[]{:S(2)}) collective-permute-start(bf16[10,16,128]{2,1,0:T(8,128)(2,1)S(1)} %get-tuple-element.28), channel_id=1, source_target_pairs={{0,1},{1,2},{2,3},{3,0},{4,5},{5,6},{6,7},{7,4},{8,9},{9,10},{10,1... | collective-permute-start | bytes 122888 | tf_op jit(solution)/shard_map/ppermute | solution.py:288
  73.9 1.1 %collective-permute-done.4.from_y = bf16[10,16,128]{2,1,0:T(8,128)(2,1)S(1)} collective-permute-done((bf16[10,16,128]{2,1,0:T(8,128)(2,1)S(1)}, bf16[10,16,128]{2,1,0:T(8,128)(2,1)S(1)}, u32[]{:S(2)}, u32[]{:S(2)}) %collective-permute-start.4) | collective-permute-done | bytes 40992 | tf_op jit(solution)/shard_map/ppermute | solution.py:288
  75.0 2.0 %all-to-all-done.3.parts = bf16[8,56,128]{2,1,0:T(8,128)(2,1)S(1)} async-done(((bf16[8,56,128]{2,1,0:T(8,128)(2,1)}), bf16[8,56,128]{2,1,0:T(8,128)(2,1)S(1)}, u32[]{:S(2)}, u32[]{:S(2)}) %all-to-all-start.3) | async-done | bytes 114720 | tf_op jit(solution)/shard_map/all_to_all | solution.py:290
  77.1 0.7 shard_map.81
  77.7 5.4 %all-to-all-start.4 = ((bf16[8,56,128]{2,1,0:T(8,128)(2,1)}), bf16[8,56,128]{2,1,0:T(8,128)(2,1)S(1)}, u32[]{:S(2)}, u32[]{:S(2)}) async-start(bf16[8,56,128]{2,1,0:T(8,128)(2,1)} %shard_map.81), calls=%async_computation.4 | async-start | bytes 229376 | tf_op jit(solution)/shard_map/all_to_all | solution.py:295
  83.1 2.0 %collective-permute-start.5 = (bf16[3,8,16,128]{3,2,1,0:T(8,128)(2,1)S(1)}, bf16[3,8,16,128]{3,2,1,0:T(8,128)(2,1)S(1)}, u32[]{:S(2)}, u32[]{:S(2)}) collective-permute-start(bf16[3,8,16,128]{3,2,1,0:T(8,128)(2,1)S(1)} %get-tuple-element.34), channel_id=1, source_target_pairs={{0,4},{4,8},{8,12},{12,16},{16,20},{20,24},{24,28},{28,32},{32,36}... | collective-permute-start | bytes 294920 | tf_op jit(solution)/shard_map/ppermute | solution.py:293
  85.1 1.7 %all-to-all-done.4.parts = bf16[8,56,128]{2,1,0:T(8,128)(2,1)S(1)} async-done(((bf16[8,56,128]{2,1,0:T(8,128)(2,1)}), bf16[8,56,128]{2,1,0:T(8,128)(2,1)S(1)}, u32[]{:S(2)}, u32[]{:S(2)}) %all-to-all-start.4) | async-done | bytes 114720 | tf_op jit(solution)/shard_map/all_to_all | solution.py:295
  86.8 0.7 shard_map.82
  87.5 2.8 %collective-permute-done.5.from_x = bf16[3,8,16,128]{3,2,1,0:T(8,128)(2,1)S(1)} collective-permute-done((bf16[3,8,16,128]{3,2,1,0:T(8,128)(2,1)S(1)}, bf16[3,8,16,128]{3,2,1,0:T(8,128)(2,1)S(1)}, u32[]{:S(2)}, u32[]{:S(2)}) %collective-permute-start.5) | collective-permute-done | bytes 98336 | tf_op jit(solution)/shard_map/ppermute | solution.py:293
  90.2 0.7 shard_map.83
  (9 shorter events, 0.1 us)
Async XLA Ops:
  2.5 7.7 %copy-start.2 = (bf16[16,16,128]{2,1,0:T(8,128)(2,1)S(1)}, bf16[16,16,128]{2,1,0:T(8,128)(2,1)}, u32[]{:S(2)}) copy-start(bf16[16,16,128]{2,1,0:T(8,128)(2,1)} %get-tuple-element.22) | copy-start | bytes 196612
  2.5 20.1 %copy-start.1 = (bf16[1,16,128]{2,1,0:T(8,128)(2,1)S(1)}, bf16[1,16,128]{2,1,0:T(8,128)(2,1)}, u32[]{:S(2)}) copy-start(bf16[1,16,128]{2,1,0:T(8,128)(2,1)} %get-tuple-element.23.own) | copy-start | bytes 12292
  2.5 26.5 %all-to-all-start = ((bf16[8,24,16,128]{3,2,1,0:T(8,128)(2,1)}), bf16[8,24,16,128]{3,2,1,0:T(8,128)(2,1)S(1)}, u32[]{:S(2)}, u32[]{:S(2)}) async-start(bf16[8,24,16,128]{3,2,1,0:T(8,128)(2,1)} %get-tuple-element.24), calls=%async_computation | async-start | bytes 1572864 | tf_op jit(solution)/shard_map/all_to_all | solution.py:246
  10.2 12.4 %collective-permute-start = (bf16[16,16,128]{2,1,0:T(8,128)(2,1)S(1)}, bf16[16,16,128]{2,1,0:T(8,128)(2,1)S(1)}, u32[]{:S(2)}, u32[]{:S(2)}) collective-permute-start(bf16[16,16,128]{2,1,0:T(8,128)(2,1)S(1)} %copy-done.2), channel_id=1, source_target_pairs={{0,60},{4,0},{8,4},{12,8},{16,12},{20,16},{24,20},{28,24},{32,28},... | collective-permute-start | bytes 196616 | tf_op jit(solution)/shard_map/ppermute | solution.py:250
  22.6 5.5 %collective-permute-start.1 = (bf16[6,16,128]{2,1,0:T(8,128)(2,1)S(1)}, bf16[6,16,128]{2,1,0:T(8,128)(2,1)S(1)}, u32[]{:S(2)}, u32[]{:S(2)}) collective-permute-start(bf16[6,16,128]{2,1,0:T(8,128)(2,1)S(1)} %shard_map.76), channel_id=1, source_target_pairs={{0,3},{1,0},{2,1},{3,2},{4,7},{5,4},{6,5},{7,6},{8,11},{9,8},{10,9... | collective-permute-start | bytes 73736 | tf_op jit(solution)/shard_map/ppermute | solution.py:251
  29.1 20.4 %all-to-all-start.1 = ((bf16[8,19,16,128]{3,2,1,0:T(8,128)(2,1)}), bf16[8,19,16,128]{3,2,1,0:T(8,128)(2,1)S(1)}, u32[]{:S(2)}, u32[]{:S(2)}) async-start(bf16[8,19,16,128]{3,2,1,0:T(8,128)(2,1)} %shard_map.77), calls=%async_computation.1 | async-start | bytes 1245184 | tf_op jit(solution)/shard_map/all_to_all | solution.py:254
  36.6 7.4 %copy-start = (bf16[27,128,128]{2,1,0:T(8,128)(2,1)S(1)}, bf16[27,128,128]{2,1,0:T(8,128)(2,1)}, u32[]{:S(2)}) copy-start(bf16[27,128,128]{2,1,0:T(8,128)(2,1)} %weight.1) | copy-start | bytes 2654212
  36.6 12.8 %collective-permute-start.3 = (bf16[8,10,16,128]{3,2,1,0:T(8,128)(2,1)S(1)}, bf16[8,10,16,128]{3,2,1,0:T(8,128)(2,1)S(1)}, u32[]{:S(2)}, u32[]{:S(2)}) collective-permute-start(bf16[8,10,16,128]{3,2,1,0:T(8,128)(2,1)S(1)} %slice.11), channel_id=1, source_target_pairs={{0,60},{4,0},{8,4},{12,8},{16,12},{20,16},{24,20},{28,24},{32,28},... | collective-permute-start | bytes 983048 | tf_op jit(solution)/shard_map/ppermute | solution.py:255
  42.0 6.6 %collective-permute-start.2 = (bf16[8,4,16,128]{3,2,1,0:T(8,128)(2,1)S(1)}, bf16[8,4,16,128]{3,2,1,0:T(8,128)(2,1)S(1)}, u32[]{:S(2)}, u32[]{:S(2)}) collective-permute-start(bf16[8,4,16,128]{3,2,1,0:T(8,128)(2,1)S(1)} %pad_maximum_fusion), channel_id=1, source_target_pairs={{0,3},{1,0},{2,1},{3,2},{4,7},{5,4},{6,5},{7,6},{8,11},{9,8},{10,9... | collective-permute-start | bytes 393224 | tf_op jit(solution)/shard_map/ppermute | solution.py:256
  60.2 16.9 %all-to-all-start.3 = ((bf16[8,56,128]{2,1,0:T(8,128)(2,1)}), bf16[8,56,128]{2,1,0:T(8,128)(2,1)S(1)}, u32[]{:S(2)}, u32[]{:S(2)}) async-start(bf16[8,56,128]{2,1,0:T(8,128)(2,1)} %shard_map.80), calls=%async_computation.3 | async-start | bytes 229376 | tf_op jit(solution)/shard_map/all_to_all | solution.py:290
  70.7 4.3 %collective-permute-start.4 = (bf16[10,16,128]{2,1,0:T(8,128)(2,1)S(1)}, bf16[10,16,128]{2,1,0:T(8,128)(2,1)S(1)}, u32[]{:S(2)}, u32[]{:S(2)}) collective-permute-start(bf16[10,16,128]{2,1,0:T(8,128)(2,1)S(1)} %get-tuple-element.28), channel_id=1, source_target_pairs={{0,1},{1,2},{2,3},{3,0},{4,5},{5,6},{6,7},{7,4},{8,9},{9,10},{10,1... | collective-permute-start | bytes 122888 | tf_op jit(solution)/shard_map/ppermute | solution.py:288
  77.7 9.1 %all-to-all-start.4 = ((bf16[8,56,128]{2,1,0:T(8,128)(2,1)}), bf16[8,56,128]{2,1,0:T(8,128)(2,1)S(1)}, u32[]{:S(2)}, u32[]{:S(2)}) async-start(bf16[8,56,128]{2,1,0:T(8,128)(2,1)} %shard_map.81), calls=%async_computation.4 | async-start | bytes 229376 | tf_op jit(solution)/shard_map/all_to_all | solution.py:295
  83.1 7.1 %collective-permute-start.5 = (bf16[3,8,16,128]{3,2,1,0:T(8,128)(2,1)S(1)}, bf16[3,8,16,128]{3,2,1,0:T(8,128)(2,1)S(1)}, u32[]{:S(2)}, u32[]{:S(2)}) collective-permute-start(bf16[3,8,16,128]{3,2,1,0:T(8,128)(2,1)S(1)} %get-tuple-element.34), channel_id=1, source_target_pairs={{0,4},{4,8},{8,12},{12,16},{16,20},{20,24},{24,28},{28,32},{32,36}... | collective-permute-start | bytes 294920 | tf_op jit(solution)/shard_map/ppermute | solution.py:293

commit v7 on v6

--- a/solution.py
+++ b/solution.py
@@ -28,12 +28,12 @@
     for x in range(2):
         rows = jnp.swapaxes(features[:, x].astype(F32), 0, 1).astype(BF)
         if x == 0:
-            x_send[0:6] = rows[0:6]
+            x_send[0:7] = rows[0:7]
         else:
-            x_send[6:8] = rows[0:2]
+            x_send[7:9] = rows[0:2]
         for p in range(out.shape[0]):
             out[p, x * 8 : (x + 1) * 8] = rows
-    x_send[8:16] = jnp.swapaxes(cotangent[:, 0].astype(F32), 0, 1).astype(BF)
+    x_send[9:17] = jnp.swapaxes(cotangent[:, 0].astype(F32), 0, 1).astype(BF)
     rows = jnp.swapaxes(cotangent[:, 1].astype(F32), 0, 1).astype(BF)
     y_send[...] = rows[0:1]
     chans = bias.shape[1]
@@ -52,16 +52,16 @@
 
 def pack_edge(own, from_x, out):
     out[0:2] = from_x[0:2]
-    out[2:4] = from_x[6:8]
+    out[2:4] = from_x[7:9]
     out[4:5] = own[...]
-    out[5:6] = from_x[8:9]
+    out[5:6] = from_x[9:10]
 
 
 def pack_layer(from_x, from_y, out):
     for p in range(out.shape[0]):
-        out[p, 0:6] = from_x[0:6]
-        out[p, 6:13] = from_x[9:16]
-        out[p, 13:19] = from_y[...]
+        out[p, 0:7] = from_x[0:7]
+        out[p, 7:14] = from_x[10:17]
+        out[p, 14:20] = from_y[...]
 
 
 def add_edge(inner, from_y, keep, send):
@@ -120,15 +120,15 @@
 
     def feature(x, y):
         if y >= 8:
-            return row(beside, 2 * x + y - 8) if x < 2 else row(layer, 13 + 2 * (x - 2) + y - 8)
+            return row(beside, 2 * x + y - 8) if x < 2 else row(layer, 14 + 2 * (x - 2) + y - 8)
         if x < 2:
             return row(got, x * 8 + y)
-        return row(layer, y) if x == 2 and y < 6 else row(across, (x - 2) * 8 + y - 6)
+        return row(layer, y) if x == 2 and y < 7 else row(across, (x - 2) * 8 + y - 7)
 
     def cotangent(x, y):
         if y == 7:
-            return row(layer, 17 + x)
-        return row(layer, 6 + y) if x else row(got, 17 + y)
+            return row(layer, 18 + x)
+        return row(layer, 7 + y) if x else row(got, 17 + y)
 
     for x in range(4):
         for y in range(10):
@@ -232,7 +232,7 @@
     anywhere = pl.BlockSpec(memory_space=pl.ANY)
     parcel, x_send, y_send = pl.pallas_call(
         pack_block,
-        out_shape=(rows_of(peers, 24), rows_of(16), rows_of(1)),
+        out_shape=(rows_of(peers, 24), rows_of(17), rows_of(1)),
         in_specs=[anywhere] * 3,
         out_specs=(vmem,) * 3,
         scratch_shapes=[
@@ -249,10 +249,10 @@
     back = [(i, (i - 1) % count_y) for i in range(count_y)]
     from_x = lax.ppermute(x_send, gx_axes, down)
     from_y = lax.ppermute(call(pack_edge, rows_of(6), y_send, from_x), "gy", back)
-    parcel = call(pack_layer, rows_of(peers, 19), from_x, from_y)
+    parcel = call(pack_layer, rows_of(peers, 20), from_x, from_y)
     parcel, got = lax.optimization_barrier((parcel, got))
     layer = lax.all_to_all(parcel, "chan", 0, 0)
-    across = lax.ppermute(got[:, 6:16], gx_axes, down)
+    across = lax.ppermute(got[:, 7:16], gx_axes, down)
     beside = lax.ppermute(jnp.concatenate([got[:, 0:2], got[:, 8:10]], axis=1), "gy", back)
     own_weight = lax.dynamic_slice_in_dim(weight, chan * chans, chans, 2)
     own_weight = jnp.transpose(own_weight, (0, 2, 1)).reshape(TAPS * chans, width)

time: 91.7 us -> 92.1 us (level)
    all_to_all x1, waiting for transfers between devices: 0.12 us -> 1.15 us  [on_device(): layer = lax.all_to_all(parcel, 'chan', 0, 0)]
  transfers between devices with their start and end apart: 10 -> 10, of which waited for: 9 -> 8; matrix products, arithmetic and copies ran while one was open for 3% -> 3% of each run, Pallas kernels for 2% -> 2%
where the time goes in v7:
time: 92.1 us; the launch traced here: 91.4 us
  starting transfers between devices  58.3 us (63%)
  waiting for transfers between devices  13.9 us (15%)
  Pallas kernels  8.83 us (10%)
  blocking collectives  6.82 us (7%)
  local copies, waits for them, and re-layouts  2.76 us (3%)
    ppermute x1, starting transfers between devices, on_device(): from_x = lax.ppermute(x_send, gx_axes, down)  11.1 us
    all_to_all x1, starting transfers between devices, on_device(): lax.all_to_all(part, 'zh', 0, 0, axis_index_groups=[[(i + far // 2 + 1) %...  10.4 us
    all_to_all x1, starting transfers between devices, on_device(): got = lax.all_to_all(parcel, 'chan', 0, 0)  7.62 us
    all_to_all x1, starting transfers between devices, on_device(): layer = lax.all_to_all(parcel, 'chan', 0, 0)  7.52 us
    all_to_all x1, blocking collectives, on_device(): lax.all_to_all(sums.reshape(near, piece, width), ('zl', 'gy'), 0, 0, axis...  6.82 us
    all_to_all x1, starting transfers between devices, on_device(): part = lax.all_to_all(part, ('zl', 'gy'), 0, 0, axis_index_groups=middle)  5.41 us
    ppermute x1, starting transfers between devices, on_device(): across = lax.ppermute(got[:, 7:16], gx_axes, down)  5.34 us
    pallas_call x7, Pallas kernels, call(): pl.pallas_call(body, out_shape=out_shape, in_specs=specs or [vmem] * len(...  3.71 us
  transfers between devices with their start and end apart: 10, of which 8 were waited for; matrix products, arithmetic and copies ran while one was open for 3% of the time, Pallas kernels for 2%

profile of v7, /device:TPU:1, one launch (start us, length us, event | category | flops | bytes accessed | tf_op | source)
XLA Modules:
  0.0 91.4 jit_solution(2721456368355556215)
XLA Ops:
  0.6 1.9 %shard_map.75 = (bf16[8,24,16,128]{3,2,1,0:T(8,128)(2,1)}, bf16[17,16,128]{2,1,0:T(8,128)(2,1)}, bf16[1,16,128]{2,1,0:T(8,128)(2,1)}) custom-call(bf16[16,2,8,128]{3,2,1,0:T(8,128)(2,1)} %features_hbm.1, bf16[16,2,8,128]{3,2,1,0:T(8,128)(2,1)} %cotangent_hbm.1, f32[1,16]{1,0:T(1,128)} %bitcast.12), custom_call_target="tpu_custom_call" | custom-call | tf_op jit(solution)/shard_map/pallas_call | solution.py:233
  2.5 0.0 copy-start.2
  2.5 0.0 copy-start.1
  2.5 7.6 %all-to-all-start = ((bf16[8,24,16,128]{3,2,1,0:T(8,128)(2,1)}), bf16[8,24,16,128]{3,2,1,0:T(8,128)(2,1)S(1)}, u32[]{:S(2)}, u32[]{:S(2)}) async-start(bf16[8,24,16,128]{3,2,1,0:T(8,128)(2,1)} %get-tuple-element.24), calls=%async_computation | async-start | bytes 1572864 | tf_op jit(solution)/shard_map/all_to_all | solution.py:246
  10.2 11.1 %collective-permute-start = (bf16[17,16,128]{2,1,0:T(8,128)(2,1)S(1)}, bf16[17,16,128]{2,1,0:T(8,128)(2,1)S(1)}, u32[]{:S(2)}, u32[]{:S(2)}) collective-permute-start(bf16[17,16,128]{2,1,0:T(8,128)(2,1)S(1)} %copy-done.2), channel_id=1, source_target_pairs={{0,60},{4,0},{8,4},{12,8},{16,12},{20,16},{24,20},{28,24},{32,28},... | collective-permute-start | bytes 208904 | tf_op jit(solution)/shard_map/ppermute | solution.py:250
  21.3 1.3 %collective-permute-done.from_x = bf16[17,16,128]{2,1,0:T(8,128)(2,1)S(1)} collective-permute-done((bf16[17,16,128]{2,1,0:T(8,128)(2,1)S(1)}, bf16[17,16,128]{2,1,0:T(8,128)(2,1)S(1)}, u32[]{:S(2)}, u32[]{:S(2)}) %collective-permute-start) | collective-permute-done | bytes 69664 | tf_op jit(solution)/shard_map/ppermute | solution.py:250
  22.7 3.7 %collective-permute-start.1 = (bf16[6,16,128]{2,1,0:T(8,128)(2,1)S(1)}, bf16[6,16,128]{2,1,0:T(8,128)(2,1)S(1)}, u32[]{:S(2)}, u32[]{:S(2)}) collective-permute-start(bf16[6,16,128]{2,1,0:T(8,128)(2,1)S(1)} %shard_map.76), channel_id=1, source_target_pairs={{0,3},{1,0},{2,1},{3,2},{4,7},{5,4},{6,5},{7,6},{8,11},{9,8},{10,9... | collective-permute-start | bytes 73736 | tf_op jit(solution)/shard_map/ppermute | solution.py:251
  26.4 1.8 %collective-permute-done.1.from_y = bf16[6,16,128]{2,1,0:T(8,128)(2,1)S(1)} collective-permute-done((bf16[6,16,128]{2,1,0:T(8,128)(2,1)S(1)}, bf16[6,16,128]{2,1,0:T(8,128)(2,1)S(1)}, u32[]{:S(2)}, u32[]{:S(2)}) %collective-permute-start.1) | collective-permute-done | bytes 24608 | tf_op jit(solution)/shard_map/ppermute | solution.py:251
  28.2 0.9 %shard_map.77 = bf16[8,20,16,128]{3,2,1,0:T(8,128)(2,1)} custom-call(bf16[17,16,128]{2,1,0:T(8,128)(2,1)S(1)} %collective-permute-done.from_x, bf16[6,16,128]{2,1,0:T(8,128)(2,1)S(1)} %collective-permute-done.1.from_y), custom_call_target="tpu_custom_call" | custom-call | tf_op jit(solution)/shard_map/pallas_call | solution.py:221
  29.1 0.0 all-to-all-done.got
  29.1 7.5 %all-to-all-start.1 = ((bf16[8,20,16,128]{3,2,1,0:T(8,128)(2,1)}), bf16[8,20,16,128]{3,2,1,0:T(8,128)(2,1)S(1)}, u32[]{:S(2)}, u32[]{:S(2)}) async-start(bf16[8,20,16,128]{3,2,1,0:T(8,128)(2,1)} %shard_map.77), calls=%async_computation.1 | async-start | bytes 1310720 | tf_op jit(solution)/shard_map/all_to_all | solution.py:254
  36.7 5.3 %collective-permute-start.3 = (bf16[8,9,16,128]{3,2,1,0:T(8,128)(2,1)S(1)}, bf16[8,9,16,128]{3,2,1,0:T(8,128)(2,1)S(1)}, u32[]{:S(2)}, u32[]{:S(2)}) collective-permute-start(bf16[8,9,16,128]{3,2,1,0:T(8,128)(2,1)S(1)} %slice.11), channel_id=1, source_target_pairs={{0,60},{4,0},{8,4},{12,8},{16,12},{20,16},{24,20},{28,24},{32,28},... | collective-permute-start | bytes 884744 | tf_op jit(solution)/shard_map/ppermute | solution.py:255
  42.1 1.9 %collective-permute-start.2 = (bf16[8,4,16,128]{3,2,1,0:T(8,128)(2,1)S(1)}, bf16[8,4,16,128]{3,2,1,0:T(8,128)(2,1)S(1)}, u32[]{:S(2)}, u32[]{:S(2)}) collective-permute-start(bf16[8,4,16,128]{3,2,1,0:T(8,128)(2,1)S(1)} %pad_maximum_fusion), channel_id=1, source_target_pairs={{0,3},{1,0},{2,1},{3,2},{4,7},{5,4},{6,5},{7,6},{8,11},{9,8},{10,9... | collective-permute-start | bytes 393224 | tf_op jit(solution)/shard_map/ppermute | solution.py:256
  44.0 1.3 %dynamic-slice_bitcast_fusion = bf16[27,16,128]{1,2,0:T(8,128)(2,1)} fusion(bf16[27,128,128]{2,1,0:T(8,128)(2,1)S(1)} %copy-done, s32[]{:T(128)S(6)} %select_n.3), kind=kLoop, calls=%fused_computation | loop fusion | bytes 221188 | tf_op jit(solution)/shard_map/transpose | solution.py:258
  45.3 1.4 %copy.8 = bf16[27,16,128]{2,1,0:T(8,128)(2,1)S(1)} copy(bf16[27,16,128]{1,2,0:T(8,128)(2,1)} %dynamic-slice_bitcast_fusion) | data formatting | bytes 221184 | tf_op jit(solution)/shard_map/transpose | solution.py:258
  46.7 2.0 %collective-permute-done.2.beside = bf16[8,4,16,128]{3,2,1,0:T(8,128)(2,1)S(1)} collective-permute-done((bf16[8,4,16,128]{3,2,1,0:T(8,128)(2,1)S(1)}, bf16[8,4,16,128]{3,2,1,0:T(8,128)(2,1)S(1)}, u32[]{:S(2)}, u32[]{:S(2)}) %collective-permute-start.2) | collective-permute-done | bytes 131104 | tf_op jit(solution)/shard_map/ppermute | solution.py:256
  48.8 0.0 collective-permute-done.3.across
  48.8 1.2 %all-to-all-done.1.layer = bf16[8,20,16,128]{3,2,1,0:T(8,128)(2,1)S(1)} async-done(((bf16[8,20,16,128]{3,2,1,0:T(8,128)(2,1)}), bf16[8,20,16,128]{3,2,1,0:T(8,128)(2,1)S(1)}, u32[]{:S(2)}, u32[]{:S(2)}) %all-to-all-start.1) | async-done | bytes 655392 | tf_op jit(solution)/shard_map/all_to_all | solution.py:254
  49.9 3.2 %shard_map.78 = (bf16[448,128]{1,0:T(8,128)(2,1)S(1)}, f32[6,8,16,128]{3,2,1,0:T(8,128)S(1)}, bf16[10,16,128]{2,1,0:T(8,128)(2,1)S(1)}) custom-call(s32[1]{0:T(128)} %bitcast.place, bf16[8,24,16,128]{3,2,1,0:T(8,128)(2,1)S(1)} %all-to-all-done.got, bf16[8,20,16,128]{3,2,1,0:T(8,128)(2,1)S(1)} %all-to-all-done.1.layer, ...), custom_call_target="tpu_custom_call" | custom-call | tf_op jit(solution)/shard_map/pallas_call | solution.py:264
  53.1 6.8 %all_to_all.25.parts = bf16[8,56,128]{2,1,0:T(8,128)(2,1)S(1)} all-to-all(bf16[8,56,128]{2,1,0:T(8,128)(2,1)S(1)} %bitcast.11), channel_id=1, replica_groups={{4,5,6,7,0,1,2,3},{12,13,14,15,8,9,10,11},{20,21,22,23,16,17,18,19},{28..., dimensions={0} | all-to-all | bytes 229376 | tf_op jit(solution)/shard_map/all_to_all | solution.py:287
  60.0 0.7 shard_map.80
  60.6 10.4 %all-to-all-start.3 = ((bf16[8,56,128]{2,1,0:T(8,128)(2,1)}), bf16[8,56,128]{2,1,0:T(8,128)(2,1)S(1)}, u32[]{:S(2)}, u32[]{:S(2)}) async-start(bf16[8,56,128]{2,1,0:T(8,128)(2,1)} %shard_map.80), calls=%async_computation.3 | async-start | bytes 229376 | tf_op jit(solution)/shard_map/all_to_all | solution.py:290
  71.1 3.2 %collective-permute-start.4 = (bf16[10,16,128]{2,1,0:T(8,128)(2,1)S(1)}, bf16[10,16,128]{2,1,0:T(8,128)(2,1)S(1)}, u32[]{:S(2)}, u32[]{:S(2)}) collective-permute-start(bf16[10,16,128]{2,1,0:T(8,128)(2,1)S(1)} %get-tuple-element.28), channel_id=1, source_target_pairs={{0,1},{1,2},{2,3},{3,0},{4,5},{5,6},{6,7},{7,4},{8,9},{9,10},{10,1... | collective-permute-start | bytes 122888 | tf_op jit(solution)/shard_map/ppermute | solution.py:288
  74.3 1.1 %collective-permute-done.4.from_y = bf16[10,16,128]{2,1,0:T(8,128)(2,1)S(1)} collective-permute-done((bf16[10,16,128]{2,1,0:T(8,128)(2,1)S(1)}, bf16[10,16,128]{2,1,0:T(8,128)(2,1)S(1)}, u32[]{:S(2)}, u32[]{:S(2)}) %collective-permute-start.4) | collective-permute-done | bytes 40992 | tf_op jit(solution)/shard_map/ppermute | solution.py:288
  75.4 2.0 %all-to-all-done.3.parts = bf16[8,56,128]{2,1,0:T(8,128)(2,1)S(1)} async-done(((bf16[8,56,128]{2,1,0:T(8,128)(2,1)}), bf16[8,56,128]{2,1,0:T(8,128)(2,1)S(1)}, u32[]{:S(2)}, u32[]{:S(2)}) %all-to-all-start.3) | async-done | bytes 114720 | tf_op jit(solution)/shard_map/all_to_all | solution.py:290
  77.5 0.7 shard_map.81
  78.1 5.4 %all-to-all-start.4 = ((bf16[8,56,128]{2,1,0:T(8,128)(2,1)}), bf16[8,56,128]{2,1,0:T(8,128)(2,1)S(1)}, u32[]{:S(2)}, u32[]{:S(2)}) async-start(bf16[8,56,128]{2,1,0:T(8,128)(2,1)} %shard_map.81), calls=%async_computation.4 | async-start | bytes 229376 | tf_op jit(solution)/shard_map/all_to_all | solution.py:295
  83.5 2.0 %collective-permute-start.5 = (bf16[3,8,16,128]{3,2,1,0:T(8,128)(2,1)S(1)}, bf16[3,8,16,128]{3,2,1,0:T(8,128)(2,1)S(1)}, u32[]{:S(2)}, u32[]{:S(2)}) collective-permute-start(bf16[3,8,16,128]{3,2,1,0:T(8,128)(2,1)S(1)} %get-tuple-element.34), channel_id=1, source_target_pairs={{0,4},{4,8},{8,12},{12,16},{16,20},{20,24},{24,28},{28,32},{32,36}... | collective-permute-start | bytes 294920 | tf_op jit(solution)/shard_map/ppermute | solution.py:293
  85.5 1.7 %all-to-all-done.4.parts = bf16[8,56,128]{2,1,0:T(8,128)(2,1)S(1)} async-done(((bf16[8,56,128]{2,1,0:T(8,128)(2,1)}), bf16[8,56,128]{2,1,0:T(8,128)(2,1)S(1)}, u32[]{:S(2)}, u32[]{:S(2)}) %all-to-all-start.4) | async-done | bytes 114720 | tf_op jit(solution)/shard_map/all_to_all | solution.py:295
  87.2 0.7 shard_map.82
  87.9 2.8 %collective-permute-done.5.from_x = bf16[3,8,16,128]{3,2,1,0:T(8,128)(2,1)S(1)} collective-permute-done((bf16[3,8,16,128]{3,2,1,0:T(8,128)(2,1)S(1)}, bf16[3,8,16,128]{3,2,1,0:T(8,128)(2,1)S(1)}, u32[]{:S(2)}, u32[]{:S(2)}) %collective-permute-start.5) | collective-permute-done | bytes 98336 | tf_op jit(solution)/shard_map/ppermute | solution.py:293
  90.7 0.7 shard_map.83
  (9 shorter events, 0.1 us)
Async XLA Ops:
  2.5 7.7 %copy-start.2 = (bf16[17,16,128]{2,1,0:T(8,128)(2,1)S(1)}, bf16[17,16,128]{2,1,0:T(8,128)(2,1)}, u32[]{:S(2)}) copy-start(bf16[17,16,128]{2,1,0:T(8,128)(2,1)} %get-tuple-element.22) | copy-start | bytes 208900
  2.5 20.1 %copy-start.1 = (bf16[1,16,128]{2,1,0:T(8,128)(2,1)S(1)}, bf16[1,16,128]{2,1,0:T(8,128)(2,1)}, u32[]{:S(2)}) copy-start(bf16[1,16,128]{2,1,0:T(8,128)(2,1)} %get-tuple-element.23.own) | copy-start | bytes 12292
  2.5 26.6 %all-to-all-start = ((bf16[8,24,16,128]{3,2,1,0:T(8,128)(2,1)}), bf16[8,24,16,128]{3,2,1,0:T(8,128)(2,1)S(1)}, u32[]{:S(2)}, u32[]{:S(2)}) async-start(bf16[8,24,16,128]{3,2,1,0:T(8,128)(2,1)} %get-tuple-element.24), calls=%async_computation | async-start | bytes 1572864 | tf_op jit(solution)/shard_map/all_to_all | solution.py:246
  10.2 12.5 %collective-permute-start = (bf16[17,16,128]{2,1,0:T(8,128)(2,1)S(1)}, bf16[17,16,128]{2,1,0:T(8,128)(2,1)S(1)}, u32[]{:S(2)}, u32[]{:S(2)}) collective-permute-start(bf16[17,16,128]{2,1,0:T(8,128)(2,1)S(1)} %copy-done.2), channel_id=1, source_target_pairs={{0,60},{4,0},{8,4},{12,8},{16,12},{20,16},{24,20},{28,24},{32,28},... | collective-permute-start | bytes 208904 | tf_op jit(solution)/shard_map/ppermute | solution.py:250
  22.7 5.5 %collective-permute-start.1 = (bf16[6,16,128]{2,1,0:T(8,128)(2,1)S(1)}, bf16[6,16,128]{2,1,0:T(8,128)(2,1)S(1)}, u32[]{:S(2)}, u32[]{:S(2)}) collective-permute-start(bf16[6,16,128]{2,1,0:T(8,128)(2,1)S(1)} %shard_map.76), channel_id=1, source_target_pairs={{0,3},{1,0},{2,1},{3,2},{4,7},{5,4},{6,5},{7,6},{8,11},{9,8},{10,9... | collective-permute-start | bytes 73736 | tf_op jit(solution)/shard_map/ppermute | solution.py:251
  29.1 20.8 %all-to-all-start.1 = ((bf16[8,20,16,128]{3,2,1,0:T(8,128)(2,1)}), bf16[8,20,16,128]{3,2,1,0:T(8,128)(2,1)S(1)}, u32[]{:S(2)}, u32[]{:S(2)}) async-start(bf16[8,20,16,128]{3,2,1,0:T(8,128)(2,1)} %shard_map.77), calls=%async_computation.1 | async-start | bytes 1310720 | tf_op jit(solution)/shard_map/all_to_all | solution.py:254
  36.6 7.4 %copy-start = (bf16[27,128,128]{2,1,0:T(8,128)(2,1)S(1)}, bf16[27,128,128]{2,1,0:T(8,128)(2,1)}, u32[]{:S(2)}) copy-start(bf16[27,128,128]{2,1,0:T(8,128)(2,1)} %weight.1) | copy-start | bytes 2654212
  36.7 12.1 %collective-permute-start.3 = (bf16[8,9,16,128]{3,2,1,0:T(8,128)(2,1)S(1)}, bf16[8,9,16,128]{3,2,1,0:T(8,128)(2,1)S(1)}, u32[]{:S(2)}, u32[]{:S(2)}) collective-permute-start(bf16[8,9,16,128]{3,2,1,0:T(8,128)(2,1)S(1)} %slice.11), channel_id=1, source_target_pairs={{0,60},{4,0},{8,4},{12,8},{16,12},{20,16},{24,20},{28,24},{32,28},... | collective-permute-start | bytes 884744 | tf_op jit(solution)/shard_map/ppermute | solution.py:255
  42.1 6.7 %collective-permute-start.2 = (bf16[8,4,16,128]{3,2,1,0:T(8,128)(2,1)S(1)}, bf16[8,4,16,128]{3,2,1,0:T(8,128)(2,1)S(1)}, u32[]{:S(2)}, u32[]{:S(2)}) collective-permute-start(bf16[8,4,16,128]{3,2,1,0:T(8,128)(2,1)S(1)} %pad_maximum_fusion), channel_id=1, source_target_pairs={{0,3},{1,0},{2,1},{3,2},{4,7},{5,4},{6,5},{7,6},{8,11},{9,8},{10,9... | collective-permute-start | bytes 393224 | tf_op jit(solution)/shard_map/ppermute | solution.py:256
  60.6 16.8 %all-to-all-start.3 = ((bf16[8,56,128]{2,1,0:T(8,128)(2,1)}), bf16[8,56,128]{2,1,0:T(8,128)(2,1)S(1)}, u32[]{:S(2)}, u32[]{:S(2)}) async-start(bf16[8,56,128]{2,1,0:T(8,128)(2,1)} %shard_map.80), calls=%async_computation.3 | async-start | bytes 229376 | tf_op jit(solution)/shard_map/all_to_all | solution.py:290
  71.1 4.3 %collective-permute-start.4 = (bf16[10,16,128]{2,1,0:T(8,128)(2,1)S(1)}, bf16[10,16,128]{2,1,0:T(8,128)(2,1)S(1)}, u32[]{:S(2)}, u32[]{:S(2)}) collective-permute-start(bf16[10,16,128]{2,1,0:T(8,128)(2,1)S(1)} %get-tuple-element.28), channel_id=1, source_target_pairs={{0,1},{1,2},{2,3},{3,0},{4,5},{5,6},{6,7},{7,4},{8,9},{9,10},{10,1... | collective-permute-start | bytes 122888 | tf_op jit(solution)/shard_map/ppermute | solution.py:288
  78.1 9.1 %all-to-all-start.4 = ((bf16[8,56,128]{2,1,0:T(8,128)(2,1)}), bf16[8,56,128]{2,1,0:T(8,128)(2,1)S(1)}, u32[]{:S(2)}, u32[]{:S(2)}) async-start(bf16[8,56,128]{2,1,0:T(8,128)(2,1)} %shard_map.81), calls=%async_computation.4 | async-start | bytes 229376 | tf_op jit(solution)/shard_map/all_to_all | solution.py:295
  83.5 7.1 %collective-permute-start.5 = (bf16[3,8,16,128]{3,2,1,0:T(8,128)(2,1)S(1)}, bf16[3,8,16,128]{3,2,1,0:T(8,128)(2,1)S(1)}, u32[]{:S(2)}, u32[]{:S(2)}) collective-permute-start(bf16[3,8,16,128]{3,2,1,0:T(8,128)(2,1)S(1)} %get-tuple-element.34), channel_id=1, source_target_pairs={{0,4},{4,8},{8,12},{12,16},{16,20},{20,24},{24,28},{28,32},{32,36}... | collective-permute-start | bytes 294920 | tf_op jit(solution)/shard_map/ppermute | solution.py:293
